TPU v7x, 32 devices: a whole 2x2x4 slice. The times are simulated.
32 devices in a mesh: rep: 2 (over x), pool: 16 (over z, y, core).
Axes of the slice: x: 2, y: 2, z: 4, core: 2. Of those that a mesh axis runs over, the one named last changes fastest.
Arguments:
- hidden_state: bfloat16 [256, 6144], P(('rep', 'pool')), parts along dimension 0, may hold values from -80 to 80
- queries: bfloat16 [256, 6144], P(('rep', 'pool')), parts along dimension 0, may hold values from -100 to 100
- new_entries: bfloat16 [256, 2, 1024], P(('rep', 'pool')), parts along dimension 0, may hold values from -5 to 5
- cached: bfloat16 [4096, 2, 1024], P(('rep', 'pool')), parts along dimension 0, may hold values from -6 to 6
- cache_lengths: int32 [32, 8], P(('rep', 'pool')), parts along dimension 0, may hold values from 1 to 64, 128 in all within a row
- routes: int32 [256, 4], P(('rep', 'pool')), parts along dimension 0, may hold values from 0 to 15, all different within a row; in each aligned block of 8 rows (0 to 7, 8 to 15, ...) at most 4 rows name the same one
- norm_gain: float32 [6144], replicated, may hold values from 0.25 to 1.75
- router_weight: bfloat16 [6144, 16], replicated, may hold values from -0.078125 to 0.078125
- expert_gate: bfloat16 [16, 6144, 1344], P('pool'), may hold values from -0.078125 to 0.078125
- expert_up: bfloat16 [16, 6144, 1344], P('pool'), may hold values from -0.078125 to 0.078125
- expert_down: bfloat16 [16, 1344, 6144], P('pool'), may hold values from -0.0625 to 0.0625
Outputs:
- mixed: bfloat16 [256, 6144], P(('rep', 'pool')), parts along dimension 0
There are 2 independent parts, one for each index of `rep`. A program takes and returns all parts, laid end to end along the dimension named above; an argument that names none is the same for every part. Nothing has to cross between parts.
Inputs may be any that keep to these rules, and one draw needn't show every extreme that they name: `routes`: each row names 4 different experts; the rows of one device name no expert more than 4 times. `cache_lengths`: the 8 lengths of a device sum to 128.
All inputs are finite; a program needn't handle non-finite values.
Results may differ from a plain program's by a relative error of at most 0.004.
Values may be sent and summed in bfloat16 or wider, within the bound.
No kernel may reach another device: no remote copies, remote signals or barrier semaphores. Data moves between devices by JAX's collectives and lax.ppermute only.
A program may use at most 128 MiB of HBM per device.

v0:
```python
import math

import jax
import jax.numpy as jnp
from jax import lax
from jax.sharding import PartitionSpec as P

HEADS = 48
KV_HEADS = 8
HEAD_DIM = 128
FLIGHT = 2


EPSILON = 1e-05


def attend_local(queries, new_entries, cached, lengths):
    requests = queries.shape[0]
    positions = cached.shape[0]
    groups = HEADS // KV_HEADS
    query_heads = queries.reshape(requests, KV_HEADS, groups, HEAD_DIM)
    cache_keys = cached[:, 0].reshape(positions, KV_HEADS, HEAD_DIM)
    cache_values = cached[:, 1].reshape(positions, KV_HEADS, HEAD_DIM)
    own_keys = new_entries[:, 0].reshape(requests, KV_HEADS, HEAD_DIM)
    own_values = new_entries[:, 1].reshape(requests, KV_HEADS, HEAD_DIM)
    scale = 1.0 / math.sqrt(HEAD_DIM)
    scores = (
        jnp.einsum("rkgd,pkd->rkgp", query_heads, cache_keys, preferred_element_type=jnp.float32)
        * scale
    )
    own_score = (
        jnp.einsum("rkgd,rkd->rkg", query_heads, own_keys, preferred_element_type=jnp.float32)
        * scale
    )
    ends = jnp.cumsum(lengths, dtype=jnp.int32)
    starts = ends - lengths
    spots = jnp.arange(positions, dtype=jnp.int32)
    inside = (spots[None, :] >= starts[:, None]) & (spots[None, :] < ends[:, None])
    masked = jnp.where(inside[:, None, None, :], scores, -jnp.inf)
    peak = jnp.maximum(jnp.max(masked, axis=-1), own_score)
    expos = jnp.exp(masked - peak[..., None])
    own_expo = jnp.exp(own_score - peak)
    total = jnp.sum(expos, axis=-1) + own_expo
    weights = (expos / total[..., None]).astype(jnp.bfloat16)
    own_weight = (own_expo / total).astype(jnp.bfloat16)
    summed = jnp.einsum("rkgp,pkd->rkgd", weights, cache_values, preferred_element_type=jnp.float32)
    summed = (
        summed
        + own_weight.astype(jnp.float32)[..., None] * own_values.astype(jnp.float32)[:, :, None, :]
    )
    return summed.reshape(requests, HEADS * HEAD_DIM).astype(jnp.bfloat16)


def layer_norm(values, gain):
    center = jnp.mean(values, axis=-1, keepdims=True)
    centered = values - center
    spread = jnp.mean(centered * centered, axis=-1, keepdims=True)
    return (centered * lax.rsqrt(spread + EPSILON) * gain).astype(jnp.bfloat16)


def body(
    hidden_state,
    queries,
    new_entries,
    cached,
    cache_lengths,
    routes,
    norm_gain,
    router_weight,
    expert_gate,
    expert_up,
    expert_down,
):
    requests, width = hidden_state.shape
    devices = lax.axis_size("pool")
    group = devices // FLIGHT
    experts = router_weight.shape[1]
    fanout = routes.shape[1]
    capacity = min(requests, 2 * requests * fanout // experts)
    attended = attend_local(queries, new_entries, cached, cache_lengths[0])
    residual_sum = hidden_state.astype(jnp.float32) + attended.astype(jnp.float32)
    normed = layer_norm(residual_sum, norm_gain)
    logits = jnp.dot(normed, router_weight, preferred_element_type=jnp.float32)
    chosen = (routes[:, :, None] == jnp.arange(experts, dtype=jnp.int32)[None, None, :]).astype(
        jnp.int32
    )
    routed = jnp.sum(chosen.astype(jnp.float32) * logits[:, None, :], axis=-1)
    gates = 1.0 / jnp.sum(jnp.exp(routed[:, None, :] - routed[:, :, None]), axis=-1)
    counts = jnp.sum(chosen, axis=1, dtype=jnp.int32)
    before = jnp.cumsum(counts, axis=0, dtype=jnp.int32) - counts
    slots = jnp.sum(chosen * before[:, None, :], axis=-1, dtype=jnp.int32)
    target = routes * capacity + slots
    limit = FLIGHT * capacity
    placing = jnp.sum(
        (target[:, :, None] == jnp.arange(limit, dtype=jnp.int32)[None, None, :]).astype(
            jnp.bfloat16
        ),
        axis=1,
    )
    packed = jnp.einsum("rs,rd->sd", placing, normed, preferred_element_type=jnp.float32).astype(
        jnp.bfloat16
    )
    packed = packed.reshape(FLIGHT, capacity, width)
    outgoing = jnp.broadcast_to(packed[:, None], (FLIGHT, group, capacity, width)).reshape(
        devices, capacity, width
    )
    arrived = lax.all_to_all(outgoing, "pool", split_axis=0, concat_axis=0, tiled=True)
    rows = arrived.reshape(devices * capacity, width)
    gate_part = jnp.dot(rows, expert_gate[0], preferred_element_type=jnp.float32)
    up_part = jnp.dot(rows, expert_up[0], preferred_element_type=jnp.float32)
    inner = (jax.nn.silu(gate_part) * up_part).astype(jnp.bfloat16)
    partial_value = jnp.dot(inner, expert_down[0], preferred_element_type=jnp.float32).reshape(
        devices, capacity, width
    )
    returned = lax.all_to_all(
        partial_value.astype(jnp.bfloat16), "pool", split_axis=0, concat_axis=0, tiled=True
    ).astype(partial_value.dtype)
    expert_out = jnp.sum(returned.reshape(FLIGHT, group, capacity, width), axis=1).astype(
        jnp.bfloat16
    )
    flat_out = expert_out.reshape(limit, width)
    held = routes < FLIGHT
    picked = flat_out[jnp.minimum(target, limit - 1)].astype(jnp.float32)
    terms = jnp.where(held[:, :, None], gates[:, :, None] * picked, jnp.float32(0.0))
    mixed = residual_sum + jnp.sum(terms, axis=1)
    return mixed.astype(jnp.bfloat16)


def solution(mesh):
    in_specs = (
        P(("rep", "pool"), None),
        P(("rep", "pool"), None),
        P(("rep", "pool"), None, None),
        P(("rep", "pool"), None, None),
        P(("rep", "pool"), None),
        P(("rep", "pool"), None),
        P(),
        P(),
        P("pool", None, None),
        P("pool", None, None),
        P("pool", None, None),
    )
    out_specs = P(("rep", "pool"), None)
    return jax.shard_map(body, mesh=mesh, in_specs=in_specs, out_specs=out_specs, check_vma=False)
```

profile of v0, /device:TPU:0, one launch (start us, length us, event | category | flops | bytes accessed | tf_op | source)
XLA Modules:
  0.0 99.5 jit_solution(16329594530588853998)
XLA Ops:
  0.0 0.9 reduce-window.7
  0.9 0.7 bitcast_subtract_fusion
  1.5 0.8 convert_reduce_fusion
  2.3 0.9 select_reduce_fusion.1
  3.2 0.7 compare_select_fusion
  4.0 0.8 slice_convert_fusion
  4.8 1.1 %fusion.22 = f32[8,8,1,6]{3,2,1,0:T(1,128)S(1)} fusion(bf16[8,8,6,128]{3,0,2,1:T(8,128)(2,1)} %bitcast.85, bf16[8,2,1024]{2,1,0:T(2,128)(2,1)} %param.13), kind=kOutput, calls=%fused_computation.28 | convolution fusion | flops 98304 | bytes 132608 | tf_op jit(solution)/shard_map/rkgd,rkd->rkg/dot_general | solution.py:32
  6.0 2.1 %fusion.36 = (bf16[128,1,1024]{2,1,0:T(2,128)(2,1)S(1)}, bf16[128,1,1024]{2,1,0:T(2,128)(2,1)S(1)}) fusion(bf16[128,2,1024]{2,1,0:T(2,128)(2,1)} %param.14), kind=kLoop, calls=%fused_computation.62 | loop fusion | bytes 1048576 | tf_op jit(solution)/shard_map/slice | solution.py:22
  8.2 0.4 copy.63
  8.7 1.2 %fusion.37 = (f32[8,8,6]{0,2,1:T(8,128)S(1)}, f32[8,8,6,128]{3,0,2,1:T(8,128)S(1)}) fusion(bf16[128,8,128,1]{0,2,3,1:T(8,128)(2,1)S(1)} %bitcast.82, bf16[8,8,6,128]{3,0,2,1:T(8,128)(2,1)} %bitcast.86, pred[8,128]{1,0:T(8,128)(4,1)S(1)} %fusion.35), kind=kOutput, calls=%fused_computation.63 | convolution fusion | flops 12729984 | bytes 559616 | tf_op jit(solution)/shard_map/rkgd,pkd->rkgp/dot_general | solution.py:28
  10.2 0.4 copy.64
  10.9 1.1 %fusion.21 = f32[8]{0:T(128)S(1)} fusion(bf16[8,6144]{1,0:T(8,128)(2,1)S(1)} %bitcast.77, bf16[8,6144]{1,0:T(8,128)(2,1)} %param.11), kind=kLoop, calls=%fused_computation.27 | loop fusion | flops 196600 | bytes 196640 | tf_op jit(solution)/shard_map/reduce_sum | solution.py:55
  12.0 1.1 %multiply_reduce_fusion = f32[8]{0:T(128)S(1)} fusion(bf16[8,6144]{1,0:T(8,128)(2,1)S(1)} %bitcast.78, bf16[8,6144]{1,0:T(8,128)(2,1)} %param.11, f32[8]{0:T(128)S(1)} %broadcast_multiply_fusion), kind=kLoop, calls=%fused_computation.22 | loop fusion | flops 294904 | bytes 196672 | tf_op jit(solution)/shard_map/reduce_sum | solution.py:57
  13.1 1.0 %multiply_convert_fusion = bf16[8,6144]{1,0:T(8,128)(2,1)S(1)} fusion(bf16[8,6144]{1,0:T(8,128)(2,1)S(1)} %bitcast.79, bf16[8,6144]{1,0:T(8,128)(2,1)} %param.11, f32[6144]{0:T(1024)} %param.17, f32[8]{0:T(128)S(1)} %add_rsqrt_fusion, f32[8]{0:T(128)S(1)} %broadcast_multiply_fusion), kind=kLoop, calls=%fused_computation.21 | loop fusion | flops 344064 | bytes 319552 | tf_op jit(solution)/shard_map/convert_element_type | solution.py:58
  14.7 27.5 %all_to_all.10 = bf16[16,4,6144]{2,1,0:T(4,128)(2,1)S(1)} all-to-all(bf16[16,4,6144]{2,1,0:T(4,128)(2,1)S(1)} %bitcast.76), channel_id=1, replica_groups=mesh['rep'=2,'pool'=16] {'pool'}, dimensions={0} | all-to-all | bytes 1572864 | tf_op jit(solution)/shard_map/all_to_all | solution.py:107
  42.3 10.7 %fusion.4 = f32[64,1344]{1,0:T(8,128)S(1)} fusion(bf16[64,6144]{1,0:T(8,128)(2,1)S(1)} %reshape.134, bf16[1,6144,1344]{1,2,0:T(8,128)(2,1)} %param.19), kind=kOutput, calls=%fused_computation.5 | convolution fusion | flops 1056964608 | bytes 17645568 | tf_op jit(solution)/shard_map/dot_general | solution.py:109
  53.1 10.7 %fusion.12 = bf16[64,1344]{1,0:T(8,128)(2,1)S(1)} fusion(bf16[64,6144]{1,0:T(8,128)(2,1)S(1)} %reshape.134, bf16[1,6144,1344]{1,2,0:T(8,128)(2,1)} %param.20, f32[64,1344]{1,0:T(8,128)S(1)} %fusion.4), kind=kOutput, calls=%fused_computation.10 | convolution fusion | flops 1057480704 | bytes 17817600 | tf_op jit(solution)/shard_map/dot_general | solution.py:110
  63.9 8.8 %fusion.6 = bf16[16,4,6144]{2,0,1:T(8,128)(2,1)S(1)} fusion(bf16[1,1344,6144]{2,1,0:T(8,128)(2,1)} %param.21, bf16[16,4,1344]{2,1,0:T(4,128)(2,1)S(1)} %dot_general.33), kind=kOutput, calls=%fused_computation.7 | convolution fusion | flops 1057357824 | bytes 17473536 | tf_op jit(solution)/shard_map/dot_general | solution.py:112
  72.6 1.5 %copy.49 = bf16[16,4,6144]{2,1,0:T(4,128)(2,1)} copy(bf16[16,4,6144]{2,0,1:T(8,128)(2,1)S(1)} %fusion.6) | data formatting | bytes 1572864 | tf_op jit(solution)/shard_map/convert_element_type | solution.py:116
  74.1 3.9 %all-to-all-start.1 = ((bf16[16,4,6144]{2,1,0:T(4,128)(2,1)}), bf16[16,4,6144]{2,1,0:T(4,128)(2,1)S(1)}, u32[]{:S(2)}, u32[]{:S(2)}) async-start(bf16[16,4,6144]{2,1,0:T(4,128)(2,1)} %copy.49), calls=%async_computation.1 | async-start | bytes 1572864 | tf_op jit(solution)/shard_map/all_to_all | solution.py:115
  78.8 17.9 %all-to-all-done.1 = bf16[16,4,6144]{2,1,0:T(4,128)(2,1)S(1)} async-done(((bf16[16,4,6144]{2,1,0:T(4,128)(2,1)}), bf16[16,4,6144]{2,1,0:T(4,128)(2,1)S(1)}, u32[]{:S(2)}, u32[]{:S(2)}) %all-to-all-start.1) | async-done | bytes 786464 | tf_op jit(solution)/shard_map/all_to_all | solution.py:115
  97.1 0.8 gather_fusion
  98.2 0.6 select_reduce_fusion
  98.8 0.7 add_convert_fusion
  (36 shorter events, 3.1 us)
Async XLA Ops:
  0.0 78.3 %copy-start = (bf16[6144,16]{0,1:T(8,128)(2,1)S(1)}, bf16[6144,16]{0,1:T(8,128)(2,1)}, u32[]{:S(2)}) copy-start(bf16[6144,16]{0,1:T(8,128)(2,1)} %param.18) | copy-start | bytes 589828
  53.1 25.0 %copy-start.2 = (s32[8,4]{0,1:T(4,128)S(1)}, s32[8,4]{0,1:T(4,128)}, u32[]{:S(2)}) copy-start(s32[8,4]{0,1:T(4,128)} %param.16) | copy-start | bytes 388
  63.8 35.0 %copy-start.1 = (bf16[8,6144]{1,0:T(8,128)(2,1)S(1)}, bf16[8,6144]{1,0:T(8,128)(2,1)}, u32[]{:S(2)}) copy-start(bf16[8,6144]{1,0:T(8,128)(2,1)} %param.11) | copy-start | bytes 294916
  74.1 22.6 %all-to-all-start.1 = ((bf16[16,4,6144]{2,1,0:T(4,128)(2,1)}), bf16[16,4,6144]{2,1,0:T(4,128)(2,1)S(1)}, u32[]{:S(2)}, u32[]{:S(2)}) async-start(bf16[16,4,6144]{2,1,0:T(4,128)(2,1)} %copy.49), calls=%async_computation.1 | async-start | bytes 1572864 | tf_op jit(solution)/shard_map/all_to_all | solution.py:115
where the time goes:
time: 100 us; the launch traced here: 99.5 us
  matrix products  33.2 us (33%)
  blocking collectives  27.5 us (28%)
  waiting for transfers between devices  17.9 us (18%)
  other arithmetic  10.2 us (10%)
  local copies, waits for them, and re-layouts  6.64 us (7%)
  starting transfers between devices  3.91 us (4%)
    all_to_all x1, blocking collectives, body(): lax.all_to_all(outgoing, 'pool', split_axis=0, concat_axis=0, tiled=True)  27.5 us
    all_to_all x1, waiting for transfers between devices, body(): lax.all_to_all(partial_value.astype(jnp.bfloat16), 'pool', split_axis=0,...  17.9 us
    dot_general x1, matrix products, body(): up_part = jnp.dot(rows, expert_up[0], preferred_element_type=jnp.float32)  10.7 us
    dot_general x1, matrix products, body(): jnp.dot(rows, expert_gate[0], preferred_element_type=jnp.float32)  10.7 us
    dot_general x1, matrix products, body(): jnp.dot(inner, expert_down[0], preferred_element_type=jnp.float32)  8.76 us
    all_to_all x1, starting transfers between devices, body(): lax.all_to_all(partial_value.astype(jnp.bfloat16), 'pool', split_axis=0,...  3.91 us
    slice x1, local copies, waits for them, and re-layouts, attend_local(): cache_keys = cached[:, 0].reshape(positions, KV_HEADS, HEAD_DIM)  2.13 us
  transfers between devices with their start and end apart: 1, of which 1 were waited for; matrix products, arithmetic and copies ran while one was open for 1% of the time, Pallas kernels for 0%

commit v1 on v0

v1 whole, which is shorter than its diff:
```python
import functools
import math

import jax
import jax.numpy as jnp
from jax import lax
from jax.experimental import pallas as pl
from jax.experimental.pallas import tpu as pltpu
from jax.sharding import PartitionSpec as P

HEADS = 48
KV_HEADS = 8
HEAD_DIM = 128
FLIGHT = 2
CORES = 2
EPSILON = 1e-05

F32 = jnp.float32
BF16 = jnp.bfloat16
NT = (((1,), (1,)), ((), ()))
TN = (((0,), (0,)), ((), ()))
MIB = 1 << 20


def whole(space=pltpu.VMEM):
    return pl.BlockSpec(memory_space=space)


def iota(shape, dim):
    return lax.broadcasted_iota(jnp.int32, shape, dim)


def slot_columns(routes, expert):
    rows = routes.shape[0]
    named = jnp.max((routes == expert).astype(F32), axis=1, keepdims=True)
    wide = jnp.broadcast_to(named, (rows, rows))
    row, lane = iota((rows, rows), 0), iota((rows, rows), 1)
    named_lanes = jnp.sum(jnp.where(row == lane, wide, 0.0), axis=0, keepdims=True)
    before_lanes = jnp.sum(jnp.where(row < lane, wide, 0.0), axis=0, keepdims=True)
    before = jnp.sum(jnp.where(lane < row, named_lanes, 0.0), axis=1, keepdims=True)
    return named, before, named_lanes, before_lanes


def front_kernel(half, hidden_ref, queries_ref, kv_ref, own_ref, lengths_ref, routes_ref, gain_ref,
                 residual_ref, normed_ref, near_ref, far_ref, att_ref):
    requests, width = hidden_ref.shape
    groups = HEADS // KV_HEADS
    pairs = kv_ref.shape[0]
    scale = 1.0 / math.sqrt(HEAD_DIM)
    row, lane = iota((requests, requests), 0), iota((requests, requests), 1)
    lengths = jnp.broadcast_to(lengths_ref[...], (requests, requests))
    starts = jnp.sum(jnp.where(lane < row, lengths, 0), axis=1, keepdims=True)
    ends = starts + jnp.sum(jnp.where(lane == row, lengths, 0), axis=1, keepdims=True)
    column = iota((requests, pairs), 1)
    inside = (column >= 2 * starts) & (column < 2 * ends) & (column % 2 == 0)
    bias = jnp.where(inside, 0.0, -jnp.inf).astype(F32)
    bias = jnp.concatenate([bias] * groups, axis=0)
    queries = queries_ref[...].astype(F32)
    own = own_ref[...].astype(F32)
    for head in range(KV_HEADS):
        spot = slice(head * HEAD_DIM, (head + 1) * HEAD_DIM)
        block = kv_ref[:, spot]
        own_key, own_value = own[:, 0, spot], own[:, 1, spot]
        parts = [queries[:, (head * groups + j) * HEAD_DIM:(head * groups + j + 1) * HEAD_DIM] for j in range(groups)]
        stacked = jnp.concatenate(parts, axis=0)
        keys = jnp.concatenate([own_key] * groups, axis=0)
        scores = lax.dot_general(stacked.astype(BF16), block, NT, preferred_element_type=F32) * scale + bias
        own_score = jnp.sum(stacked * keys, axis=1, keepdims=True) * scale
        peak = jnp.maximum(jnp.max(scores, axis=1, keepdims=True), own_score)
        expos = jnp.exp(scores - peak)
        own_expo = jnp.exp(own_score - peak)
        total = jnp.sum(expos, axis=1, keepdims=True) + own_expo
        weights = pltpu.roll(expos / total, 1, 1).astype(BF16)
        own_weight = (own_expo / total).astype(BF16).astype(F32)
        summed = jnp.dot(weights, block, preferred_element_type=F32)
        summed = summed + own_weight * jnp.concatenate([own_value] * groups, axis=0)
        for j in range(groups):
            at = (head * groups + j) * HEAD_DIM
            att_ref[:, at:at + HEAD_DIM] = summed[j * requests:(j + 1) * requests].astype(BF16).astype(F32)
    residual = hidden_ref[...].astype(F32) + att_ref[...]
    residual_ref[...] = residual
    centered = residual - jnp.mean(residual, axis=1, keepdims=True)
    spread = jnp.mean(centered * centered, axis=1, keepdims=True)
    normed = (centered * lax.rsqrt(spread + EPSILON) * gain_ref[...]).astype(BF16)
    normed_ref[...] = normed
    mine = half()
    capacity = near_ref.shape[0]
    slot = iota((capacity, requests), 0).astype(F32)
    for expert, out in ((mine, near_ref), (1 - mine, far_ref)):
        _, _, named, before = slot_columns(routes_ref[...], expert)
        placing = jnp.where(before == slot, named, 0.0).astype(BF16)
        out[...] = jnp.dot(placing, normed, preferred_element_type=F32).astype(BF16)


def gate_kernel(half, normed_ref, router_ref, routes_ref, mix_ref):
    routes = routes_ref[...]
    requests, fanout = routes.shape
    experts = router_ref.shape[1]
    capacity = mix_ref.shape[1] // FLIGHT
    logits = jnp.dot(normed_ref[...], router_ref[...], preferred_element_type=F32)
    lane = iota((requests, experts), 1)
    routed = [
        jnp.sum(jnp.where(lane == routes[:, k:k + 1], logits, 0.0), axis=1, keepdims=True) for k in range(fanout)
    ]
    mine = half()
    column = iota((requests, FLIGHT * capacity), 1)
    mix = jnp.zeros((requests, FLIGHT * capacity), F32)
    for turn, expert in enumerate((mine, 1 - mine)):
        named, before, _, _ = slot_columns(routes, expert)
        gate = jnp.zeros((requests, 1), F32)
        for k in range(fanout):
            total = sum(jnp.exp(routed[j] - routed[k]) for j in range(fanout))
            gate = jnp.where(routes[:, k:k + 1] == expert, 1.0 / total, gate)
        place = (column - turn * capacity).astype(F32)
        mix = jnp.where((before == place) & (named > 0.0), gate, mix)
    mix_ref[...] = mix


def expert_kernel(chips, chunk, *refs):
    pieces = refs[:2 * chips]
    gate_hbm, up_hbm, down_hbm, keep_ref, send_ref, rows_ref, gate_ref, up_ref, down_ref, inner_ref, sems = refs[2 * chips:]
    hidden, width = gate_ref.shape
    steps = hidden // chunk

    pairs = ((gate_hbm, gate_ref), (up_hbm, up_ref), (down_hbm, down_ref))

    def copy(i, n):
        at = pl.ds(i * chunk, chunk)
        return pltpu.make_async_copy(pairs[n][0].at[at], pairs[n][1].at[at], sems.at[i, n])

    for i in range(steps):
        copy(i, 0).start()
        copy(i, 1).start()
    for i in range(steps):
        copy(i, 2).start()
    count = pieces[0].shape[0]
    for i, piece in enumerate(pieces):
        rows_ref[i * count:(i + 1) * count, :] = piece[...]
    for i in range(steps):
        at = slice(i * chunk, (i + 1) * chunk)
        copy(i, 0).wait()
        copy(i, 1).wait()
        rows = rows_ref[...]
        gate_part = lax.dot_general(gate_ref[at], rows, NT, preferred_element_type=F32)
        up_part = lax.dot_general(up_ref[at], rows, NT, preferred_element_type=F32)
        inner = gate_part / (1.0 + jnp.exp(-gate_part)) * up_part
        inner_ref[:, at] = inner.T.astype(BF16)
    for i in range(steps):
        copy(i, 2).wait()
    out = jnp.dot(inner_ref[...], down_ref[...], preferred_element_type=F32)
    keep_ref[...] = out[:chips * count]
    send_ref[...] = out[chips * count:].astype(BF16)


def core_sum_kernel(keep_ref, recv_ref, first_ref, *rest):
    count = first_ref.shape[0]
    total = keep_ref[...] + recv_ref[...].astype(F32)
    first_ref[...] = total[:count]
    for i, out in enumerate(rest):
        out[...] = total[(i + 1) * count:(i + 2) * count].astype(BF16)


def chip_sum_kernel(first_ref, *refs):
    *parts, near_ref, far_ref = refs
    total = first_ref[...]
    for part in parts:
        total = total + part[...].astype(F32)
    capacity = near_ref.shape[0]
    near_ref[...] = total[:capacity].astype(BF16)
    far_ref[...] = total[capacity:].astype(BF16)


def mix_kernel(residual_ref, mix_ref, near_ref, far_ref, out_ref):
    mix = mix_ref[...]
    capacity = near_ref.shape[0]
    total = jnp.zeros(residual_ref.shape, F32)
    for i, ref in enumerate((near_ref, far_ref)):
        rows = ref[...].astype(F32)
        for j in range(capacity):
            at = i * capacity + j
            total = total + mix[:, at:at + 1] * rows[j:j + 1]
    out_ref[...] = (residual_ref[...] + total).astype(BF16)


def like(*shape, dtype=BF16):
    return jax.ShapeDtypeStruct(shape, dtype)


def params(mib=16):
    return pltpu.CompilerParams(vmem_limit_bytes=mib * MIB)


def body(
    hidden_state,
    queries,
    new_entries,
    cached,
    cache_lengths,
    routes,
    norm_gain,
    router_weight,
    expert_gate,
    expert_up,
    expert_down,
):
    requests, width = hidden_state.shape
    devices = lax.axis_size("pool")
    group = devices // FLIGHT
    chips = group // CORES
    experts = router_weight.shape[1]
    fanout = routes.shape[1]
    capacity = min(requests, 2 * requests * fanout // experts)
    count = 2 * capacity
    hidden = expert_gate.shape[2]

    def half():
        return lax.axis_index("pool") // group

    def exchange(value, bit):
        return lax.ppermute(value, "pool", [(i, i ^ bit) for i in range(devices)])

    positions = cached.shape[0]
    residual, normed, near, far = pl.pallas_call(
        functools.partial(front_kernel, half),
        out_shape=(like(requests, width, dtype=F32), like(requests, width), like(capacity, width), like(capacity, width)),
        in_specs=[whole()] * 7,
        out_specs=(whole(),) * 4,
        scratch_shapes=[pltpu.VMEM((requests, width), F32)],
        compiler_params=params(),
    )(hidden_state, queries, cached.reshape(2 * positions, -1), new_entries, cache_lengths, routes, norm_gain[None])
    arrived = exchange(far, group)
    mix = pl.pallas_call(
        functools.partial(gate_kernel, half),
        out_shape=like(requests, count, dtype=F32),
        in_specs=[whole()] * 3,
        out_specs=whole(),
        compiler_params=params(),
    )(normed, router_weight, routes)
    own = jnp.concatenate([near, arrived], axis=0)
    mine = [own] + [exchange(own, CORES * j) for j in range(1, chips)]
    beside = [exchange(piece, 1) for piece in mine]
    chunk = hidden // 6 if hidden % 96 == 0 else hidden
    steps = hidden // chunk
    keep, send = pl.pallas_call(
        functools.partial(expert_kernel, chips, chunk),
        out_shape=(like(chips * count, width, dtype=F32), like(chips * count, width)),
        in_specs=[whole()] * (2 * chips) + [whole(pl.ANY)] * 3,
        out_specs=(whole(), whole()),
        scratch_shapes=[
            pltpu.VMEM((2 * chips * count, width), BF16),
            pltpu.VMEM((hidden, width), BF16),
            pltpu.VMEM((hidden, width), BF16),
            pltpu.VMEM((hidden, width), BF16),
            pltpu.VMEM((2 * chips * count, hidden), BF16),
            pltpu.SemaphoreType.DMA((steps, 3)),
        ],
        compiler_params=params(60),
    )(*mine, *beside, jnp.swapaxes(expert_gate, 1, 2)[0], jnp.swapaxes(expert_up, 1, 2)[0], expert_down[0])
    recv = exchange(send, 1)
    first, *rest = pl.pallas_call(
        core_sum_kernel,
        out_shape=(like(count, width, dtype=F32),) + (like(count, width),) * (chips - 1),
        in_specs=[whole()] * 2,
        out_specs=(whole(),) * chips,
        compiler_params=params(32),
    )(keep, recv)
    parts = [exchange(piece, CORES * (j + 1)) for j, piece in enumerate(rest)]
    near_out, far_out = pl.pallas_call(
        chip_sum_kernel,
        out_shape=(like(capacity, width), like(capacity, width)),
        in_specs=[whole()] * chips,
        out_specs=(whole(), whole()),
        compiler_params=params(),
    )(first, *parts)
    back = exchange(far_out, group)
    return pl.pallas_call(
        mix_kernel,
        out_shape=like(requests, width),
        in_specs=[whole()] * 4,
        out_specs=whole(),
        compiler_params=params(),
    )(residual, mix, near_out, back)


def solution(mesh):
    in_specs = (
        P(("rep", "pool"), None),
        P(("rep", "pool"), None),
        P(("rep", "pool"), None, None),
        P(("rep", "pool"), None, None),
        P(("rep", "pool"), None),
        P(("rep", "pool"), None),
        P(),
        P(),
        P("pool", None, None),
        P("pool", None, None),
        P("pool", None, None),
    )
    out_specs = P(("rep", "pool"), None)
    return jax.shard_map(body, mesh=mesh, in_specs=in_specs, out_specs=out_specs, check_vma=False)
```

time: 100 us -> 66 us (0.66)
  matrix products: 33.2 us -> 0 us
  blocking collectives: 27.5 us -> 0 us
  Pallas kernels: 0 us -> 26.1 us
  starting transfers between devices: 3.91 us -> 14.5 us
  other arithmetic: 10.2 us -> 0.05 us
  local copies, waits for them, and re-layouts: 6.64 us -> 8.49 us
  waiting for transfers between devices: 17.9 us -> 16.3 us
    dot_general x8 -> x0, matrix products: 33.2 us -> none  [the longest x1 10.7 us: body(): up_part = jnp.dot(rows, expert_up[0], preferred_element_type=jnp.float32)]
    all_to_all x1 -> x0, blocking collectives: 27.5 us -> none  [body(): lax.all_to_all(outgoing, 'pool', split_axis=0, concat_axis=0, tiled=True)]
    pallas_call x0 -> x6, Pallas kernels: none -> 26.1 us  [the longest x1 20.6 us: body(): pl.pallas_call(functools.partial(expert_kernel, chips, chunk), out_shape=...]
    all_to_all x1 -> x0, waiting for transfers between devices: 17.9 us -> none  [body(): lax.all_to_all(partial_value.astype(jnp.bfloat16), 'pool', split_axis=0,...]
    ppermute x0 -> x13, waiting for transfers between devices: none -> 16.3 us  [exchange(): return lax.ppermute(value, 'pool', [(i, i ^ bit) for i in range(devices)])]
    ppermute x0 -> x13, starting transfers between devices: none -> 14.5 us  [exchange(): return lax.ppermute(value, 'pool', [(i, i ^ bit) for i in range(devices)])]
    unnamed x8 -> x32, local copies, waits for them, and re-layouts: 0.91 us -> 7.25 us
    reduce_sum x10 -> x0, other arithmetic: 5.32 us -> none  [the longest x1 1.13 us: layer_norm(): spread = jnp.mean(centered * centered, axis=-1, keepdims=True)]
  transfers between devices with their start and end apart: 1 -> 13, of which waited for: 1 -> 10; matrix products, arithmetic and copies ran while one was open for 1% -> 1% of each run, Pallas kernels for 0% -> 1%
where the time goes in v1:
time: 66 us; the launch traced here: 65.6 us
  Pallas kernels  26.1 us (40%)
  waiting for transfers between devices  16.3 us (25%)
  starting transfers between devices  14.5 us (22%)
  local copies, waits for them, and re-layouts  8.49 us (13%)
    pallas_call x1, Pallas kernels, body(): pl.pallas_call(functools.partial(expert_kernel, chips, chunk), out_shape=...  20.6 us
    ppermute x13, waiting for transfers between devices, exchange(): return lax.ppermute(value, 'pool', [(i, i ^ bit) for i in range(devices)])  16.3 us
    ppermute x13, starting transfers between devices, exchange(): return lax.ppermute(value, 'pool', [(i, i ^ bit) for i in range(devices)])  14.5 us
    unnamed x32, local copies, waits for them, and re-layouts  7.25 us
    pallas_call x1, Pallas kernels, body(): pl.pallas_call(functools.partial(front_kernel, half), out_shape=(like(req...  3.71 us
  transfers between devices with their start and end apart: 13, of which 10 were waited for; matrix products, arithmetic and copies ran while one was open for 1% of the time, Pallas kernels for 1%

profile of v1, /device:TPU:0, one launch (start us, length us, event | category | flops | bytes accessed | tf_op | source)
XLA Modules:
  0.0 65.6 jit_solution(3787868815556312013)
XLA Ops:
  0.0 1.2 %reshape.3.kv_ref = bf16[256,1024]{1,0:T(8,128)(2,1)S(1)} reshape(bf16[128,2,1024]{2,1,0:T(2,128)(2,1)} %param.14) | data formatting | bytes 1048576 | tf_op jit(solution)/shard_map/reshape | solution.py:230
  2.0 0.9 %copy-done.1 = bf16[8,6144]{1,0:T(8,128)(2,1)S(1)} copy-done((bf16[8,6144]{1,0:T(8,128)(2,1)S(1)}, bf16[8,6144]{1,0:T(8,128)(2,1)}, u32[]{:S(2)}) %copy-start.1) | copy-done | bytes 98328
  2.9 0.9 %copy-done.2 = bf16[8,6144]{1,0:T(8,128)(2,1)S(1)} copy-done((bf16[8,6144]{1,0:T(8,128)(2,1)S(1)}, bf16[8,6144]{1,0:T(8,128)(2,1)}, u32[]{:S(2)}) %copy-start.2) | copy-done | bytes 98328
  5.9 3.7 %shard_map.109 = (f32[8,6144]{1,0:T(8,128)S(1)}, bf16[8,6144]{1,0:T(8,128)(2,1)S(1)}, bf16[4,6144]{1,0:T(4,128)(2,1)S(1)}, bf16[4,6144]{1,0:T(4,128)(2,1)S(1)}) custom-call(bf16[8,6144]{1,0:T(8,128)(2,1)S(1)} %copy-done.1, bf16[8,6144]{1,0:T(8,128)(2,1)S(1)} %copy-done.2, bf16[256,1024]{1,0:T(8,128)(2,1)S(1)} %reshape.3.kv_ref, ...), custom_call_target="tpu_custom_call" | custom-call | tf_op jit(solution)/shard_map/pallas_call | solution.py:223
  9.7 4.1 %collective-permute-start = (bf16[4,6144]{1,0:T(4,128)(2,1)S(1)}, bf16[4,6144]{1,0:T(4,128)(2,1)S(1)}, u32[]{:S(2)}, u32[]{:S(2)}) collective-permute-start(bf16[4,6144]{1,0:T(4,128)(2,1)S(1)} %get-tuple-element.20), channel_id=1, source_target_pairs={{0,8},{1,9},{2,10},{3,11},{4,12},{5,13},{6,14},{7,15},{8,0},{9,1},... | collective-permute-start | bytes 147464 | tf_op jit(solution)/shard_map/ppermute | solution.py:220
  13.8 2.6 %collective-permute-done = bf16[4,6144]{1,0:T(4,128)(2,1)S(1)} collective-permute-done((bf16[4,6144]{1,0:T(4,128)(2,1)S(1)}, bf16[4,6144]{1,0:T(4,128)(2,1)S(1)}, u32[]{:S(2)}, u32[]{:S(2)}) %collective-permute-start) | collective-permute-done | bytes 49184 | tf_op jit(solution)/shard_map/ppermute | solution.py:220
  16.4 1.8 %collective-permute-start.1 = (bf16[8,6144]{1,0:T(8,128)(2,1)S(1)}, bf16[8,6144]{1,0:T(8,128)(2,1)S(1)}, u32[]{:S(2)}, u32[]{:S(2)}) collective-permute-start(bf16[8,6144]{1,0:T(8,128)(2,1)S(1)} %pad_maximum_fusion.refs_0_), channel_id=1, source_target_pairs={{0,2},{1,3},{2,0},{3,1},{4,6},{5,7},{6,4},{7,5},{8,10},{9,11},{10,... | collective-permute-start | bytes 294920 | tf_op jit(solution)/shard_map/ppermute | solution.py:220
  18.2 1.2 %collective-permute-start.2 = (bf16[8,6144]{1,0:T(8,128)(2,1)S(1)}, bf16[8,6144]{1,0:T(8,128)(2,1)S(1)}, u32[]{:S(2)}, u32[]{:S(2)}) collective-permute-start(bf16[8,6144]{1,0:T(8,128)(2,1)S(1)} %pad_maximum_fusion.refs_0_), channel_id=1, source_target_pairs={{0,4},{1,5},{2,6},{3,7},{4,0},{5,1},{6,2},{7,3},{8,12},{9,13},{10,... | collective-permute-start | bytes 294920 | tf_op jit(solution)/shard_map/ppermute | solution.py:220
  20.0 1.3 %collective-permute-done.1.refs_1_ = bf16[8,6144]{1,0:T(8,128)(2,1)S(1)} collective-permute-done((bf16[8,6144]{1,0:T(8,128)(2,1)S(1)}, bf16[8,6144]{1,0:T(8,128)(2,1)S(1)}, u32[]{:S(2)}, u32[]{:S(2)}) %collective-permute-start.1) | collective-permute-done | bytes 98336 | tf_op jit(solution)/shard_map/ppermute | solution.py:220
  21.3 1.6 %collective-permute-done.2.refs_2_ = bf16[8,6144]{1,0:T(8,128)(2,1)S(1)} collective-permute-done((bf16[8,6144]{1,0:T(8,128)(2,1)S(1)}, bf16[8,6144]{1,0:T(8,128)(2,1)S(1)}, u32[]{:S(2)}, u32[]{:S(2)}) %collective-permute-start.2) | collective-permute-done | bytes 98336 | tf_op jit(solution)/shard_map/ppermute | solution.py:220
  22.8 2.1 %collective-permute-done.3.refs_3_ = bf16[8,6144]{1,0:T(8,128)(2,1)S(1)} collective-permute-done((bf16[8,6144]{1,0:T(8,128)(2,1)S(1)}, bf16[8,6144]{1,0:T(8,128)(2,1)S(1)}, u32[]{:S(2)}, u32[]{:S(2)}) %collective-permute-start.3) | collective-permute-done | bytes 98336 | tf_op jit(solution)/shard_map/ppermute | solution.py:220
  25.0 1.2 %collective-permute-done.7.refs_7_ = bf16[8,6144]{1,0:T(8,128)(2,1)S(1)} collective-permute-done((bf16[8,6144]{1,0:T(8,128)(2,1)S(1)}, bf16[8,6144]{1,0:T(8,128)(2,1)S(1)}, u32[]{:S(2)}, u32[]{:S(2)}) %collective-permute-start.7) | collective-permute-done | bytes 98336 | tf_op jit(solution)/shard_map/ppermute | solution.py:220
  26.9 20.6 %shard_map.111 = (f32[32,6144]{1,0:T(8,128)}, bf16[32,6144]{1,0:T(8,128)(2,1)}) custom-call(bf16[8,6144]{1,0:T(8,128)(2,1)} %copy-done.6, bf16[8,6144]{1,0:T(8,128)(2,1)} %copy-done.8, bf16[8,6144]{1,0:T(8,128)(2,1)} %copy-done.9, bf16[8,6144]{1,0:T(8,128)(2,1)} %copy-done.10, bf16[8,6144]{1,0:T(8,128)(2,1)} %copy-done.11, bf16[8,6144]{1,0:T(8,128)(2,1)} %copy-done.12, ...), custom_call_target="tpu_custom_call" | custom-call | tf_op jit(solution)/shard_map/pallas_call | solution.py:244
  47.7 1.8 %collective-permute-done.8.recv_ref = bf16[32,6144]{1,0:T(8,128)(2,1)S(1)} collective-permute-done((bf16[32,6144]{1,0:T(8,128)(2,1)}, bf16[32,6144]{1,0:T(8,128)(2,1)S(1)}, u32[]{:S(2)}, u32[]{:S(2)}) %collective-permute-start.8) | collective-permute-done | bytes 393248 | tf_op jit(solution)/shard_map/ppermute | solution.py:220
  49.5 1.1 %copy-done = f32[32,6144]{1,0:T(8,128)S(1)} copy-done((f32[32,6144]{1,0:T(8,128)S(1)}, f32[32,6144]{1,0:T(8,128)}, u32[]{:S(2)}) %copy-start) | copy-done | bytes 786456
  51.3 1.1 %collective-permute-start.10 = (bf16[8,6144]{1,0:T(8,128)(2,1)S(1)}, bf16[8,6144]{1,0:T(8,128)(2,1)S(1)}, u32[]{:S(2)}, u32[]{:S(2)}) collective-permute-start(bf16[8,6144]{1,0:T(8,128)(2,1)S(1)} %get-tuple-element.25), channel_id=1, source_target_pairs={{0,4},{1,5},{2,6},{3,7},{4,0},{5,1},{6,2},{7,3},{8,12},{9,13},{10,... | collective-permute-start | bytes 294920 | tf_op jit(solution)/shard_map/ppermute | solution.py:220
  52.4 1.9 %collective-permute-start.11 = (bf16[8,6144]{1,0:T(8,128)(2,1)S(1)}, bf16[8,6144]{1,0:T(8,128)(2,1)S(1)}, u32[]{:S(2)}, u32[]{:S(2)}) collective-permute-start(bf16[8,6144]{1,0:T(8,128)(2,1)S(1)} %get-tuple-element.26), channel_id=1, source_target_pairs={{0,6},{1,7},{2,4},{3,5},{4,2},{5,3},{6,0},{7,1},{8,14},{9,15},{10,... | collective-permute-start | bytes 294920 | tf_op jit(solution)/shard_map/ppermute | solution.py:220
  54.3 1.4 %collective-permute-done.9.refs_0_ = bf16[8,6144]{1,0:T(8,128)(2,1)S(1)} collective-permute-done((bf16[8,6144]{1,0:T(8,128)(2,1)S(1)}, bf16[8,6144]{1,0:T(8,128)(2,1)S(1)}, u32[]{:S(2)}, u32[]{:S(2)}) %collective-permute-start.9) | collective-permute-done | bytes 98336 | tf_op jit(solution)/shard_map/ppermute | solution.py:220
  55.6 1.0 %collective-permute-done.10.refs_1_ = bf16[8,6144]{1,0:T(8,128)(2,1)S(1)} collective-permute-done((bf16[8,6144]{1,0:T(8,128)(2,1)S(1)}, bf16[8,6144]{1,0:T(8,128)(2,1)S(1)}, u32[]{:S(2)}, u32[]{:S(2)}) %collective-permute-start.10) | collective-permute-done | bytes 98336 | tf_op jit(solution)/shard_map/ppermute | solution.py:220
  56.6 2.3 %collective-permute-done.11.refs_2_ = bf16[8,6144]{1,0:T(8,128)(2,1)S(1)} collective-permute-done((bf16[8,6144]{1,0:T(8,128)(2,1)S(1)}, bf16[8,6144]{1,0:T(8,128)(2,1)S(1)}, u32[]{:S(2)}, u32[]{:S(2)}) %collective-permute-start.11) | collective-permute-done | bytes 98336 | tf_op jit(solution)/shard_map/ppermute | solution.py:220
  59.0 3.1 %collective-permute-start.12 = (bf16[4,6144]{1,0:T(4,128)(2,1)S(1)}, bf16[4,6144]{1,0:T(4,128)(2,1)S(1)}, u32[]{:S(2)}, u32[]{:S(2)}) collective-permute-start(bf16[4,6144]{1,0:T(4,128)(2,1)S(1)} %get-tuple-element.28), channel_id=1, source_target_pairs={{0,8},{1,9},{2,10},{3,11},{4,12},{5,13},{6,14},{7,15},{8,0},{9,1},... | collective-permute-start | bytes 147464 | tf_op jit(solution)/shard_map/ppermute | solution.py:220
  62.0 0.8 %copy.13.router_ref = bf16[6144,16]{1,0:T(8,128)(2,1)S(1)} copy(bf16[6144,16]{0,1:T(8,128)(2,1)S(1)} %copy-done.7) | data formatting | bytes 393216 | tf_op args[7]
  63.6 1.1 %collective-permute-done.12.far_ref = bf16[4,6144]{1,0:T(4,128)(2,1)S(1)} collective-permute-done((bf16[4,6144]{1,0:T(4,128)(2,1)S(1)}, bf16[4,6144]{1,0:T(4,128)(2,1)S(1)}, u32[]{:S(2)}, u32[]{:S(2)}) %collective-permute-start.12) | collective-permute-done | bytes 49184 | tf_op jit(solution)/shard_map/ppermute | solution.py:220
  64.6 1.0 %shard_map.114 = bf16[8,6144]{1,0:T(8,128)(2,1)} custom-call(f32[8,6144]{1,0:T(8,128)S(1)} %get-tuple-element.17.residual_ref, f32[8,8]{1,0:T(8,128)S(1)} %shard_map.110.mix_ref, bf16[4,6144]{1,0:T(4,128)(2,1)S(1)} %get-tuple-element.27.near_ref, bf16[4,6144]{1,0:T(4,128)(2,1)S(1)} %collective-permute-done.12.far_ref), custom_call_target="tpu_custom_call" | custom-call | tf_op jit(solution)/shard_map/pallas_call | solution.py:276
  (42 shorter events, 5.8 us)
Async XLA Ops:
  2.0 0.9 %copy-start.1 = (bf16[8,6144]{1,0:T(8,128)(2,1)S(1)}, bf16[8,6144]{1,0:T(8,128)(2,1)}, u32[]{:S(2)}) copy-start(bf16[8,6144]{1,0:T(8,128)(2,1)} %hidden_ref.1) | copy-start | bytes 294916
  2.9 0.9 %copy-start.2 = (bf16[8,6144]{1,0:T(8,128)(2,1)S(1)}, bf16[8,6144]{1,0:T(8,128)(2,1)}, u32[]{:S(2)}) copy-start(bf16[8,6144]{1,0:T(8,128)(2,1)} %queries_ref.1) | copy-start | bytes 294916
  9.7 6.7 %collective-permute-start = (bf16[4,6144]{1,0:T(4,128)(2,1)S(1)}, bf16[4,6144]{1,0:T(4,128)(2,1)S(1)}, u32[]{:S(2)}, u32[]{:S(2)}) collective-permute-start(bf16[4,6144]{1,0:T(4,128)(2,1)S(1)} %get-tuple-element.20), channel_id=1, source_target_pairs={{0,8},{1,9},{2,10},{3,11},{4,12},{5,13},{6,14},{7,15},{8,0},{9,1},... | collective-permute-start | bytes 147464 | tf_op jit(solution)/shard_map/ppermute | solution.py:220
  16.4 9.8 %copy-start.6 = (bf16[8,6144]{1,0:T(8,128)(2,1)}, bf16[8,6144]{1,0:T(8,128)(2,1)S(1)}, u32[]{:S(2)}) copy-start(bf16[8,6144]{1,0:T(8,128)(2,1)S(1)} %pad_maximum_fusion.refs_0_) | copy-start | bytes 294916
  16.4 4.8 %collective-permute-start.1 = (bf16[8,6144]{1,0:T(8,128)(2,1)S(1)}, bf16[8,6144]{1,0:T(8,128)(2,1)S(1)}, u32[]{:S(2)}, u32[]{:S(2)}) collective-permute-start(bf16[8,6144]{1,0:T(8,128)(2,1)S(1)} %pad_maximum_fusion.refs_0_), channel_id=1, source_target_pairs={{0,2},{1,3},{2,0},{3,1},{4,6},{5,7},{6,4},{7,5},{8,10},{9,11},{10,... | collective-permute-start | bytes 294920 | tf_op jit(solution)/shard_map/ppermute | solution.py:220
  18.2 4.6 %collective-permute-start.2 = (bf16[8,6144]{1,0:T(8,128)(2,1)S(1)}, bf16[8,6144]{1,0:T(8,128)(2,1)S(1)}, u32[]{:S(2)}, u32[]{:S(2)}) collective-permute-start(bf16[8,6144]{1,0:T(8,128)(2,1)S(1)} %pad_maximum_fusion.refs_0_), channel_id=1, source_target_pairs={{0,4},{1,5},{2,6},{3,7},{4,0},{5,1},{6,2},{7,3},{8,12},{9,13},{10,... | collective-permute-start | bytes 294920 | tf_op jit(solution)/shard_map/ppermute | solution.py:220
  19.4 5.5 %collective-permute-start.3 = (bf16[8,6144]{1,0:T(8,128)(2,1)S(1)}, bf16[8,6144]{1,0:T(8,128)(2,1)S(1)}, u32[]{:S(2)}, u32[]{:S(2)}) collective-permute-start(bf16[8,6144]{1,0:T(8,128)(2,1)S(1)} %pad_maximum_fusion.refs_0_), channel_id=1, source_target_pairs={{0,6},{1,7},{2,4},{3,5},{4,2},{5,3},{6,0},{7,1},{8,14},{9,15},{10,... | collective-permute-start | bytes 294920 | tf_op jit(solution)/shard_map/ppermute | solution.py:220
  20.0 4.9 %collective-permute-start.4 = (bf16[8,6144]{1,0:T(8,128)(2,1)S(1)}, bf16[8,6144]{1,0:T(8,128)(2,1)S(1)}, u32[]{:S(2)}, u32[]{:S(2)}) collective-permute-start(bf16[8,6144]{1,0:T(8,128)(2,1)S(1)} %pad_maximum_fusion.refs_0_), channel_id=1, source_target_pairs={{0,1},{1,0},{2,3},{3,2},{4,5},{5,4},{6,7},{7,6},{8,9},{9,8},{10,11... | collective-permute-start | bytes 294920 | tf_op jit(solution)/shard_map/ppermute | solution.py:220
  21.2 5.0 %copy-start.8 = (bf16[8,6144]{1,0:T(8,128)(2,1)}, bf16[8,6144]{1,0:T(8,128)(2,1)S(1)}, u32[]{:S(2)}) copy-start(bf16[8,6144]{1,0:T(8,128)(2,1)S(1)} %collective-permute-done.1.refs_1_) | copy-start | bytes 294916
  21.2 3.7 %collective-permute-start.5 = (bf16[8,6144]{1,0:T(8,128)(2,1)S(1)}, bf16[8,6144]{1,0:T(8,128)(2,1)S(1)}, u32[]{:S(2)}, u32[]{:S(2)}) collective-permute-start(bf16[8,6144]{1,0:T(8,128)(2,1)S(1)} %collective-permute-done.1.refs_1_), channel_id=1, source_target_pairs={{0,1},{1,0},{2,3},{3,2},{4,5},{5,4},{6,7},{7,6},{8,9},{9,8},{10,11... | collective-permute-start | bytes 294920 | tf_op jit(solution)/shard_map/ppermute | solution.py:220
  22.8 3.4 %copy-start.9 = (bf16[8,6144]{1,0:T(8,128)(2,1)}, bf16[8,6144]{1,0:T(8,128)(2,1)S(1)}, u32[]{:S(2)}) copy-start(bf16[8,6144]{1,0:T(8,128)(2,1)S(1)} %collective-permute-done.2.refs_2_) | copy-start | bytes 294916
  22.8 2.1 %collective-permute-start.6 = (bf16[8,6144]{1,0:T(8,128)(2,1)S(1)}, bf16[8,6144]{1,0:T(8,128)(2,1)S(1)}, u32[]{:S(2)}, u32[]{:S(2)}) collective-permute-start(bf16[8,6144]{1,0:T(8,128)(2,1)S(1)} %collective-permute-done.2.refs_2_), channel_id=1, source_target_pairs={{0,1},{1,0},{2,3},{3,2},{4,5},{5,4},{6,7},{7,6},{8,9},{9,8},{10,11... | collective-permute-start | bytes 294920 | tf_op jit(solution)/shard_map/ppermute | solution.py:220
  24.9 1.3 %copy-start.10 = (bf16[8,6144]{1,0:T(8,128)(2,1)}, bf16[8,6144]{1,0:T(8,128)(2,1)S(1)}, u32[]{:S(2)}) copy-start(bf16[8,6144]{1,0:T(8,128)(2,1)S(1)} %collective-permute-done.3.refs_3_) | copy-start | bytes 294916
  24.9 1.3 %collective-permute-start.7 = (bf16[8,6144]{1,0:T(8,128)(2,1)S(1)}, bf16[8,6144]{1,0:T(8,128)(2,1)S(1)}, u32[]{:S(2)}, u32[]{:S(2)}) collective-permute-start(bf16[8,6144]{1,0:T(8,128)(2,1)S(1)} %collective-permute-done.3.refs_3_), channel_id=1, source_target_pairs={{0,1},{1,0},{2,3},{3,2},{4,5},{5,4},{6,7},{7,6},{8,9},{9,8},{10,11... | collective-permute-start | bytes 294920 | tf_op jit(solution)/shard_map/ppermute | solution.py:220
  24.9 1.3 %copy-start.11 = (bf16[8,6144]{1,0:T(8,128)(2,1)}, bf16[8,6144]{1,0:T(8,128)(2,1)S(1)}, u32[]{:S(2)}) copy-start(bf16[8,6144]{1,0:T(8,128)(2,1)S(1)} %collective-permute-done.4.refs_4_) | copy-start | bytes 294916
  24.9 1.3 %copy-start.12 = (bf16[8,6144]{1,0:T(8,128)(2,1)}, bf16[8,6144]{1,0:T(8,128)(2,1)S(1)}, u32[]{:S(2)}) copy-start(bf16[8,6144]{1,0:T(8,128)(2,1)S(1)} %collective-permute-done.5.refs_5_) | copy-start | bytes 294916
  25.0 1.3 %copy-start.13 = (bf16[8,6144]{1,0:T(8,128)(2,1)}, bf16[8,6144]{1,0:T(8,128)(2,1)S(1)}, u32[]{:S(2)}) copy-start(bf16[8,6144]{1,0:T(8,128)(2,1)S(1)} %collective-permute-done.6.refs_6_) | copy-start | bytes 294916
  26.9 35.2 %copy-start.7 = (bf16[6144,16]{0,1:T(8,128)(2,1)S(1)}, bf16[6144,16]{0,1:T(8,128)(2,1)}, u32[]{:S(2)}) copy-start(bf16[6144,16]{0,1:T(8,128)(2,1)} %param.18) | copy-start | bytes 589828
  47.5 2.0 %collective-permute-start.8 = (bf16[32,6144]{1,0:T(8,128)(2,1)}, bf16[32,6144]{1,0:T(8,128)(2,1)S(1)}, u32[]{:S(2)}, u32[]{:S(2)}) collective-permute-start(bf16[32,6144]{1,0:T(8,128)(2,1)} %get-tuple-element.22), channel_id=1, source_target_pairs={{0,1},{1,0},{2,3},{3,2},{4,5},{5,4},{6,7},{7,6},{8,9},{9,8},{10,11... | collective-permute-start | bytes 1179656 | tf_op jit(solution)/shard_map/ppermute | solution.py:220
  49.5 1.1 %copy-start = (f32[32,6144]{1,0:T(8,128)S(1)}, f32[32,6144]{1,0:T(8,128)}, u32[]{:S(2)}) copy-start(f32[32,6144]{1,0:T(8,128)} %get-tuple-element.21.keep_ref) | copy-start | bytes 2359300
  50.7 4.9 %collective-permute-start.9 = (bf16[8,6144]{1,0:T(8,128)(2,1)S(1)}, bf16[8,6144]{1,0:T(8,128)(2,1)S(1)}, u32[]{:S(2)}, u32[]{:S(2)}) collective-permute-start(bf16[8,6144]{1,0:T(8,128)(2,1)S(1)} %get-tuple-element.24), channel_id=1, source_target_pairs={{0,2},{1,3},{2,0},{3,1},{4,6},{5,7},{6,4},{7,5},{8,10},{9,11},{10,... | collective-permute-start | bytes 294920 | tf_op jit(solution)/shard_map/ppermute | solution.py:220
  51.3 5.3 %collective-permute-start.10 = (bf16[8,6144]{1,0:T(8,128)(2,1)S(1)}, bf16[8,6144]{1,0:T(8,128)(2,1)S(1)}, u32[]{:S(2)}, u32[]{:S(2)}) collective-permute-start(bf16[8,6144]{1,0:T(8,128)(2,1)S(1)} %get-tuple-element.25), channel_id=1, source_target_pairs={{0,4},{1,5},{2,6},{3,7},{4,0},{5,1},{6,2},{7,3},{8,12},{9,13},{10,... | collective-permute-start | bytes 294920 | tf_op jit(solution)/shard_map/ppermute | solution.py:220
  52.4 6.5 %collective-permute-start.11 = (bf16[8,6144]{1,0:T(8,128)(2,1)S(1)}, bf16[8,6144]{1,0:T(8,128)(2,1)S(1)}, u32[]{:S(2)}, u32[]{:S(2)}) collective-permute-start(bf16[8,6144]{1,0:T(8,128)(2,1)S(1)} %get-tuple-element.26), channel_id=1, source_target_pairs={{0,6},{1,7},{2,4},{3,5},{4,2},{5,3},{6,0},{7,1},{8,14},{9,15},{10,... | collective-permute-start | bytes 294920 | tf_op jit(solution)/shard_map/ppermute | solution.py:220
  59.0 5.7 %collective-permute-start.12 = (bf16[4,6144]{1,0:T(4,128)(2,1)S(1)}, bf16[4,6144]{1,0:T(4,128)(2,1)S(1)}, u32[]{:S(2)}, u32[]{:S(2)}) collective-permute-start(bf16[4,6144]{1,0:T(4,128)(2,1)S(1)} %get-tuple-element.28), channel_id=1, source_target_pairs={{0,8},{1,9},{2,10},{3,11},{4,12},{5,13},{6,14},{7,15},{8,0},{9,1},... | collective-permute-start | bytes 147464 | tf_op jit(solution)/shard_map/ppermute | solution.py:220
  (4 other events, 2.8 us)

commit v2 on v1

v2 whole, which is shorter than its diff:
```python
import functools
import math

import jax
import jax.numpy as jnp
from jax import lax
from jax.experimental import pallas as pl
from jax.experimental.pallas import tpu as pltpu
from jax.sharding import PartitionSpec as P

HEADS = 48
KV_HEADS = 8
HEAD_DIM = 128
FLIGHT = 2
CORES = 2
EPSILON = 1e-05

F32 = jnp.float32
BF16 = jnp.bfloat16
NT = (((1,), (1,)), ((), ()))
TN = (((0,), (0,)), ((), ()))
MIB = 1 << 20


def whole(space=pltpu.VMEM):
    return pl.BlockSpec(memory_space=space)


def iota(shape, dim):
    return lax.broadcasted_iota(jnp.int32, shape, dim)


def spread(rows):
    n = rows.shape[1]
    return jnp.broadcast_to(rows, (n, n)), iota((n, n), 0), iota((n, n), 1)


def to_column(values):
    wide, row, lane = spread(values)
    return jnp.sum(jnp.where(row == lane, wide, 0.0), axis=1, keepdims=True)


def slot_rows(routes, expert):
    named = jnp.max((routes == expert).astype(F32), axis=0, keepdims=True)
    column = to_column(named)
    _, row, lane = spread(named)
    before = jnp.sum(jnp.where(row < lane, column, 0.0), axis=0, keepdims=True)
    return named, before


def front_kernel(half, hidden_hbm, queries_hbm, cached_hbm, own_hbm, lengths_hbm, routes_hbm, gain_hbm,
                 residual_ref, normed_ref, near_ref, far_ref,
                 hidden_ref, queries_ref, kv_ref, own_ref, lengths_ref, routes_ref, gain_ref, wide_ref, att_ref, sems):
    pairs = (
        (lengths_hbm, lengths_ref),
        (queries_hbm, queries_ref),
        (cached_hbm.reshape(kv_ref.shape), kv_ref),
        (own_hbm.reshape(own_ref.shape), own_ref),
        (hidden_hbm, hidden_ref),
        (gain_hbm, gain_ref),
        (routes_hbm, routes_ref),
    )
    copies = [pltpu.make_async_copy(src, dst, sems.at[i]) for i, (src, dst) in enumerate(pairs)]
    for copy in copies:
        copy.start()
    requests, width = hidden_ref.shape
    groups = HEADS // KV_HEADS
    positions = kv_ref.shape[0]
    scale = 1.0 / math.sqrt(HEAD_DIM)
    row, lane = iota((requests, requests), 0), iota((requests, requests), 1)
    copies[0].wait()
    lengths = jnp.broadcast_to(lengths_ref[...], (requests, requests))
    starts = jnp.sum(jnp.where(lane < row, lengths, 0), axis=1, keepdims=True)
    ends = starts + jnp.sum(jnp.where(lane == row, lengths, 0), axis=1, keepdims=True)
    column = iota((requests, positions), 1)
    inside = (column >= 2 * starts) & (column < 2 * ends) & (column % 2 == 0)
    bias = jnp.where(inside, 0.0, -jnp.inf).astype(F32)
    bias = jnp.concatenate([bias] * groups, axis=0)
    copies[1].wait()
    queries = queries_ref[...].astype(F32)
    copies[3].wait()
    for head in range(KV_HEADS):
        wide_ref[head] = own_ref[:, head * HEAD_DIM:(head + 1) * HEAD_DIM].astype(F32)
    copies[2].wait()
    for head in range(KV_HEADS):
        spot = slice(head * HEAD_DIM, (head + 1) * HEAD_DIM)
        block = kv_ref[:, spot]
        parts = [queries[:, (head * groups + j) * HEAD_DIM:(head * groups + j + 1) * HEAD_DIM] for j in range(groups)]
        stacked = jnp.concatenate(parts, axis=0)
        keys = jnp.concatenate([wide_ref[head, pl.ds(0, requests, stride=2), :]] * groups, axis=0)
        scores = lax.dot_general(stacked.astype(BF16), block, NT, preferred_element_type=F32) * scale + bias
        own_score = jnp.sum(stacked * keys, axis=1, keepdims=True) * scale
        peak = jnp.maximum(jnp.max(scores, axis=1, keepdims=True), own_score)
        expos = jnp.exp(scores - peak)
        own_expo = jnp.exp(own_score - peak)
        total = jnp.sum(expos, axis=1, keepdims=True) + own_expo
        weights = pltpu.roll(expos / total, 1, 1).astype(BF16)
        own_weight = (own_expo / total).astype(BF16).astype(F32)
        summed = jnp.dot(weights, block, preferred_element_type=F32)
        summed = summed + own_weight * jnp.concatenate([wide_ref[head, pl.ds(1, requests, stride=2), :]] * groups, axis=0)
        for j in range(groups):
            at = (head * groups + j) * HEAD_DIM
            att_ref[:, at:at + HEAD_DIM] = summed[j * requests:(j + 1) * requests].astype(BF16).astype(F32)
    copies[4].wait()
    residual = hidden_ref[...].astype(F32) + att_ref[...]
    residual_ref[...] = residual
    centered = residual - jnp.mean(residual, axis=1, keepdims=True)
    spread_of = jnp.mean(centered * centered, axis=1, keepdims=True)
    copies[5].wait()
    normed = (centered * lax.rsqrt(spread_of + EPSILON) * gain_ref[...]).astype(BF16)
    normed_ref[...] = normed
    copies[6].wait()
    mine = half()
    capacity = near_ref.shape[0]
    slot = iota((capacity, requests), 0).astype(F32)
    for expert, out in ((mine, near_ref), (1 - mine, far_ref)):
        named, before = slot_rows(routes_ref[...], expert)
        placing = jnp.where(before == slot, named, 0.0).astype(BF16)
        out[...] = jnp.dot(placing, normed, preferred_element_type=F32).astype(BF16)


def gate_kernel(half, normed_ref, router_ref, routes_ref, mix_ref):
    routes = routes_ref[...]
    fanout, requests = routes.shape
    experts = router_ref.shape[0]
    capacity = mix_ref.shape[1] // FLIGHT
    logits = lax.dot_general(normed_ref[...], router_ref[...], NT, preferred_element_type=F32)
    lane = iota((requests, experts), 1).astype(F32)
    columns = [to_column(routes[k:k + 1].astype(F32)) for k in range(fanout)]
    routed = [jnp.sum(jnp.where(lane == columns[k], logits, 0.0), axis=1, keepdims=True) for k in range(fanout)]
    gates = [1.0 / sum(jnp.exp(routed[j] - routed[k]) for j in range(fanout)) for k in range(fanout)]
    mine = half()
    column = iota((requests, FLIGHT * capacity), 1)
    mix = jnp.zeros((requests, FLIGHT * capacity), F32)
    for turn, expert in enumerate((mine, 1 - mine)):
        named, before = slot_rows(routes, expert)
        named, before = to_column(named), to_column(before)
        gate = jnp.zeros((requests, 1), F32)
        for k in range(fanout):
            gate = jnp.where(columns[k] == expert.astype(F32), gates[k], gate)
        place = (column - turn * capacity).astype(F32)
        mix = jnp.where((before == place) & (named > 0.0), gate, mix)
    mix_ref[...] = mix


def join_kernel(near_ref, arrived_ref, out_ref):
    out_ref[...] = jnp.concatenate([near_ref[...], arrived_ref[...]], axis=0)


def expert_kernel(chips, chunk, *refs):
    pieces = refs[:2 * chips]
    gate_ref, up_ref, down_ref, keep_ref, send_ref, rows_ref, inner_ref = refs[2 * chips:]
    hidden, width = gate_ref.shape
    steps = hidden // chunk
    count = pieces[0].shape[0]
    for i, piece in enumerate(pieces):
        rows_ref[i * count:(i + 1) * count, :] = piece[...]
    for i in range(steps):
        at = slice(i * chunk, (i + 1) * chunk)
        rows = rows_ref[...]
        gate_part = lax.dot_general(gate_ref[at], rows, NT, preferred_element_type=F32)
        up_part = lax.dot_general(up_ref[at], rows, NT, preferred_element_type=F32)
        inner = gate_part / (1.0 + jnp.exp(-gate_part)) * up_part
        inner_ref[:, at] = inner.T.astype(BF16)
    part = width // 8 if width % 1024 == 0 else width
    for i in range(width // part):
        at = slice(i * part, (i + 1) * part)
        out = jnp.dot(inner_ref[...], down_ref[:, at], preferred_element_type=F32)
        keep_ref[:, at] = out[:chips * count]
        send_ref[:, at] = out[chips * count:].astype(BF16)


def core_sum_kernel(keep_ref, recv_ref, first_ref, *rest):
    count = first_ref.shape[0]
    total = keep_ref[...] + recv_ref[...].astype(F32)
    first_ref[...] = total[:count]
    for i, out in enumerate(rest):
        out[...] = total[(i + 1) * count:(i + 2) * count].astype(BF16)


def chip_sum_kernel(first_ref, *refs):
    *parts, near_ref, far_ref = refs
    total = first_ref[...]
    for part in parts:
        total = total + part[...].astype(F32)
    capacity = near_ref.shape[0]
    near_ref[...] = total[:capacity].astype(BF16)
    far_ref[...] = total[capacity:].astype(BF16)


def mix_kernel(residual_ref, mix_ref, near_ref, far_ref, out_ref):
    mix = mix_ref[...]
    capacity = near_ref.shape[0]
    total = jnp.zeros(residual_ref.shape, F32)
    for i, ref in enumerate((near_ref, far_ref)):
        rows = ref[...].astype(F32)
        for j in range(capacity):
            at = i * capacity + j
            total = total + mix[:, at:at + 1] * rows[j:j + 1]
    out_ref[...] = (residual_ref[...] + total).astype(BF16)


def like(*shape, dtype=BF16):
    return jax.ShapeDtypeStruct(shape, dtype)


def params(mib):
    return pltpu.CompilerParams(vmem_limit_bytes=mib * MIB)


def body(
    hidden_state,
    queries,
    new_entries,
    cached,
    cache_lengths,
    routes,
    norm_gain,
    router_weight,
    expert_gate,
    expert_up,
    expert_down,
):
    requests, width = hidden_state.shape
    devices = lax.axis_size("pool")
    group = devices // FLIGHT
    chips = group // CORES
    experts = router_weight.shape[1]
    fanout = routes.shape[1]
    capacity = min(requests, 2 * requests * fanout // experts)
    count = 2 * capacity
    hidden = expert_gate.shape[2]

    tight = 6 * hidden * width > 24 * MIB

    def half():
        return lax.axis_index("pool") // group

    def exchange(value, bit):
        return lax.ppermute(value, "pool", [(i, i ^ bit) for i in range(devices)])

    positions = cached.shape[0]
    heads = cached.shape[2]
    weights = [
        pltpu.with_memory_space_constraint(w, pltpu.VMEM)
        for w in (jnp.swapaxes(expert_gate, 1, 2)[0], jnp.swapaxes(expert_up, 1, 2)[0], expert_down[0])
    ]
    routes = routes.T
    front = (hidden_state, queries, cached, new_entries, cache_lengths, routes, norm_gain[None])
    residual, normed, near, far = pl.pallas_call(
        functools.partial(front_kernel, half),
        out_shape=(like(requests, width, dtype=F32), like(requests, width), like(capacity, width), like(capacity, width)),
        in_specs=[whole(pltpu.HBM)] * 7,
        out_specs=(whole(),) * 4,
        scratch_shapes=[
            pltpu.VMEM((requests, width), BF16),
            pltpu.VMEM((requests, width), BF16),
            pltpu.VMEM((2 * positions, heads), BF16),
            pltpu.VMEM((2 * requests, heads), BF16),
            pltpu.VMEM((1, requests), jnp.int32),
            pltpu.VMEM((fanout, requests), jnp.int32),
            pltpu.VMEM((1, width), F32),
            pltpu.VMEM((KV_HEADS, 2 * requests, HEAD_DIM), F32),
            pltpu.VMEM((requests, width), F32),
            pltpu.SemaphoreType.DMA((7,)),
        ],
        compiler_params=params(2 if tight else 24),
        cost_estimate=pl.CostEstimate(flops=200_000_000_000, bytes_accessed=50_000_000, transcendentals=0),
    )(*(pltpu.with_memory_space_constraint(x, pltpu.HBM) for x in front))
    arrived = exchange(far, group)
    mix = pl.pallas_call(
        functools.partial(gate_kernel, half),
        out_shape=like(requests, count, dtype=F32),
        in_specs=[whole()] * 3,
        out_specs=whole(),
        compiler_params=params(2 if tight else 24),
    )(normed, router_weight.T, routes)
    own = pl.pallas_call(
        join_kernel,
        out_shape=like(count, width),
        in_specs=[whole()] * 2,
        out_specs=whole(),
        compiler_params=params(2 if tight else 24),
    )(near, arrived)
    mine = [own] + [exchange(own, CORES * j) for j in range(1, chips)]
    beside = [exchange(piece, 1) for piece in mine]
    chunk = hidden // 6 if hidden % 96 == 0 else hidden
    steps = hidden // chunk
    keep, send = pl.pallas_call(
        functools.partial(expert_kernel, chips, chunk),
        out_shape=(like(chips * count, width, dtype=F32), like(chips * count, width)),
        in_specs=[whole()] * (2 * chips + 3),
        out_specs=(whole(), whole()),
        scratch_shapes=[
            pltpu.VMEM((2 * chips * count, width), BF16),
            pltpu.VMEM((2 * chips * count, hidden), BF16),
        ],
        compiler_params=params(3 if tight else 24),
    )(*mine, *beside, *weights)
    recv = exchange(send, 1)
    first, *rest = pl.pallas_call(
        core_sum_kernel,
        out_shape=(like(count, width, dtype=F32),) + (like(count, width),) * (chips - 1),
        in_specs=[whole()] * 2,
        out_specs=(whole(),) * chips,
        compiler_params=params(2 if tight else 24),
    )(pltpu.with_memory_space_constraint(keep, pltpu.VMEM), recv)
    parts = [exchange(piece, CORES * (j + 1)) for j, piece in enumerate(rest)]
    near_out, far_out = pl.pallas_call(
        chip_sum_kernel,
        out_shape=(like(capacity, width), like(capacity, width)),
        in_specs=[whole()] * chips,
        out_specs=(whole(), whole()),
        compiler_params=params(2 if tight else 24),
    )(first, *parts)
    back = exchange(far_out, group)
    return pl.pallas_call(
        mix_kernel,
        out_shape=like(requests, width),
        in_specs=[whole()] * 4,
        out_specs=whole(),
        compiler_params=params(2 if tight else 24),
    )(residual, mix, near_out, back)


def solution(mesh):
    in_specs = (
        P(("rep", "pool"), None),
        P(("rep", "pool"), None),
        P(("rep", "pool"), None, None),
        P(("rep", "pool"), None, None),
        P(("rep", "pool"), None),
        P(("rep", "pool"), None),
        P(),
        P(),
        P("pool", None, None),
        P("pool", None, None),
        P("pool", None, None),
    )
    out_specs = P(("rep", "pool"), None)
    return jax.shard_map(body, mesh=mesh, in_specs=in_specs, out_specs=out_specs, check_vma=False)
```

time: 66 us -> 49.2 us (0.75)
  local copies, waits for them, and re-layouts: 8.49 us -> 0.02 us
  Pallas kernels: 26.1 us -> 18.3 us
    pallas_call x1, Pallas kernels: 20.6 us -> 11.7 us  [body(): pl.pallas_call(functools.partial(expert_kernel, chips, chunk), out_shape=...]
    unnamed x32 -> x10, local copies, waits for them, and re-layouts: 7.25 us -> 0.02 us
    pallas_call x1, Pallas kernels: 3.71 us -> 5.22 us  [body(): pl.pallas_call(functools.partial(front_kernel, half), out_shape=(like(req...]
    reshape x1 -> x0, local copies, waits for them, and re-layouts: 1.24 us -> none  [body(): cached.reshape(2 * positions, -1)]
  transfers between devices with their start and end apart: 13 -> 13, of which waited for: 10 -> 11; matrix products, arithmetic and copies ran while one was open for 1% -> 0% of each run, Pallas kernels for 1% -> 1%
where the time goes in v2:
time: 49.2 us; the launch traced here: 49 us
  Pallas kernels  18.3 us (37%)
  waiting for transfers between devices  16.6 us (34%)
  starting transfers between devices  14 us (28%)
    ppermute x13, waiting for transfers between devices, exchange(): return lax.ppermute(value, 'pool', [(i, i ^ bit) for i in range(devices)])  16.6 us
    ppermute x13, starting transfers between devices, exchange(): return lax.ppermute(value, 'pool', [(i, i ^ bit) for i in range(devices)])  14 us
    pallas_call x1, Pallas kernels, body(): pl.pallas_call(functools.partial(expert_kernel, chips, chunk), out_shape=...  11.7 us
    pallas_call x1, Pallas kernels, body(): pl.pallas_call(functools.partial(front_kernel, half), out_shape=(like(req...  5.22 us
  transfers between devices with their start and end apart: 13, of which 11 were waited for; matrix products, arithmetic and copies ran while one was open for 0% of the time, Pallas kernels for 1%

profile of v2, /device:TPU:0, one launch (start us, length us, event | category | flops | bytes accessed | tf_op | source)
XLA Modules:
  0.0 49.0 jit_solution(14618600781922790990)
XLA Ops:
  0.0 5.2 %shard_map.109 = (f32[8,6144]{1,0:T(8,128)S(1)}, bf16[8,6144]{1,0:T(8,128)(2,1)S(1)}, bf16[4,6144]{1,0:T(4,128)(2,1)S(1)}, bf16[4,6144]{1,0:T(4,128)(2,1)S(1)}) custom-call(bf16[8,6144]{1,0:T(8,128)(2,1)} %hidden_hbm.1, bf16[8,6144]{1,0:T(8,128)(2,1)} %queries_hbm.1, bf16[128,2,1024]{2,1,0:T(2,128)(2,1)} %cached_hbm.1, bf16[8,2,1024]{2,1,0:T(2,128)(2,1)} %own_hbm.1, ...), custom_call_target="tpu_custom_call" | custom-call | flops 199999995904 | bytes 50000000 | tf_op jit(solution)/shard_map/pallas_call | solution.py:250
  5.2 4.1 %collective-permute-start = (bf16[4,6144]{1,0:T(4,128)(2,1)S(1)}, bf16[4,6144]{1,0:T(4,128)(2,1)S(1)}, u32[]{:S(2)}, u32[]{:S(2)}) collective-permute-start(bf16[4,6144]{1,0:T(4,128)(2,1)S(1)} %get-tuple-element.20), channel_id=1, source_target_pairs={{0,8},{1,9},{2,10},{3,11},{4,12},{5,13},{6,14},{7,15},{8,0},{9,1},... | collective-permute-start | bytes 147464 | tf_op jit(solution)/shard_map/ppermute | solution.py:240
  9.3 2.6 %collective-permute-done.arrived_ref = bf16[4,6144]{1,0:T(4,128)(2,1)S(1)} collective-permute-done((bf16[4,6144]{1,0:T(4,128)(2,1)S(1)}, bf16[4,6144]{1,0:T(4,128)(2,1)S(1)}, u32[]{:S(2)}, u32[]{:S(2)}) %collective-permute-start) | collective-permute-done | bytes 49184 | tf_op jit(solution)/shard_map/ppermute | solution.py:240
  12.0 2.4 %collective-permute-start.3 = (bf16[8,6144]{1,0:T(8,128)(2,1)S(1)}, bf16[8,6144]{1,0:T(8,128)(2,1)S(1)}, u32[]{:S(2)}, u32[]{:S(2)}) collective-permute-start(bf16[8,6144]{1,0:T(8,128)(2,1)S(1)} %shard_map.111.refs_0_), channel_id=1, source_target_pairs={{0,6},{1,7},{2,4},{3,5},{4,2},{5,3},{6,0},{7,1},{8,14},{9,15},{10,... | collective-permute-start | bytes 294920 | tf_op jit(solution)/shard_map/ppermute | solution.py:240
  14.4 0.8 %collective-permute-start.2 = (bf16[8,6144]{1,0:T(8,128)(2,1)S(1)}, bf16[8,6144]{1,0:T(8,128)(2,1)S(1)}, u32[]{:S(2)}, u32[]{:S(2)}) collective-permute-start(bf16[8,6144]{1,0:T(8,128)(2,1)S(1)} %shard_map.111.refs_0_), channel_id=1, source_target_pairs={{0,4},{1,5},{2,6},{3,7},{4,0},{5,1},{6,2},{7,3},{8,12},{9,13},{10,... | collective-permute-start | bytes 294920 | tf_op jit(solution)/shard_map/ppermute | solution.py:240
  15.2 0.3 collective-permute-start.1
  15.5 2.1 %collective-permute-done.3.refs_3_ = bf16[8,6144]{1,0:T(8,128)(2,1)S(1)} collective-permute-done((bf16[8,6144]{1,0:T(8,128)(2,1)S(1)}, bf16[8,6144]{1,0:T(8,128)(2,1)S(1)}, u32[]{:S(2)}, u32[]{:S(2)}) %collective-permute-start.3) | collective-permute-done | bytes 98336 | tf_op jit(solution)/shard_map/ppermute | solution.py:240
  17.7 1.3 %collective-permute-done.2.refs_2_ = bf16[8,6144]{1,0:T(8,128)(2,1)S(1)} collective-permute-done((bf16[8,6144]{1,0:T(8,128)(2,1)S(1)}, bf16[8,6144]{1,0:T(8,128)(2,1)S(1)}, u32[]{:S(2)}, u32[]{:S(2)}) %collective-permute-start.2) | collective-permute-done | bytes 98336 | tf_op jit(solution)/shard_map/ppermute | solution.py:240
  19.0 0.8 %collective-permute-done.1.refs_1_ = bf16[8,6144]{1,0:T(8,128)(2,1)S(1)} collective-permute-done((bf16[8,6144]{1,0:T(8,128)(2,1)S(1)}, bf16[8,6144]{1,0:T(8,128)(2,1)S(1)}, u32[]{:S(2)}, u32[]{:S(2)}) %collective-permute-start.1) | collective-permute-done | bytes 98336 | tf_op jit(solution)/shard_map/ppermute | solution.py:240
  19.9 0.4 collective-permute-done.6.refs_6_
  20.3 0.8 %collective-permute-done.5.refs_5_ = bf16[8,6144]{1,0:T(8,128)(2,1)S(1)} collective-permute-done((bf16[8,6144]{1,0:T(8,128)(2,1)S(1)}, bf16[8,6144]{1,0:T(8,128)(2,1)S(1)}, u32[]{:S(2)}, u32[]{:S(2)}) %collective-permute-start.5) | collective-permute-done | bytes 98336 | tf_op jit(solution)/shard_map/ppermute | solution.py:240
  21.2 11.7 %shard_map.112 = (f32[32,6144]{1,0:T(8,128)S(1)}, bf16[32,6144]{1,0:T(8,128)(2,1)S(1)}) custom-call(bf16[8,6144]{1,0:T(8,128)(2,1)S(1)} %shard_map.111.refs_0_, bf16[8,6144]{1,0:T(8,128)(2,1)S(1)} %collective-permute-done.1.refs_1_, bf16[8,6144]{1,0:T(8,128)(2,1)S(1)} %collective-permute-done.2.refs_2_, bf16[8,6144]{1,0:T(8,128)(2,1)S(1)} %collective-permute-done.3.refs_3_, ...), custom_call_target="tpu_custom_call" | custom-call | tf_op jit(solution)/shard_map/pallas_call | solution.py:289
  32.9 0.2 collective-permute-start.8
  33.1 1.6 %collective-permute-done.8.recv_ref = bf16[32,6144]{1,0:T(8,128)(2,1)S(1)} collective-permute-done((bf16[32,6144]{1,0:T(8,128)(2,1)S(1)}, bf16[32,6144]{1,0:T(8,128)(2,1)S(1)}, u32[]{:S(2)}, u32[]{:S(2)}) %collective-permute-start.8) | collective-permute-done | bytes 393248 | tf_op jit(solution)/shard_map/ppermute | solution.py:240
  34.7 0.6 %collective-permute-start.9 = (bf16[8,6144]{1,0:T(8,128)(2,1)S(1)}, bf16[8,6144]{1,0:T(8,128)(2,1)S(1)}, u32[]{:S(2)}, u32[]{:S(2)}) collective-permute-start(bf16[8,6144]{1,0:T(8,128)(2,1)S(1)} %get-tuple-element.24), channel_id=1, source_target_pairs={{0,2},{1,3},{2,0},{3,1},{4,6},{5,7},{6,4},{7,5},{8,10},{9,11},{10,... | collective-permute-start | bytes 294920 | tf_op jit(solution)/shard_map/ppermute | solution.py:240
  35.3 1.2 %collective-permute-start.10 = (bf16[8,6144]{1,0:T(8,128)(2,1)S(1)}, bf16[8,6144]{1,0:T(8,128)(2,1)S(1)}, u32[]{:S(2)}, u32[]{:S(2)}) collective-permute-start(bf16[8,6144]{1,0:T(8,128)(2,1)S(1)} %get-tuple-element.25), channel_id=1, source_target_pairs={{0,4},{1,5},{2,6},{3,7},{4,0},{5,1},{6,2},{7,3},{8,12},{9,13},{10,... | collective-permute-start | bytes 294920 | tf_op jit(solution)/shard_map/ppermute | solution.py:240
  36.5 1.8 %collective-permute-start.11 = (bf16[8,6144]{1,0:T(8,128)(2,1)S(1)}, bf16[8,6144]{1,0:T(8,128)(2,1)S(1)}, u32[]{:S(2)}, u32[]{:S(2)}) collective-permute-start(bf16[8,6144]{1,0:T(8,128)(2,1)S(1)} %get-tuple-element.26), channel_id=1, source_target_pairs={{0,6},{1,7},{2,4},{3,5},{4,2},{5,3},{6,0},{7,1},{8,14},{9,15},{10,... | collective-permute-start | bytes 294920 | tf_op jit(solution)/shard_map/ppermute | solution.py:240
  38.3 1.4 %collective-permute-done.9.refs_0_ = bf16[8,6144]{1,0:T(8,128)(2,1)S(1)} collective-permute-done((bf16[8,6144]{1,0:T(8,128)(2,1)S(1)}, bf16[8,6144]{1,0:T(8,128)(2,1)S(1)}, u32[]{:S(2)}, u32[]{:S(2)}) %collective-permute-start.9) | collective-permute-done | bytes 98336 | tf_op jit(solution)/shard_map/ppermute | solution.py:240
  39.7 0.6 %collective-permute-done.10.refs_1_ = bf16[8,6144]{1,0:T(8,128)(2,1)S(1)} collective-permute-done((bf16[8,6144]{1,0:T(8,128)(2,1)S(1)}, bf16[8,6144]{1,0:T(8,128)(2,1)S(1)}, u32[]{:S(2)}, u32[]{:S(2)}) %collective-permute-start.10) | collective-permute-done | bytes 98336 | tf_op jit(solution)/shard_map/ppermute | solution.py:240
  40.2 2.7 %collective-permute-done.11.refs_2_ = bf16[8,6144]{1,0:T(8,128)(2,1)S(1)} collective-permute-done((bf16[8,6144]{1,0:T(8,128)(2,1)S(1)}, bf16[8,6144]{1,0:T(8,128)(2,1)S(1)}, u32[]{:S(2)}, u32[]{:S(2)}) %collective-permute-start.11) | collective-permute-done | bytes 98336 | tf_op jit(solution)/shard_map/ppermute | solution.py:240
  43.0 2.6 %collective-permute-start.12 = (bf16[4,6144]{1,0:T(4,128)(2,1)S(1)}, bf16[4,6144]{1,0:T(4,128)(2,1)S(1)}, u32[]{:S(2)}, u32[]{:S(2)}) collective-permute-start(bf16[4,6144]{1,0:T(4,128)(2,1)S(1)} %get-tuple-element.28), channel_id=1, source_target_pairs={{0,8},{1,9},{2,10},{3,11},{4,12},{5,13},{6,14},{7,15},{8,0},{9,1},... | collective-permute-start | bytes 147464 | tf_op jit(solution)/shard_map/ppermute | solution.py:240
  45.6 0.3 shard_map.110.mix_ref
  45.9 2.2 %collective-permute-done.12.far_ref = bf16[4,6144]{1,0:T(4,128)(2,1)S(1)} collective-permute-done((bf16[4,6144]{1,0:T(4,128)(2,1)S(1)}, bf16[4,6144]{1,0:T(4,128)(2,1)S(1)}, u32[]{:S(2)}, u32[]{:S(2)}) %collective-permute-start.12) | collective-permute-done | bytes 49184 | tf_op jit(solution)/shard_map/ppermute | solution.py:240
  48.1 1.0 %shard_map.115 = bf16[8,6144]{1,0:T(8,128)(2,1)} custom-call(f32[8,6144]{1,0:T(8,128)S(1)} %get-tuple-element.17.residual_ref, f32[8,8]{1,0:T(8,128)S(1)} %shard_map.110.mix_ref, bf16[4,6144]{1,0:T(4,128)(2,1)S(1)} %get-tuple-element.27.near_ref, bf16[4,6144]{1,0:T(4,128)(2,1)S(1)} %collective-permute-done.12.far_ref), custom_call_target="tpu_custom_call" | custom-call | tf_op jit(solution)/shard_map/pallas_call | solution.py:317
  (19 shorter events, 0.2 us)
Async XLA Ops:
  0.0 21.1 %copy-start = (bf16[1,6144,1344]{1,2,0:T(8,128)(2,1)S(1)}, bf16[1,6144,1344]{1,2,0:T(8,128)(2,1)}, u32[]{:S(2)}) copy-start(bf16[1,6144,1344]{1,2,0:T(8,128)(2,1)} %param.19) | copy-start | bytes 49545220
  0.0 21.1 %copy-start.1 = (bf16[1,6144,1344]{1,2,0:T(8,128)(2,1)S(1)}, bf16[1,6144,1344]{1,2,0:T(8,128)(2,1)}, u32[]{:S(2)}) copy-start(bf16[1,6144,1344]{1,2,0:T(8,128)(2,1)} %param.20) | copy-start | bytes 49545220
  0.0 21.1 %copy-start.2 = (bf16[1,1344,6144]{2,1,0:T(8,128)(2,1)S(1)}, bf16[1,1344,6144]{2,1,0:T(8,128)(2,1)}, u32[]{:S(2)}) copy-start(bf16[1,1344,6144]{2,1,0:T(8,128)(2,1)} %param.21) | copy-start | bytes 49545220
  5.2 6.7 %collective-permute-start = (bf16[4,6144]{1,0:T(4,128)(2,1)S(1)}, bf16[4,6144]{1,0:T(4,128)(2,1)S(1)}, u32[]{:S(2)}, u32[]{:S(2)}) collective-permute-start(bf16[4,6144]{1,0:T(4,128)(2,1)S(1)} %get-tuple-element.20), channel_id=1, source_target_pairs={{0,8},{1,9},{2,10},{3,11},{4,12},{5,13},{6,14},{7,15},{8,0},{9,1},... | collective-permute-start | bytes 147464 | tf_op jit(solution)/shard_map/ppermute | solution.py:240
  12.0 5.7 %collective-permute-start.3 = (bf16[8,6144]{1,0:T(8,128)(2,1)S(1)}, bf16[8,6144]{1,0:T(8,128)(2,1)S(1)}, u32[]{:S(2)}, u32[]{:S(2)}) collective-permute-start(bf16[8,6144]{1,0:T(8,128)(2,1)S(1)} %shard_map.111.refs_0_), channel_id=1, source_target_pairs={{0,6},{1,7},{2,4},{3,5},{4,2},{5,3},{6,0},{7,1},{8,14},{9,15},{10,... | collective-permute-start | bytes 294920 | tf_op jit(solution)/shard_map/ppermute | solution.py:240
  14.4 4.6 %collective-permute-start.2 = (bf16[8,6144]{1,0:T(8,128)(2,1)S(1)}, bf16[8,6144]{1,0:T(8,128)(2,1)S(1)}, u32[]{:S(2)}, u32[]{:S(2)}) collective-permute-start(bf16[8,6144]{1,0:T(8,128)(2,1)S(1)} %shard_map.111.refs_0_), channel_id=1, source_target_pairs={{0,4},{1,5},{2,6},{3,7},{4,0},{5,1},{6,2},{7,3},{8,12},{9,13},{10,... | collective-permute-start | bytes 294920 | tf_op jit(solution)/shard_map/ppermute | solution.py:240
  15.2 4.6 %collective-permute-start.1 = (bf16[8,6144]{1,0:T(8,128)(2,1)S(1)}, bf16[8,6144]{1,0:T(8,128)(2,1)S(1)}, u32[]{:S(2)}, u32[]{:S(2)}) collective-permute-start(bf16[8,6144]{1,0:T(8,128)(2,1)S(1)} %shard_map.111.refs_0_), channel_id=1, source_target_pairs={{0,2},{1,3},{2,0},{3,1},{4,6},{5,7},{6,4},{7,5},{8,10},{9,11},{10,... | collective-permute-start | bytes 294920 | tf_op jit(solution)/shard_map/ppermute | solution.py:240
  15.5 4.3 %collective-permute-start.4 = (bf16[8,6144]{1,0:T(8,128)(2,1)S(1)}, bf16[8,6144]{1,0:T(8,128)(2,1)S(1)}, u32[]{:S(2)}, u32[]{:S(2)}) collective-permute-start(bf16[8,6144]{1,0:T(8,128)(2,1)S(1)} %shard_map.111.refs_0_), channel_id=1, source_target_pairs={{0,1},{1,0},{2,3},{3,2},{4,5},{5,4},{6,7},{7,6},{8,9},{9,8},{10,11... | collective-permute-start | bytes 294920 | tf_op jit(solution)/shard_map/ppermute | solution.py:240
  17.6 2.2 %collective-permute-start.7 = (bf16[8,6144]{1,0:T(8,128)(2,1)S(1)}, bf16[8,6144]{1,0:T(8,128)(2,1)S(1)}, u32[]{:S(2)}, u32[]{:S(2)}) collective-permute-start(bf16[8,6144]{1,0:T(8,128)(2,1)S(1)} %collective-permute-done.3.refs_3_), channel_id=1, source_target_pairs={{0,1},{1,0},{2,3},{3,2},{4,5},{5,4},{6,7},{7,6},{8,9},{9,8},{10,11... | collective-permute-start | bytes 294920 | tf_op jit(solution)/shard_map/ppermute | solution.py:240
  19.0 1.3 %collective-permute-start.6 = (bf16[8,6144]{1,0:T(8,128)(2,1)S(1)}, bf16[8,6144]{1,0:T(8,128)(2,1)S(1)}, u32[]{:S(2)}, u32[]{:S(2)}) collective-permute-start(bf16[8,6144]{1,0:T(8,128)(2,1)S(1)} %collective-permute-done.2.refs_2_), channel_id=1, source_target_pairs={{0,1},{1,0},{2,3},{3,2},{4,5},{5,4},{6,7},{7,6},{8,9},{9,8},{10,11... | collective-permute-start | bytes 294920 | tf_op jit(solution)/shard_map/ppermute | solution.py:240
  19.8 1.3 %collective-permute-start.5 = (bf16[8,6144]{1,0:T(8,128)(2,1)S(1)}, bf16[8,6144]{1,0:T(8,128)(2,1)S(1)}, u32[]{:S(2)}, u32[]{:S(2)}) collective-permute-start(bf16[8,6144]{1,0:T(8,128)(2,1)S(1)} %collective-permute-done.1.refs_1_), channel_id=1, source_target_pairs={{0,1},{1,0},{2,3},{3,2},{4,5},{5,4},{6,7},{7,6},{8,9},{9,8},{10,11... | collective-permute-start | bytes 294920 | tf_op jit(solution)/shard_map/ppermute | solution.py:240
  21.2 24.4 %copy-start.3 = (bf16[6144,16]{0,1:T(8,128)(2,1)S(1)}, bf16[6144,16]{0,1:T(8,128)(2,1)}, u32[]{:S(2)}) copy-start(bf16[6144,16]{0,1:T(8,128)(2,1)} %param.18) | copy-start | bytes 589828
  21.2 24.4 %copy-start.4 = (s32[8,4]{0,1:T(4,128)S(1)}, s32[8,4]{0,1:T(4,128)}, u32[]{:S(2)}) copy-start(s32[8,4]{0,1:T(4,128)} %param.16) | copy-start | bytes 388
  32.9 1.8 %collective-permute-start.8 = (bf16[32,6144]{1,0:T(8,128)(2,1)S(1)}, bf16[32,6144]{1,0:T(8,128)(2,1)S(1)}, u32[]{:S(2)}, u32[]{:S(2)}) collective-permute-start(bf16[32,6144]{1,0:T(8,128)(2,1)S(1)} %get-tuple-element.22), channel_id=1, source_target_pairs={{0,1},{1,0},{2,3},{3,2},{4,5},{5,4},{6,7},{7,6},{8,9},{9,8},{10,11... | collective-permute-start | bytes 1179656 | tf_op jit(solution)/shard_map/ppermute | solution.py:240
  34.7 4.9 %collective-permute-start.9 = (bf16[8,6144]{1,0:T(8,128)(2,1)S(1)}, bf16[8,6144]{1,0:T(8,128)(2,1)S(1)}, u32[]{:S(2)}, u32[]{:S(2)}) collective-permute-start(bf16[8,6144]{1,0:T(8,128)(2,1)S(1)} %get-tuple-element.24), channel_id=1, source_target_pairs={{0,2},{1,3},{2,0},{3,1},{4,6},{5,7},{6,4},{7,5},{8,10},{9,11},{10,... | collective-permute-start | bytes 294920 | tf_op jit(solution)/shard_map/ppermute | solution.py:240
  35.3 4.9 %collective-permute-start.10 = (bf16[8,6144]{1,0:T(8,128)(2,1)S(1)}, bf16[8,6144]{1,0:T(8,128)(2,1)S(1)}, u32[]{:S(2)}, u32[]{:S(2)}) collective-permute-start(bf16[8,6144]{1,0:T(8,128)(2,1)S(1)} %get-tuple-element.25), channel_id=1, source_target_pairs={{0,4},{1,5},{2,6},{3,7},{4,0},{5,1},{6,2},{7,3},{8,12},{9,13},{10,... | collective-permute-start | bytes 294920 | tf_op jit(solution)/shard_map/ppermute | solution.py:240
  36.5 6.5 %collective-permute-start.11 = (bf16[8,6144]{1,0:T(8,128)(2,1)S(1)}, bf16[8,6144]{1,0:T(8,128)(2,1)S(1)}, u32[]{:S(2)}, u32[]{:S(2)}) collective-permute-start(bf16[8,6144]{1,0:T(8,128)(2,1)S(1)} %get-tuple-element.26), channel_id=1, source_target_pairs={{0,6},{1,7},{2,4},{3,5},{4,2},{5,3},{6,0},{7,1},{8,14},{9,15},{10,... | collective-permute-start | bytes 294920 | tf_op jit(solution)/shard_map/ppermute | solution.py:240
  43.0 5.1 %collective-permute-start.12 = (bf16[4,6144]{1,0:T(4,128)(2,1)S(1)}, bf16[4,6144]{1,0:T(4,128)(2,1)S(1)}, u32[]{:S(2)}, u32[]{:S(2)}) collective-permute-start(bf16[4,6144]{1,0:T(4,128)(2,1)S(1)} %get-tuple-element.28), channel_id=1, source_target_pairs={{0,8},{1,9},{2,10},{3,11},{4,12},{5,13},{6,14},{7,15},{8,0},{9,1},... | collective-permute-start | bytes 147464 | tf_op jit(solution)/shard_map/ppermute | solution.py:240

commit v3 on v2

--- a/solution.py
+++ b/solution.py
@@ -82,21 +82,26 @@
     for head in range(KV_HEADS):
         wide_ref[head] = own_ref[:, head * HEAD_DIM:(head + 1) * HEAD_DIM].astype(F32)
     copies[2].wait()
-    for head in range(KV_HEADS):
-        spot = slice(head * HEAD_DIM, (head + 1) * HEAD_DIM)
-        block = kv_ref[:, spot]
-        parts = [queries[:, (head * groups + j) * HEAD_DIM:(head * groups + j + 1) * HEAD_DIM] for j in range(groups)]
-        stacked = jnp.concatenate(parts, axis=0)
-        keys = jnp.concatenate([wide_ref[head, pl.ds(0, requests, stride=2), :]] * groups, axis=0)
-        scores = lax.dot_general(stacked.astype(BF16), block, NT, preferred_element_type=F32) * scale + bias
-        own_score = jnp.sum(stacked * keys, axis=1, keepdims=True) * scale
+    heads = range(KV_HEADS)
+    blocks = [kv_ref[:, head * HEAD_DIM:(head + 1) * HEAD_DIM] for head in heads]
+    stacks = []
+    for head in heads:
+        at = head * groups * HEAD_DIM
+        stacks.append(jnp.concatenate([queries[:, at + j * HEAD_DIM:at + (j + 1) * HEAD_DIM] for j in range(groups)], axis=0))
+    keys = [jnp.concatenate([wide_ref[head, pl.ds(0, requests, stride=2), :]] * groups, axis=0) for head in heads]
+    raw = [lax.dot_general(s.astype(BF16), k, NT, preferred_element_type=F32) for s, k in zip(stacks, blocks)]
+    own_scores = [jnp.sum(s * k, axis=1, keepdims=True) * scale for s, k in zip(stacks, keys)]
+    weights, own_weights = [], []
+    for r, own_score in zip(raw, own_scores):
+        scores = r * scale + bias
         peak = jnp.maximum(jnp.max(scores, axis=1, keepdims=True), own_score)
         expos = jnp.exp(scores - peak)
         own_expo = jnp.exp(own_score - peak)
         total = jnp.sum(expos, axis=1, keepdims=True) + own_expo
-        weights = pltpu.roll(expos / total, 1, 1).astype(BF16)
-        own_weight = (own_expo / total).astype(BF16).astype(F32)
-        summed = jnp.dot(weights, block, preferred_element_type=F32)
+        weights.append(pltpu.roll(expos / total, 1, 1).astype(BF16))
+        own_weights.append((own_expo / total).astype(BF16).astype(F32))
+    sums = [jnp.dot(w, k, preferred_element_type=F32) for w, k in zip(weights, blocks)]
+    for head, summed, own_weight in zip(heads, sums, own_weights):
         summed = summed + own_weight * jnp.concatenate([wide_ref[head, pl.ds(1, requests, stride=2), :]] * groups, axis=0)
         for j in range(groups):
             at = (head * groups + j) * HEAD_DIM

time: 49.2 us -> 46.6 us (0.947)
  Pallas kernels: 18.3 us -> 15.8 us
    pallas_call x1, Pallas kernels: 5.22 us -> 2.66 us  [body(): pl.pallas_call(functools.partial(front_kernel, half), out_shape=(like(req...]
where the time goes in v3:
time: 46.6 us; the launch traced here: 46.5 us
  waiting for transfers between devices  16.6 us (36%)
  Pallas kernels  15.8 us (34%)
  starting transfers between devices  14 us (30%)
    ppermute x13, waiting for transfers between devices, exchange(): return lax.ppermute(value, 'pool', [(i, i ^ bit) for i in range(devices)])  16.6 us
    ppermute x13, starting transfers between devices, exchange(): return lax.ppermute(value, 'pool', [(i, i ^ bit) for i in range(devices)])  14 us
    pallas_call x1, Pallas kernels, body(): pl.pallas_call(functools.partial(expert_kernel, chips, chunk), out_shape=...  11.7 us
    pallas_call x1, Pallas kernels, body(): pl.pallas_call(functools.partial(front_kernel, half), out_shape=(like(req...  2.66 us
    pallas_call x1, Pallas kernels, body(): pl.pallas_call(mix_kernel, out_shape=like(requests, width), in_specs=[who...  0.96 us
  transfers between devices with their start and end apart: 13, of which 11 were waited for; matrix products, arithmetic and copies ran while one was open for 0% of the time, Pallas kernels for 1%

profile of v3, /device:TPU:0, one launch (start us, length us, event | category | flops | bytes accessed | tf_op | source)
XLA Modules:
  0.0 46.5 jit_solution(1906113578669530898)
XLA Ops:
  0.0 2.7 %shard_map.109 = (f32[8,6144]{1,0:T(8,128)S(1)}, bf16[8,6144]{1,0:T(8,128)(2,1)S(1)}, bf16[4,6144]{1,0:T(4,128)(2,1)S(1)}, bf16[4,6144]{1,0:T(4,128)(2,1)S(1)}) custom-call(bf16[8,6144]{1,0:T(8,128)(2,1)} %hidden_hbm.1, bf16[8,6144]{1,0:T(8,128)(2,1)} %queries_hbm.1, bf16[128,2,1024]{2,1,0:T(2,128)(2,1)} %cached_hbm.1, bf16[8,2,1024]{2,1,0:T(2,128)(2,1)} %own_hbm.1, ...), custom_call_target="tpu_custom_call" | custom-call | flops 199999995904 | bytes 50000000 | tf_op jit(solution)/shard_map/pallas_call | solution.py:255
  2.7 4.1 %collective-permute-start = (bf16[4,6144]{1,0:T(4,128)(2,1)S(1)}, bf16[4,6144]{1,0:T(4,128)(2,1)S(1)}, u32[]{:S(2)}, u32[]{:S(2)}) collective-permute-start(bf16[4,6144]{1,0:T(4,128)(2,1)S(1)} %get-tuple-element.20), channel_id=1, source_target_pairs={{0,8},{1,9},{2,10},{3,11},{4,12},{5,13},{6,14},{7,15},{8,0},{9,1},... | collective-permute-start | bytes 147464 | tf_op jit(solution)/shard_map/ppermute | solution.py:245
  6.8 2.6 %collective-permute-done.arrived_ref = bf16[4,6144]{1,0:T(4,128)(2,1)S(1)} collective-permute-done((bf16[4,6144]{1,0:T(4,128)(2,1)S(1)}, bf16[4,6144]{1,0:T(4,128)(2,1)S(1)}, u32[]{:S(2)}, u32[]{:S(2)}) %collective-permute-start) | collective-permute-done | bytes 49184 | tf_op jit(solution)/shard_map/ppermute | solution.py:245
  9.4 2.4 %collective-permute-start.3 = (bf16[8,6144]{1,0:T(8,128)(2,1)S(1)}, bf16[8,6144]{1,0:T(8,128)(2,1)S(1)}, u32[]{:S(2)}, u32[]{:S(2)}) collective-permute-start(bf16[8,6144]{1,0:T(8,128)(2,1)S(1)} %shard_map.111.refs_0_), channel_id=1, source_target_pairs={{0,6},{1,7},{2,4},{3,5},{4,2},{5,3},{6,0},{7,1},{8,14},{9,15},{10,... | collective-permute-start | bytes 294920 | tf_op jit(solution)/shard_map/ppermute | solution.py:245
  11.8 0.9 %collective-permute-start.2 = (bf16[8,6144]{1,0:T(8,128)(2,1)S(1)}, bf16[8,6144]{1,0:T(8,128)(2,1)S(1)}, u32[]{:S(2)}, u32[]{:S(2)}) collective-permute-start(bf16[8,6144]{1,0:T(8,128)(2,1)S(1)} %shard_map.111.refs_0_), channel_id=1, source_target_pairs={{0,4},{1,5},{2,6},{3,7},{4,0},{5,1},{6,2},{7,3},{8,12},{9,13},{10,... | collective-permute-start | bytes 294920 | tf_op jit(solution)/shard_map/ppermute | solution.py:245
  12.7 0.3 collective-permute-start.1
  13.0 2.1 %collective-permute-done.3.refs_3_ = bf16[8,6144]{1,0:T(8,128)(2,1)S(1)} collective-permute-done((bf16[8,6144]{1,0:T(8,128)(2,1)S(1)}, bf16[8,6144]{1,0:T(8,128)(2,1)S(1)}, u32[]{:S(2)}, u32[]{:S(2)}) %collective-permute-start.3) | collective-permute-done | bytes 98336 | tf_op jit(solution)/shard_map/ppermute | solution.py:245
  15.1 1.3 %collective-permute-done.2.refs_2_ = bf16[8,6144]{1,0:T(8,128)(2,1)S(1)} collective-permute-done((bf16[8,6144]{1,0:T(8,128)(2,1)S(1)}, bf16[8,6144]{1,0:T(8,128)(2,1)S(1)}, u32[]{:S(2)}, u32[]{:S(2)}) %collective-permute-start.2) | collective-permute-done | bytes 98336 | tf_op jit(solution)/shard_map/ppermute | solution.py:245
  16.4 0.9 %collective-permute-done.1.refs_1_ = bf16[8,6144]{1,0:T(8,128)(2,1)S(1)} collective-permute-done((bf16[8,6144]{1,0:T(8,128)(2,1)S(1)}, bf16[8,6144]{1,0:T(8,128)(2,1)S(1)}, u32[]{:S(2)}, u32[]{:S(2)}) %collective-permute-start.1) | collective-permute-done | bytes 98336 | tf_op jit(solution)/shard_map/ppermute | solution.py:245
  17.3 0.4 collective-permute-done.6.refs_6_
  17.7 0.9 %collective-permute-done.5.refs_5_ = bf16[8,6144]{1,0:T(8,128)(2,1)S(1)} collective-permute-done((bf16[8,6144]{1,0:T(8,128)(2,1)S(1)}, bf16[8,6144]{1,0:T(8,128)(2,1)S(1)}, u32[]{:S(2)}, u32[]{:S(2)}) %collective-permute-start.5) | collective-permute-done | bytes 98336 | tf_op jit(solution)/shard_map/ppermute | solution.py:245
  18.6 11.7 %shard_map.112 = (f32[32,6144]{1,0:T(8,128)S(1)}, bf16[32,6144]{1,0:T(8,128)(2,1)S(1)}) custom-call(bf16[8,6144]{1,0:T(8,128)(2,1)S(1)} %shard_map.111.refs_0_, bf16[8,6144]{1,0:T(8,128)(2,1)S(1)} %collective-permute-done.1.refs_1_, bf16[8,6144]{1,0:T(8,128)(2,1)S(1)} %collective-permute-done.2.refs_2_, bf16[8,6144]{1,0:T(8,128)(2,1)S(1)} %collective-permute-done.3.refs_3_, ...), custom_call_target="tpu_custom_call" | custom-call | tf_op jit(solution)/shard_map/pallas_call | solution.py:294
  30.3 0.2 collective-permute-start.8
  30.5 1.6 %collective-permute-done.8.recv_ref = bf16[32,6144]{1,0:T(8,128)(2,1)S(1)} collective-permute-done((bf16[32,6144]{1,0:T(8,128)(2,1)S(1)}, bf16[32,6144]{1,0:T(8,128)(2,1)S(1)}, u32[]{:S(2)}, u32[]{:S(2)}) %collective-permute-start.8) | collective-permute-done | bytes 393248 | tf_op jit(solution)/shard_map/ppermute | solution.py:245
  32.2 0.6 %collective-permute-start.9 = (bf16[8,6144]{1,0:T(8,128)(2,1)S(1)}, bf16[8,6144]{1,0:T(8,128)(2,1)S(1)}, u32[]{:S(2)}, u32[]{:S(2)}) collective-permute-start(bf16[8,6144]{1,0:T(8,128)(2,1)S(1)} %get-tuple-element.24), channel_id=1, source_target_pairs={{0,2},{1,3},{2,0},{3,1},{4,6},{5,7},{6,4},{7,5},{8,10},{9,11},{10,... | collective-permute-start | bytes 294920 | tf_op jit(solution)/shard_map/ppermute | solution.py:245
  32.8 1.2 %collective-permute-start.10 = (bf16[8,6144]{1,0:T(8,128)(2,1)S(1)}, bf16[8,6144]{1,0:T(8,128)(2,1)S(1)}, u32[]{:S(2)}, u32[]{:S(2)}) collective-permute-start(bf16[8,6144]{1,0:T(8,128)(2,1)S(1)} %get-tuple-element.25), channel_id=1, source_target_pairs={{0,4},{1,5},{2,6},{3,7},{4,0},{5,1},{6,2},{7,3},{8,12},{9,13},{10,... | collective-permute-start | bytes 294920 | tf_op jit(solution)/shard_map/ppermute | solution.py:245
  33.9 1.8 %collective-permute-start.11 = (bf16[8,6144]{1,0:T(8,128)(2,1)S(1)}, bf16[8,6144]{1,0:T(8,128)(2,1)S(1)}, u32[]{:S(2)}, u32[]{:S(2)}) collective-permute-start(bf16[8,6144]{1,0:T(8,128)(2,1)S(1)} %get-tuple-element.26), channel_id=1, source_target_pairs={{0,6},{1,7},{2,4},{3,5},{4,2},{5,3},{6,0},{7,1},{8,14},{9,15},{10,... | collective-permute-start | bytes 294920 | tf_op jit(solution)/shard_map/ppermute | solution.py:245
  35.7 1.4 %collective-permute-done.9.refs_0_ = bf16[8,6144]{1,0:T(8,128)(2,1)S(1)} collective-permute-done((bf16[8,6144]{1,0:T(8,128)(2,1)S(1)}, bf16[8,6144]{1,0:T(8,128)(2,1)S(1)}, u32[]{:S(2)}, u32[]{:S(2)}) %collective-permute-start.9) | collective-permute-done | bytes 98336 | tf_op jit(solution)/shard_map/ppermute | solution.py:245
  37.1 0.6 %collective-permute-done.10.refs_1_ = bf16[8,6144]{1,0:T(8,128)(2,1)S(1)} collective-permute-done((bf16[8,6144]{1,0:T(8,128)(2,1)S(1)}, bf16[8,6144]{1,0:T(8,128)(2,1)S(1)}, u32[]{:S(2)}, u32[]{:S(2)}) %collective-permute-start.10) | collective-permute-done | bytes 98336 | tf_op jit(solution)/shard_map/ppermute | solution.py:245
  37.7 2.7 %collective-permute-done.11.refs_2_ = bf16[8,6144]{1,0:T(8,128)(2,1)S(1)} collective-permute-done((bf16[8,6144]{1,0:T(8,128)(2,1)S(1)}, bf16[8,6144]{1,0:T(8,128)(2,1)S(1)}, u32[]{:S(2)}, u32[]{:S(2)}) %collective-permute-start.11) | collective-permute-done | bytes 98336 | tf_op jit(solution)/shard_map/ppermute | solution.py:245
  40.5 2.6 %collective-permute-start.12 = (bf16[4,6144]{1,0:T(4,128)(2,1)S(1)}, bf16[4,6144]{1,0:T(4,128)(2,1)S(1)}, u32[]{:S(2)}, u32[]{:S(2)}) collective-permute-start(bf16[4,6144]{1,0:T(4,128)(2,1)S(1)} %get-tuple-element.28), channel_id=1, source_target_pairs={{0,8},{1,9},{2,10},{3,11},{4,12},{5,13},{6,14},{7,15},{8,0},{9,1},... | collective-permute-start | bytes 147464 | tf_op jit(solution)/shard_map/ppermute | solution.py:245
  43.0 0.3 shard_map.110.mix_ref
  43.3 2.2 %collective-permute-done.12.far_ref = bf16[4,6144]{1,0:T(4,128)(2,1)S(1)} collective-permute-done((bf16[4,6144]{1,0:T(4,128)(2,1)S(1)}, bf16[4,6144]{1,0:T(4,128)(2,1)S(1)}, u32[]{:S(2)}, u32[]{:S(2)}) %collective-permute-start.12) | collective-permute-done | bytes 49184 | tf_op jit(solution)/shard_map/ppermute | solution.py:245
  45.5 1.0 %shard_map.115 = bf16[8,6144]{1,0:T(8,128)(2,1)} custom-call(f32[8,6144]{1,0:T(8,128)S(1)} %get-tuple-element.17.residual_ref, f32[8,8]{1,0:T(8,128)S(1)} %shard_map.110.mix_ref, bf16[4,6144]{1,0:T(4,128)(2,1)S(1)} %get-tuple-element.27.near_ref, bf16[4,6144]{1,0:T(4,128)(2,1)S(1)} %collective-permute-done.12.far_ref), custom_call_target="tpu_custom_call" | custom-call | tf_op jit(solution)/shard_map/pallas_call | solution.py:322
  (19 shorter events, 0.2 us)
Async XLA Ops:
  0.0 18.6 %copy-start = (bf16[1,6144,1344]{1,2,0:T(8,128)(2,1)S(1)}, bf16[1,6144,1344]{1,2,0:T(8,128)(2,1)}, u32[]{:S(2)}) copy-start(bf16[1,6144,1344]{1,2,0:T(8,128)(2,1)} %param.19) | copy-start | bytes 49545220
  0.0 18.6 %copy-start.1 = (bf16[1,6144,1344]{1,2,0:T(8,128)(2,1)S(1)}, bf16[1,6144,1344]{1,2,0:T(8,128)(2,1)}, u32[]{:S(2)}) copy-start(bf16[1,6144,1344]{1,2,0:T(8,128)(2,1)} %param.20) | copy-start | bytes 49545220
  0.0 18.6 %copy-start.2 = (bf16[1,1344,6144]{2,1,0:T(8,128)(2,1)S(1)}, bf16[1,1344,6144]{2,1,0:T(8,128)(2,1)}, u32[]{:S(2)}) copy-start(bf16[1,1344,6144]{2,1,0:T(8,128)(2,1)} %param.21) | copy-start | bytes 49545220
  2.7 6.7 %collective-permute-start = (bf16[4,6144]{1,0:T(4,128)(2,1)S(1)}, bf16[4,6144]{1,0:T(4,128)(2,1)S(1)}, u32[]{:S(2)}, u32[]{:S(2)}) collective-permute-start(bf16[4,6144]{1,0:T(4,128)(2,1)S(1)} %get-tuple-element.20), channel_id=1, source_target_pairs={{0,8},{1,9},{2,10},{3,11},{4,12},{5,13},{6,14},{7,15},{8,0},{9,1},... | collective-permute-start | bytes 147464 | tf_op jit(solution)/shard_map/ppermute | solution.py:245
  9.4 5.7 %collective-permute-start.3 = (bf16[8,6144]{1,0:T(8,128)(2,1)S(1)}, bf16[8,6144]{1,0:T(8,128)(2,1)S(1)}, u32[]{:S(2)}, u32[]{:S(2)}) collective-permute-start(bf16[8,6144]{1,0:T(8,128)(2,1)S(1)} %shard_map.111.refs_0_), channel_id=1, source_target_pairs={{0,6},{1,7},{2,4},{3,5},{4,2},{5,3},{6,0},{7,1},{8,14},{9,15},{10,... | collective-permute-start | bytes 294920 | tf_op jit(solution)/shard_map/ppermute | solution.py:245
  11.8 4.6 %collective-permute-start.2 = (bf16[8,6144]{1,0:T(8,128)(2,1)S(1)}, bf16[8,6144]{1,0:T(8,128)(2,1)S(1)}, u32[]{:S(2)}, u32[]{:S(2)}) collective-permute-start(bf16[8,6144]{1,0:T(8,128)(2,1)S(1)} %shard_map.111.refs_0_), channel_id=1, source_target_pairs={{0,4},{1,5},{2,6},{3,7},{4,0},{5,1},{6,2},{7,3},{8,12},{9,13},{10,... | collective-permute-start | bytes 294920 | tf_op jit(solution)/shard_map/ppermute | solution.py:245
  12.7 4.6 %collective-permute-start.1 = (bf16[8,6144]{1,0:T(8,128)(2,1)S(1)}, bf16[8,6144]{1,0:T(8,128)(2,1)S(1)}, u32[]{:S(2)}, u32[]{:S(2)}) collective-permute-start(bf16[8,6144]{1,0:T(8,128)(2,1)S(1)} %shard_map.111.refs_0_), channel_id=1, source_target_pairs={{0,2},{1,3},{2,0},{3,1},{4,6},{5,7},{6,4},{7,5},{8,10},{9,11},{10,... | collective-permute-start | bytes 294920 | tf_op jit(solution)/shard_map/ppermute | solution.py:245
  13.0 4.3 %collective-permute-start.4 = (bf16[8,6144]{1,0:T(8,128)(2,1)S(1)}, bf16[8,6144]{1,0:T(8,128)(2,1)S(1)}, u32[]{:S(2)}, u32[]{:S(2)}) collective-permute-start(bf16[8,6144]{1,0:T(8,128)(2,1)S(1)} %shard_map.111.refs_0_), channel_id=1, source_target_pairs={{0,1},{1,0},{2,3},{3,2},{4,5},{5,4},{6,7},{7,6},{8,9},{9,8},{10,11... | collective-permute-start | bytes 294920 | tf_op jit(solution)/shard_map/ppermute | solution.py:245
  15.1 2.2 %collective-permute-start.7 = (bf16[8,6144]{1,0:T(8,128)(2,1)S(1)}, bf16[8,6144]{1,0:T(8,128)(2,1)S(1)}, u32[]{:S(2)}, u32[]{:S(2)}) collective-permute-start(bf16[8,6144]{1,0:T(8,128)(2,1)S(1)} %collective-permute-done.3.refs_3_), channel_id=1, source_target_pairs={{0,1},{1,0},{2,3},{3,2},{4,5},{5,4},{6,7},{7,6},{8,9},{9,8},{10,11... | collective-permute-start | bytes 294920 | tf_op jit(solution)/shard_map/ppermute | solution.py:245
  16.4 1.3 %collective-permute-start.6 = (bf16[8,6144]{1,0:T(8,128)(2,1)S(1)}, bf16[8,6144]{1,0:T(8,128)(2,1)S(1)}, u32[]{:S(2)}, u32[]{:S(2)}) collective-permute-start(bf16[8,6144]{1,0:T(8,128)(2,1)S(1)} %collective-permute-done.2.refs_2_), channel_id=1, source_target_pairs={{0,1},{1,0},{2,3},{3,2},{4,5},{5,4},{6,7},{7,6},{8,9},{9,8},{10,11... | collective-permute-start | bytes 294920 | tf_op jit(solution)/shard_map/ppermute | solution.py:245
  17.3 1.3 %collective-permute-start.5 = (bf16[8,6144]{1,0:T(8,128)(2,1)S(1)}, bf16[8,6144]{1,0:T(8,128)(2,1)S(1)}, u32[]{:S(2)}, u32[]{:S(2)}) collective-permute-start(bf16[8,6144]{1,0:T(8,128)(2,1)S(1)} %collective-permute-done.1.refs_1_), channel_id=1, source_target_pairs={{0,1},{1,0},{2,3},{3,2},{4,5},{5,4},{6,7},{7,6},{8,9},{9,8},{10,11... | collective-permute-start | bytes 294920 | tf_op jit(solution)/shard_map/ppermute | solution.py:245
  18.6 24.4 %copy-start.3 = (bf16[6144,16]{0,1:T(8,128)(2,1)S(1)}, bf16[6144,16]{0,1:T(8,128)(2,1)}, u32[]{:S(2)}) copy-start(bf16[6144,16]{0,1:T(8,128)(2,1)} %param.18) | copy-start | bytes 589828
  18.6 24.4 %copy-start.4 = (s32[8,4]{0,1:T(4,128)S(1)}, s32[8,4]{0,1:T(4,128)}, u32[]{:S(2)}) copy-start(s32[8,4]{0,1:T(4,128)} %param.16) | copy-start | bytes 388
  30.3 1.8 %collective-permute-start.8 = (bf16[32,6144]{1,0:T(8,128)(2,1)S(1)}, bf16[32,6144]{1,0:T(8,128)(2,1)S(1)}, u32[]{:S(2)}, u32[]{:S(2)}) collective-permute-start(bf16[32,6144]{1,0:T(8,128)(2,1)S(1)} %get-tuple-element.22), channel_id=1, source_target_pairs={{0,1},{1,0},{2,3},{3,2},{4,5},{5,4},{6,7},{7,6},{8,9},{9,8},{10,11... | collective-permute-start | bytes 1179656 | tf_op jit(solution)/shard_map/ppermute | solution.py:245
  32.2 4.9 %collective-permute-start.9 = (bf16[8,6144]{1,0:T(8,128)(2,1)S(1)}, bf16[8,6144]{1,0:T(8,128)(2,1)S(1)}, u32[]{:S(2)}, u32[]{:S(2)}) collective-permute-start(bf16[8,6144]{1,0:T(8,128)(2,1)S(1)} %get-tuple-element.24), channel_id=1, source_target_pairs={{0,2},{1,3},{2,0},{3,1},{4,6},{5,7},{6,4},{7,5},{8,10},{9,11},{10,... | collective-permute-start | bytes 294920 | tf_op jit(solution)/shard_map/ppermute | solution.py:245
  32.8 5.0 %collective-permute-start.10 = (bf16[8,6144]{1,0:T(8,128)(2,1)S(1)}, bf16[8,6144]{1,0:T(8,128)(2,1)S(1)}, u32[]{:S(2)}, u32[]{:S(2)}) collective-permute-start(bf16[8,6144]{1,0:T(8,128)(2,1)S(1)} %get-tuple-element.25), channel_id=1, source_target_pairs={{0,4},{1,5},{2,6},{3,7},{4,0},{5,1},{6,2},{7,3},{8,12},{9,13},{10,... | collective-permute-start | bytes 294920 | tf_op jit(solution)/shard_map/ppermute | solution.py:245
  33.9 6.5 %collective-permute-start.11 = (bf16[8,6144]{1,0:T(8,128)(2,1)S(1)}, bf16[8,6144]{1,0:T(8,128)(2,1)S(1)}, u32[]{:S(2)}, u32[]{:S(2)}) collective-permute-start(bf16[8,6144]{1,0:T(8,128)(2,1)S(1)} %get-tuple-element.26), channel_id=1, source_target_pairs={{0,6},{1,7},{2,4},{3,5},{4,2},{5,3},{6,0},{7,1},{8,14},{9,15},{10,... | collective-permute-start | bytes 294920 | tf_op jit(solution)/shard_map/ppermute | solution.py:245
  40.5 5.1 %collective-permute-start.12 = (bf16[4,6144]{1,0:T(4,128)(2,1)S(1)}, bf16[4,6144]{1,0:T(4,128)(2,1)S(1)}, u32[]{:S(2)}, u32[]{:S(2)}) collective-permute-start(bf16[4,6144]{1,0:T(4,128)(2,1)S(1)} %get-tuple-element.28), channel_id=1, source_target_pairs={{0,8},{1,9},{2,10},{3,11},{4,12},{5,13},{6,14},{7,15},{8,0},{9,1},... | collective-permute-start | bytes 147464 | tf_op jit(solution)/shard_map/ppermute | solution.py:245

commit v4 on v3

--- a/solution.py
+++ b/solution.py
@@ -124,11 +124,10 @@
         out[...] = jnp.dot(placing, normed, preferred_element_type=F32).astype(BF16)
 
 
-def gate_kernel(half, normed_ref, router_ref, routes_ref, mix_ref):
+def gate_mix(half, normed_ref, router_ref, routes_ref, capacity):
     routes = routes_ref[...]
     fanout, requests = routes.shape
     experts = router_ref.shape[0]
-    capacity = mix_ref.shape[1] // FLIGHT
     logits = lax.dot_general(normed_ref[...], router_ref[...], NT, preferred_element_type=F32)
     lane = iota((requests, experts), 1).astype(F32)
     columns = [to_column(routes[k:k + 1].astype(F32)) for k in range(fanout)]
@@ -145,64 +144,85 @@
             gate = jnp.where(columns[k] == expert.astype(F32), gates[k], gate)
         place = (column - turn * capacity).astype(F32)
         mix = jnp.where((before == place) & (named > 0.0), gate, mix)
-    mix_ref[...] = mix
+    return mix
 
 
 def join_kernel(near_ref, arrived_ref, out_ref):
     out_ref[...] = jnp.concatenate([near_ref[...], arrived_ref[...]], axis=0)
 
 
+def project(inner_ref, down_ref, keep_ref, send_ref, start):
+    rows = inner_ref[...]
+    half = rows.shape[0] // 2
+    doubled = jnp.concatenate([rows, rows], axis=0)
+    width = keep_ref.shape[1]
+    part = 1024 if width % 1024 == 0 else width
+    for i in range(width // part):
+        at = slice(i * part, (i + 1) * part)
+        out = jnp.dot(doubled, down_ref[:, start + i * part:start + (i + 1) * part], preferred_element_type=F32)
+        keep_ref[:, at] = out[:half]
+        send_ref[:, at] = out[half:2 * half].astype(BF16)
+
+
 def expert_kernel(chips, chunk, *refs):
     pieces = refs[:2 * chips]
-    gate_ref, up_ref, down_ref, keep_ref, send_ref, rows_ref, inner_ref = refs[2 * chips:]
+    gate_ref, up_ref, down_ref, inner_ref, keep_ref, send_ref, rows_ref = refs[2 * chips:]
     hidden, width = gate_ref.shape
-    steps = hidden // chunk
     count = pieces[0].shape[0]
     for i, piece in enumerate(pieces):
         rows_ref[i * count:(i + 1) * count, :] = piece[...]
-    for i in range(steps):
+    for i in range(hidden // chunk):
         at = slice(i * chunk, (i + 1) * chunk)
         rows = rows_ref[...]
         gate_part = lax.dot_general(gate_ref[at], rows, NT, preferred_element_type=F32)
         up_part = lax.dot_general(up_ref[at], rows, NT, preferred_element_type=F32)
         inner = gate_part / (1.0 + jnp.exp(-gate_part)) * up_part
         inner_ref[:, at] = inner.T.astype(BF16)
-    part = width // 8 if width % 1024 == 0 else width
-    for i in range(width // part):
-        at = slice(i * part, (i + 1) * part)
-        out = jnp.dot(inner_ref[...], down_ref[:, at], preferred_element_type=F32)
-        keep_ref[:, at] = out[:chips * count]
-        send_ref[:, at] = out[chips * count:].astype(BF16)
-
-
-def core_sum_kernel(keep_ref, recv_ref, first_ref, *rest):
-    count = first_ref.shape[0]
-    total = keep_ref[...] + recv_ref[...].astype(F32)
-    first_ref[...] = total[:count]
-    for i, out in enumerate(rest):
-        out[...] = total[(i + 1) * count:(i + 2) * count].astype(BF16)
-
-
-def chip_sum_kernel(first_ref, *refs):
-    *parts, near_ref, far_ref = refs
-    total = first_ref[...]
+    project(inner_ref, down_ref, keep_ref, send_ref, 0)
+
+
+def rest_kernel(start, inner_ref, down_ref, keep_ref, send_ref):
+    project(inner_ref, down_ref, keep_ref, send_ref, start)
+
+
+def core_sum_kernel(keep_ref, recv_ref, keep_rest_ref, recv_rest_ref, near_ref, far_ref, *rest):
+    capacity = near_ref.shape[0]
+    start = keep_ref.shape[1]
+    for keep, recv, at in (
+        (keep_ref, recv_ref, slice(0, start)),
+        (keep_rest_ref, recv_rest_ref, slice(start, near_ref.shape[1])),
+    ):
+        total = keep[...] + recv[...].astype(F32)
+        for i, out in enumerate((near_ref, far_ref) + rest):
+            out[:, at] = total[i * capacity:(i + 1) * capacity].astype(out.dtype)
+
+
+def far_sum_kernel(far_ref, *refs):
+    *parts, out_ref = refs
+    total = far_ref[...]
     for part in parts:
         total = total + part[...].astype(F32)
-    capacity = near_ref.shape[0]
-    near_ref[...] = total[:capacity].astype(BF16)
-    far_ref[...] = total[capacity:].astype(BF16)
-
-
-def mix_kernel(residual_ref, mix_ref, near_ref, far_ref, out_ref):
-    mix = mix_ref[...]
-    capacity = near_ref.shape[0]
-    total = jnp.zeros(residual_ref.shape, F32)
-    for i, ref in enumerate((near_ref, far_ref)):
-        rows = ref[...].astype(F32)
-        for j in range(capacity):
-            at = i * capacity + j
-            total = total + mix[:, at:at + 1] * rows[j:j + 1]
-    out_ref[...] = (residual_ref[...] + total).astype(BF16)
+    out_ref[...] = total.astype(BF16)
+
+
+def weighted(mix, rows, start):
+    terms = [mix[:, start + j:start + j + 1] * rows[j:j + 1] for j in range(rows.shape[0])]
+    return sum(terms[1:], terms[0])
+
+
+def near_kernel(half, residual_ref, normed_ref, router_ref, routes_ref, near_ref, *refs):
+    *parts, base_ref, mix_ref = refs
+    mix = gate_mix(half, normed_ref, router_ref, routes_ref, near_ref.shape[0])
+    mix_ref[...] = mix
+    total = near_ref[...]
+    for part in parts:
+        total = total + part[...].astype(F32)
+    base_ref[...] = residual_ref[...] + weighted(mix, total.astype(BF16).astype(F32), 0)
+
+
+def mix_kernel(base_ref, mix_ref, far_ref, out_ref):
+    rows = far_ref[...].astype(F32)
+    out_ref[...] = (base_ref[...] + weighted(mix_ref[...], rows, rows.shape[0])).astype(BF16)
 
 
 def like(*shape, dtype=BF16):
@@ -273,13 +293,6 @@
         cost_estimate=pl.CostEstimate(flops=200_000_000_000, bytes_accessed=50_000_000, transcendentals=0),
     )(*(pltpu.with_memory_space_constraint(x, pltpu.HBM) for x in front))
     arrived = exchange(far, group)
-    mix = pl.pallas_call(
-        functools.partial(gate_kernel, half),
-        out_shape=like(requests, count, dtype=F32),
-        in_specs=[whole()] * 3,
-        out_specs=whole(),
-        compiler_params=params(2 if tight else 24),
-    )(normed, router_weight.T, routes)
     own = pl.pallas_call(
         join_kernel,
         out_shape=like(count, width),
@@ -291,41 +304,58 @@
     beside = [exchange(piece, 1) for piece in mine]
     chunk = hidden // 6 if hidden % 96 == 0 else hidden
     steps = hidden // chunk
-    keep, send = pl.pallas_call(
+    rows = chips * count
+    start = 2 * width // 3 // 1024 * 1024
+    inner, keep, send = pl.pallas_call(
         functools.partial(expert_kernel, chips, chunk),
-        out_shape=(like(chips * count, width, dtype=F32), like(chips * count, width)),
+        out_shape=(like(2 * rows, hidden), like(rows, start, dtype=F32), like(rows, start)),
         in_specs=[whole()] * (2 * chips + 3),
-        out_specs=(whole(), whole()),
-        scratch_shapes=[
-            pltpu.VMEM((2 * chips * count, width), BF16),
-            pltpu.VMEM((2 * chips * count, hidden), BF16),
-        ],
+        out_specs=(whole(),) * 3,
+        scratch_shapes=[pltpu.VMEM((2 * rows, width), BF16)],
         compiler_params=params(3 if tight else 24),
     )(*mine, *beside, *weights)
     recv = exchange(send, 1)
-    first, *rest = pl.pallas_call(
+    keep_rest, send_rest = pl.pallas_call(
+        functools.partial(rest_kernel, start),
+        out_shape=(like(rows, width - start, dtype=F32), like(rows, width - start)),
+        in_specs=[whole()] * 2,
+        out_specs=(whole(),) * 2,
+        compiler_params=params(2 if tight else 24),
+    )(inner, weights[2])
+    recv_rest = exchange(send_rest, 1)
+    in_vmem = [pltpu.with_memory_space_constraint(x, pltpu.VMEM) for x in (keep, recv, keep_rest, recv_rest)]
+    near_sum, far_sum, *rest = pl.pallas_call(
         core_sum_kernel,
-        out_shape=(like(count, width, dtype=F32),) + (like(count, width),) * (chips - 1),
-        in_specs=[whole()] * 2,
-        out_specs=(whole(),) * chips,
-        compiler_params=params(2 if tight else 24),
-    )(pltpu.with_memory_space_constraint(keep, pltpu.VMEM), recv)
-    parts = [exchange(piece, CORES * (j + 1)) for j, piece in enumerate(rest)]
-    near_out, far_out = pl.pallas_call(
-        chip_sum_kernel,
-        out_shape=(like(capacity, width), like(capacity, width)),
+        out_shape=(like(capacity, width, dtype=F32),) * 2 + (like(capacity, width),) * (2 * chips - 2),
+        in_specs=[whole()] * 4,
+        out_specs=(whole(),) * (2 * chips),
+        compiler_params=params(2 if tight else 24),
+    )(*in_vmem)
+    order = range(chips - 1, 0, -1)
+    far_parts = [exchange(rest[2 * j - 1], CORES * j) for j in order]
+    near_parts = [exchange(rest[2 * j - 2], CORES * j) for j in order]
+    far_out = pl.pallas_call(
+        far_sum_kernel,
+        out_shape=like(capacity, width),
         in_specs=[whole()] * chips,
-        out_specs=(whole(), whole()),
-        compiler_params=params(2 if tight else 24),
-    )(first, *parts)
+        out_specs=whole(),
+        compiler_params=params(2 if tight else 24),
+    )(far_sum, *far_parts)
     back = exchange(far_out, group)
+    base, mix = pl.pallas_call(
+        functools.partial(near_kernel, half),
+        out_shape=(like(requests, width, dtype=F32), like(requests, count, dtype=F32)),
+        in_specs=[whole()] * (4 + chips),
+        out_specs=(whole(),) * 2,
+        compiler_params=params(2 if tight else 24),
+    )(residual, normed, router_weight.T, routes, near_sum, *near_parts)
     return pl.pallas_call(
         mix_kernel,
         out_shape=like(requests, width),
-        in_specs=[whole()] * 4,
+        in_specs=[whole()] * 3,
         out_specs=whole(),
         compiler_params=params(2 if tight else 24),
-    )(residual, mix, near_out, back)
+    )(base, mix, back)
 
 
 def solution(mesh):

time: 46.6 us -> 44.9 us (0.964)
  waiting for transfers between devices: 16.6 us -> 11.2 us
  starting transfers between devices: 14 us -> 17.9 us
    ppermute x13 -> x17, waiting for transfers between devices: 16.6 us -> 11.2 us  [exchange(): return lax.ppermute(value, 'pool', [(i, i ^ bit) for i in range(devices)])]
    ppermute x13 -> x17, starting transfers between devices: 14 us -> 17.9 us  [exchange(): return lax.ppermute(value, 'pool', [(i, i ^ bit) for i in range(devices)])]
    pallas_call x1, Pallas kernels: 11.7 us -> 10.5 us  [body(): pl.pallas_call(functools.partial(expert_kernel, chips, chunk), out_shape=...]
    pallas_call x3 -> x4, Pallas kernels: 0.42 us -> 1.61 us  [the longest x1 0.98 us: body(): pl.pallas_call(functools.partial(rest_kernel, start), out_shape=(like(row...]
  transfers between devices with their start and end apart: 13 -> 17, of which waited for: 11 -> 8; matrix products, arithmetic and copies ran while one was open for 0% -> 0% of each run, Pallas kernels for 1% -> 3%
where the time goes in v4:
time: 44.9 us; the launch traced here: 44.8 us
  starting transfers between devices  17.9 us (40%)
  Pallas kernels  15.6 us (35%)
  waiting for transfers between devices  11.2 us (25%)
    ppermute x17, starting transfers between devices, exchange(): return lax.ppermute(value, 'pool', [(i, i ^ bit) for i in range(devices)])  17.9 us
    ppermute x17, waiting for transfers between devices, exchange(): return lax.ppermute(value, 'pool', [(i, i ^ bit) for i in range(devices)])  11.2 us
    pallas_call x1, Pallas kernels, body(): pl.pallas_call(functools.partial(expert_kernel, chips, chunk), out_shape=...  10.5 us
    pallas_call x1, Pallas kernels, body(): pl.pallas_call(functools.partial(front_kernel, half), out_shape=(like(req...  2.66 us
    pallas_call x1, Pallas kernels, body(): pl.pallas_call(functools.partial(rest_kernel, start), out_shape=(like(row...  0.98 us
  transfers between devices with their start and end apart: 17, of which 8 were waited for; matrix products, arithmetic and copies ran while one was open for 0% of the time, Pallas kernels for 3%

profile of v4, /device:TPU:0, one launch (start us, length us, event | category | flops | bytes accessed | tf_op | source)
XLA Modules:
  0.0 44.8 jit_solution(8490175375013860815)
XLA Ops:
  0.0 2.7 %shard_map.109 = (f32[8,6144]{1,0:T(8,128)S(1)}, bf16[8,6144]{1,0:T(8,128)(2,1)S(1)}, bf16[4,6144]{1,0:T(4,128)(2,1)S(1)}, bf16[4,6144]{1,0:T(4,128)(2,1)S(1)}) custom-call(bf16[8,6144]{1,0:T(8,128)(2,1)} %hidden_hbm.1, bf16[8,6144]{1,0:T(8,128)(2,1)} %queries_hbm.1, bf16[128,2,1024]{2,1,0:T(2,128)(2,1)} %cached_hbm.1, bf16[8,2,1024]{2,1,0:T(2,128)(2,1)} %own_hbm.1, ...), custom_call_target="tpu_custom_call" | custom-call | flops 199999995904 | bytes 50000000 | tf_op jit(solution)/shard_map/pallas_call | solution.py:275
  2.7 4.1 %collective-permute-start = (bf16[4,6144]{1,0:T(4,128)(2,1)S(1)}, bf16[4,6144]{1,0:T(4,128)(2,1)S(1)}, u32[]{:S(2)}, u32[]{:S(2)}) collective-permute-start(bf16[4,6144]{1,0:T(4,128)(2,1)S(1)} %get-tuple-element.27), channel_id=1, source_target_pairs={{0,8},{1,9},{2,10},{3,11},{4,12},{5,13},{6,14},{7,15},{8,0},{9,1},... | collective-permute-start | bytes 147464 | tf_op jit(solution)/shard_map/ppermute | solution.py:265
  6.8 2.6 %collective-permute-done.arrived_ref = bf16[4,6144]{1,0:T(4,128)(2,1)S(1)} collective-permute-done((bf16[4,6144]{1,0:T(4,128)(2,1)S(1)}, bf16[4,6144]{1,0:T(4,128)(2,1)S(1)}, u32[]{:S(2)}, u32[]{:S(2)}) %collective-permute-start) | collective-permute-done | bytes 49184 | tf_op jit(solution)/shard_map/ppermute | solution.py:265
  9.4 2.4 %collective-permute-start.3 = (bf16[8,6144]{1,0:T(8,128)(2,1)S(1)}, bf16[8,6144]{1,0:T(8,128)(2,1)S(1)}, u32[]{:S(2)}, u32[]{:S(2)}) collective-permute-start(bf16[8,6144]{1,0:T(8,128)(2,1)S(1)} %shard_map.110.refs_0_), channel_id=1, source_target_pairs={{0,6},{1,7},{2,4},{3,5},{4,2},{5,3},{6,0},{7,1},{8,14},{9,15},{10,... | collective-permute-start | bytes 294920 | tf_op jit(solution)/shard_map/ppermute | solution.py:265
  11.8 0.9 %collective-permute-start.2 = (bf16[8,6144]{1,0:T(8,128)(2,1)S(1)}, bf16[8,6144]{1,0:T(8,128)(2,1)S(1)}, u32[]{:S(2)}, u32[]{:S(2)}) collective-permute-start(bf16[8,6144]{1,0:T(8,128)(2,1)S(1)} %shard_map.110.refs_0_), channel_id=1, source_target_pairs={{0,4},{1,5},{2,6},{3,7},{4,0},{5,1},{6,2},{7,3},{8,12},{9,13},{10,... | collective-permute-start | bytes 294920 | tf_op jit(solution)/shard_map/ppermute | solution.py:265
  13.0 2.1 %collective-permute-done.3.refs_3_ = bf16[8,6144]{1,0:T(8,128)(2,1)S(1)} collective-permute-done((bf16[8,6144]{1,0:T(8,128)(2,1)S(1)}, bf16[8,6144]{1,0:T(8,128)(2,1)S(1)}, u32[]{:S(2)}, u32[]{:S(2)}) %collective-permute-start.3) | collective-permute-done | bytes 98336 | tf_op jit(solution)/shard_map/ppermute | solution.py:265
  15.1 1.3 %collective-permute-done.2.refs_2_ = bf16[8,6144]{1,0:T(8,128)(2,1)S(1)} collective-permute-done((bf16[8,6144]{1,0:T(8,128)(2,1)S(1)}, bf16[8,6144]{1,0:T(8,128)(2,1)S(1)}, u32[]{:S(2)}, u32[]{:S(2)}) %collective-permute-start.2) | collective-permute-done | bytes 98336 | tf_op jit(solution)/shard_map/ppermute | solution.py:265
  16.4 0.9 %collective-permute-done.1.refs_1_ = bf16[8,6144]{1,0:T(8,128)(2,1)S(1)} collective-permute-done((bf16[8,6144]{1,0:T(8,128)(2,1)S(1)}, bf16[8,6144]{1,0:T(8,128)(2,1)S(1)}, u32[]{:S(2)}, u32[]{:S(2)}) %collective-permute-start.1) | collective-permute-done | bytes 98336 | tf_op jit(solution)/shard_map/ppermute | solution.py:265
  17.3 0.4 collective-permute-done.6.refs_6_
  17.7 0.9 %collective-permute-done.5.refs_5_ = bf16[8,6144]{1,0:T(8,128)(2,1)S(1)} collective-permute-done((bf16[8,6144]{1,0:T(8,128)(2,1)S(1)}, bf16[8,6144]{1,0:T(8,128)(2,1)S(1)}, u32[]{:S(2)}, u32[]{:S(2)}) %collective-permute-start.5) | collective-permute-done | bytes 98336 | tf_op jit(solution)/shard_map/ppermute | solution.py:265
  18.6 10.5 %shard_map.111 = (bf16[64,1344]{1,0:T(8,128)(2,1)S(1)}, f32[32,4096]{1,0:T(8,128)S(1)}, bf16[32,4096]{1,0:T(8,128)(2,1)S(1)}) custom-call(bf16[8,6144]{1,0:T(8,128)(2,1)S(1)} %shard_map.110.refs_0_, bf16[8,6144]{1,0:T(8,128)(2,1)S(1)} %collective-permute-done.1.refs_1_, bf16[8,6144]{1,0:T(8,128)(2,1)S(1)} %collective-permute-done.2.refs_2_, ...), custom_call_target="tpu_custom_call" | custom-call | tf_op jit(solution)/shard_map/pallas_call | solution.py:309
  29.3 1.0 %shard_map.112 = (f32[32,2048]{1,0:T(8,128)S(1)}, bf16[32,2048]{1,0:T(8,128)(2,1)S(1)}) custom-call(bf16[64,1344]{1,0:T(8,128)(2,1)S(1)} %get-tuple-element.30.inner_ref, bf16[1344,6144]{1,0:T(8,128)(2,1)S(1)} %bitcast.11), custom_call_target="tpu_custom_call" | custom-call | tf_op jit(solution)/shard_map/pallas_call | solution.py:318
  30.3 0.4 collective-permute-start.9
  30.7 1.0 %collective-permute-done.9.recv_rest_ref = bf16[32,2048]{1,0:T(8,128)(2,1)S(1)} collective-permute-done((bf16[32,2048]{1,0:T(8,128)(2,1)S(1)}, bf16[32,2048]{1,0:T(8,128)(2,1)S(1)}, u32[]{:S(2)}, u32[]{:S(2)}) %collective-permute-start.9) | collective-permute-done | bytes 131104 | tf_op jit(solution)/shard_map/ppermute | solution.py:265
  31.8 1.2 %collective-permute-start.13 = (bf16[4,6144]{1,0:T(4,128)(2,1)S(1)}, bf16[4,6144]{1,0:T(4,128)(2,1)S(1)}, u32[]{:S(2)}, u32[]{:S(2)}) collective-permute-start(bf16[4,6144]{1,0:T(4,128)(2,1)S(1)} %get-tuple-element.40), channel_id=1, source_target_pairs={{0,6},{1,7},{2,4},{3,5},{4,2},{5,3},{6,0},{7,1},{8,14},{9,15},{10,... | collective-permute-start | bytes 147464 | tf_op jit(solution)/shard_map/ppermute | solution.py:265
  33.0 0.8 %collective-permute-start.14 = (bf16[4,6144]{1,0:T(4,128)(2,1)S(1)}, bf16[4,6144]{1,0:T(4,128)(2,1)S(1)}, u32[]{:S(2)}, u32[]{:S(2)}) collective-permute-start(bf16[4,6144]{1,0:T(4,128)(2,1)S(1)} %get-tuple-element.41), channel_id=1, source_target_pairs={{0,4},{1,5},{2,6},{3,7},{4,0},{5,1},{6,2},{7,3},{8,12},{9,13},{10,... | collective-permute-start | bytes 147464 | tf_op jit(solution)/shard_map/ppermute | solution.py:265
  33.8 1.6 %collective-permute-start.15 = (bf16[4,6144]{1,0:T(4,128)(2,1)S(1)}, bf16[4,6144]{1,0:T(4,128)(2,1)S(1)}, u32[]{:S(2)}, u32[]{:S(2)}) collective-permute-start(bf16[4,6144]{1,0:T(4,128)(2,1)S(1)} %get-tuple-element.42), channel_id=1, source_target_pairs={{0,2},{1,3},{2,0},{3,1},{4,6},{5,7},{6,4},{7,5},{8,10},{9,11},{10,... | collective-permute-start | bytes 147464 | tf_op jit(solution)/shard_map/ppermute | solution.py:265
  35.4 1.1 %collective-permute-start.10 = (bf16[4,6144]{1,0:T(4,128)(2,1)S(1)}, bf16[4,6144]{1,0:T(4,128)(2,1)S(1)}, u32[]{:S(2)}, u32[]{:S(2)}) collective-permute-start(bf16[4,6144]{1,0:T(4,128)(2,1)S(1)} %get-tuple-element.34), channel_id=1, source_target_pairs={{0,6},{1,7},{2,4},{3,5},{4,2},{5,3},{6,0},{7,1},{8,14},{9,15},{10,... | collective-permute-start | bytes 147464 | tf_op jit(solution)/shard_map/ppermute | solution.py:265
  36.5 0.8 %collective-permute-start.11 = (bf16[4,6144]{1,0:T(4,128)(2,1)S(1)}, bf16[4,6144]{1,0:T(4,128)(2,1)S(1)}, u32[]{:S(2)}, u32[]{:S(2)}) collective-permute-start(bf16[4,6144]{1,0:T(4,128)(2,1)S(1)} %get-tuple-element.35), channel_id=1, source_target_pairs={{0,4},{1,5},{2,6},{3,7},{4,0},{5,1},{6,2},{7,3},{8,12},{9,13},{10,... | collective-permute-start | bytes 147464 | tf_op jit(solution)/shard_map/ppermute | solution.py:265
  37.3 1.6 %collective-permute-start.12 = (bf16[4,6144]{1,0:T(4,128)(2,1)S(1)}, bf16[4,6144]{1,0:T(4,128)(2,1)S(1)}, u32[]{:S(2)}, u32[]{:S(2)}) collective-permute-start(bf16[4,6144]{1,0:T(4,128)(2,1)S(1)} %get-tuple-element.36), channel_id=1, source_target_pairs={{0,2},{1,3},{2,0},{3,1},{4,6},{5,7},{6,4},{7,5},{8,10},{9,11},{10,... | collective-permute-start | bytes 147464 | tf_op jit(solution)/shard_map/ppermute | solution.py:265
  38.9 2.6 %collective-permute-start.16 = (bf16[4,6144]{1,0:T(4,128)(2,1)S(1)}, bf16[4,6144]{1,0:T(4,128)(2,1)S(1)}, u32[]{:S(2)}, u32[]{:S(2)}) collective-permute-start(bf16[4,6144]{1,0:T(4,128)(2,1)S(1)} %shard_map.115), channel_id=1, source_target_pairs={{0,8},{1,9},{2,10},{3,11},{4,12},{5,13},{6,14},{7,15},{8,0},{9,1},... | collective-permute-start | bytes 147464 | tf_op jit(solution)/shard_map/ppermute | solution.py:265
  41.5 0.5 %shard_map.114 = (f32[8,6144]{1,0:T(8,128)S(1)}, f32[8,8]{1,0:T(8,128)S(1)}) custom-call(f32[8,6144]{1,0:T(8,128)S(1)} %get-tuple-element.24.residual_ref, bf16[8,6144]{1,0:T(8,128)(2,1)S(1)} %get-tuple-element.25.normed_ref, bf16[16,6144]{1,0:T(8,128)(2,1)S(1)} %bitcast.14, s32[4,8]{1,0:T(4,128)S(1)} %bitcast.16, f32[4,6144]{1,0:T(4,128)S(1)} %get-tuple-element.33.near_ref, ...), custom_call_target="tpu_custom_call" | custom-call | tf_op jit(solution)/shard_map/pallas_call | solution.py:345
  42.0 2.0 %collective-permute-done.16.far_ref = bf16[4,6144]{1,0:T(4,128)(2,1)S(1)} collective-permute-done((bf16[4,6144]{1,0:T(4,128)(2,1)S(1)}, bf16[4,6144]{1,0:T(4,128)(2,1)S(1)}, u32[]{:S(2)}, u32[]{:S(2)}) %collective-permute-start.16) | collective-permute-done | bytes 49184 | tf_op jit(solution)/shard_map/ppermute | solution.py:265
  44.0 0.8 %shard_map.116 = bf16[8,6144]{1,0:T(8,128)(2,1)} custom-call(f32[8,6144]{1,0:T(8,128)S(1)} %get-tuple-element.37.base_ref, f32[8,8]{1,0:T(8,128)S(1)} %get-tuple-element.38.mix_ref, bf16[4,6144]{1,0:T(4,128)(2,1)S(1)} %collective-permute-done.16.far_ref), custom_call_target="tpu_custom_call" | custom-call | tf_op jit(solution)/shard_map/pallas_call | solution.py:352
  (28 shorter events, 0.7 us)
Async XLA Ops:
  0.0 18.6 %copy-start = (bf16[1,1344,6144]{2,1,0:T(8,128)(2,1)S(1)}, bf16[1,1344,6144]{2,1,0:T(8,128)(2,1)}, u32[]{:S(2)}) copy-start(bf16[1,1344,6144]{2,1,0:T(8,128)(2,1)} %param.21) | copy-start | bytes 49545220
  0.0 18.6 %copy-start.1 = (bf16[1,6144,1344]{1,2,0:T(8,128)(2,1)S(1)}, bf16[1,6144,1344]{1,2,0:T(8,128)(2,1)}, u32[]{:S(2)}) copy-start(bf16[1,6144,1344]{1,2,0:T(8,128)(2,1)} %param.19) | copy-start | bytes 49545220
  0.0 18.6 %copy-start.2 = (bf16[1,6144,1344]{1,2,0:T(8,128)(2,1)S(1)}, bf16[1,6144,1344]{1,2,0:T(8,128)(2,1)}, u32[]{:S(2)}) copy-start(bf16[1,6144,1344]{1,2,0:T(8,128)(2,1)} %param.20) | copy-start | bytes 49545220
  2.7 6.7 %collective-permute-start = (bf16[4,6144]{1,0:T(4,128)(2,1)S(1)}, bf16[4,6144]{1,0:T(4,128)(2,1)S(1)}, u32[]{:S(2)}, u32[]{:S(2)}) collective-permute-start(bf16[4,6144]{1,0:T(4,128)(2,1)S(1)} %get-tuple-element.27), channel_id=1, source_target_pairs={{0,8},{1,9},{2,10},{3,11},{4,12},{5,13},{6,14},{7,15},{8,0},{9,1},... | collective-permute-start | bytes 147464 | tf_op jit(solution)/shard_map/ppermute | solution.py:265
  9.4 5.7 %collective-permute-start.3 = (bf16[8,6144]{1,0:T(8,128)(2,1)S(1)}, bf16[8,6144]{1,0:T(8,128)(2,1)S(1)}, u32[]{:S(2)}, u32[]{:S(2)}) collective-permute-start(bf16[8,6144]{1,0:T(8,128)(2,1)S(1)} %shard_map.110.refs_0_), channel_id=1, source_target_pairs={{0,6},{1,7},{2,4},{3,5},{4,2},{5,3},{6,0},{7,1},{8,14},{9,15},{10,... | collective-permute-start | bytes 294920 | tf_op jit(solution)/shard_map/ppermute | solution.py:265
  11.8 4.6 %collective-permute-start.2 = (bf16[8,6144]{1,0:T(8,128)(2,1)S(1)}, bf16[8,6144]{1,0:T(8,128)(2,1)S(1)}, u32[]{:S(2)}, u32[]{:S(2)}) collective-permute-start(bf16[8,6144]{1,0:T(8,128)(2,1)S(1)} %shard_map.110.refs_0_), channel_id=1, source_target_pairs={{0,4},{1,5},{2,6},{3,7},{4,0},{5,1},{6,2},{7,3},{8,12},{9,13},{10,... | collective-permute-start | bytes 294920 | tf_op jit(solution)/shard_map/ppermute | solution.py:265
  12.7 4.6 %collective-permute-start.1 = (bf16[8,6144]{1,0:T(8,128)(2,1)S(1)}, bf16[8,6144]{1,0:T(8,128)(2,1)S(1)}, u32[]{:S(2)}, u32[]{:S(2)}) collective-permute-start(bf16[8,6144]{1,0:T(8,128)(2,1)S(1)} %shard_map.110.refs_0_), channel_id=1, source_target_pairs={{0,2},{1,3},{2,0},{3,1},{4,6},{5,7},{6,4},{7,5},{8,10},{9,11},{10,... | collective-permute-start | bytes 294920 | tf_op jit(solution)/shard_map/ppermute | solution.py:265
  13.0 4.3 %collective-permute-start.4 = (bf16[8,6144]{1,0:T(8,128)(2,1)S(1)}, bf16[8,6144]{1,0:T(8,128)(2,1)S(1)}, u32[]{:S(2)}, u32[]{:S(2)}) collective-permute-start(bf16[8,6144]{1,0:T(8,128)(2,1)S(1)} %shard_map.110.refs_0_), channel_id=1, source_target_pairs={{0,1},{1,0},{2,3},{3,2},{4,5},{5,4},{6,7},{7,6},{8,9},{9,8},{10,11... | collective-permute-start | bytes 294920 | tf_op jit(solution)/shard_map/ppermute | solution.py:265
  15.1 2.2 %collective-permute-start.7 = (bf16[8,6144]{1,0:T(8,128)(2,1)S(1)}, bf16[8,6144]{1,0:T(8,128)(2,1)S(1)}, u32[]{:S(2)}, u32[]{:S(2)}) collective-permute-start(bf16[8,6144]{1,0:T(8,128)(2,1)S(1)} %collective-permute-done.3.refs_3_), channel_id=1, source_target_pairs={{0,1},{1,0},{2,3},{3,2},{4,5},{5,4},{6,7},{7,6},{8,9},{9,8},{10,11... | collective-permute-start | bytes 294920 | tf_op jit(solution)/shard_map/ppermute | solution.py:265
  16.4 1.3 %collective-permute-start.6 = (bf16[8,6144]{1,0:T(8,128)(2,1)S(1)}, bf16[8,6144]{1,0:T(8,128)(2,1)S(1)}, u32[]{:S(2)}, u32[]{:S(2)}) collective-permute-start(bf16[8,6144]{1,0:T(8,128)(2,1)S(1)} %collective-permute-done.2.refs_2_), channel_id=1, source_target_pairs={{0,1},{1,0},{2,3},{3,2},{4,5},{5,4},{6,7},{7,6},{8,9},{9,8},{10,11... | collective-permute-start | bytes 294920 | tf_op jit(solution)/shard_map/ppermute | solution.py:265
  17.3 1.3 %collective-permute-start.5 = (bf16[8,6144]{1,0:T(8,128)(2,1)S(1)}, bf16[8,6144]{1,0:T(8,128)(2,1)S(1)}, u32[]{:S(2)}, u32[]{:S(2)}) collective-permute-start(bf16[8,6144]{1,0:T(8,128)(2,1)S(1)} %collective-permute-done.1.refs_1_), channel_id=1, source_target_pairs={{0,1},{1,0},{2,3},{3,2},{4,5},{5,4},{6,7},{7,6},{8,9},{9,8},{10,11... | collective-permute-start | bytes 294920 | tf_op jit(solution)/shard_map/ppermute | solution.py:265
  29.1 12.4 %copy-start.3 = (bf16[6144,16]{0,1:T(8,128)(2,1)S(1)}, bf16[6144,16]{0,1:T(8,128)(2,1)}, u32[]{:S(2)}) copy-start(bf16[6144,16]{0,1:T(8,128)(2,1)} %param.18) | copy-start | bytes 589828
  29.1 12.4 %copy-start.4 = (s32[8,4]{0,1:T(4,128)S(1)}, s32[8,4]{0,1:T(4,128)}, u32[]{:S(2)}) copy-start(s32[8,4]{0,1:T(4,128)} %param.16) | copy-start | bytes 388
  29.1 2.6 %collective-permute-start.8 = (bf16[32,4096]{1,0:T(8,128)(2,1)S(1)}, bf16[32,4096]{1,0:T(8,128)(2,1)S(1)}, u32[]{:S(2)}, u32[]{:S(2)}) collective-permute-start(bf16[32,4096]{1,0:T(8,128)(2,1)S(1)} %get-tuple-element.29), channel_id=1, source_target_pairs={{0,1},{1,0},{2,3},{3,2},{4,5},{5,4},{6,7},{7,6},{8,9},{9,8},{10,11... | collective-permute-start | bytes 786440 | tf_op jit(solution)/shard_map/ppermute | solution.py:265
  30.3 1.4 %collective-permute-start.9 = (bf16[32,2048]{1,0:T(8,128)(2,1)S(1)}, bf16[32,2048]{1,0:T(8,128)(2,1)S(1)}, u32[]{:S(2)}, u32[]{:S(2)}) collective-permute-start(bf16[32,2048]{1,0:T(8,128)(2,1)S(1)} %get-tuple-element.32), channel_id=1, source_target_pairs={{0,1},{1,0},{2,3},{3,2},{4,5},{5,4},{6,7},{7,6},{8,9},{9,8},{10,11... | collective-permute-start | bytes 393224 | tf_op jit(solution)/shard_map/ppermute | solution.py:265
  31.8 5.5 %collective-permute-start.13 = (bf16[4,6144]{1,0:T(4,128)(2,1)S(1)}, bf16[4,6144]{1,0:T(4,128)(2,1)S(1)}, u32[]{:S(2)}, u32[]{:S(2)}) collective-permute-start(bf16[4,6144]{1,0:T(4,128)(2,1)S(1)} %get-tuple-element.40), channel_id=1, source_target_pairs={{0,6},{1,7},{2,4},{3,5},{4,2},{5,3},{6,0},{7,1},{8,14},{9,15},{10,... | collective-permute-start | bytes 147464 | tf_op jit(solution)/shard_map/ppermute | solution.py:265
  33.0 5.9 %collective-permute-start.14 = (bf16[4,6144]{1,0:T(4,128)(2,1)S(1)}, bf16[4,6144]{1,0:T(4,128)(2,1)S(1)}, u32[]{:S(2)}, u32[]{:S(2)}) collective-permute-start(bf16[4,6144]{1,0:T(4,128)(2,1)S(1)} %get-tuple-element.41), channel_id=1, source_target_pairs={{0,4},{1,5},{2,6},{3,7},{4,0},{5,1},{6,2},{7,3},{8,12},{9,13},{10,... | collective-permute-start | bytes 147464 | tf_op jit(solution)/shard_map/ppermute | solution.py:265
  33.8 5.1 %collective-permute-start.15 = (bf16[4,6144]{1,0:T(4,128)(2,1)S(1)}, bf16[4,6144]{1,0:T(4,128)(2,1)S(1)}, u32[]{:S(2)}, u32[]{:S(2)}) collective-permute-start(bf16[4,6144]{1,0:T(4,128)(2,1)S(1)} %get-tuple-element.42), channel_id=1, source_target_pairs={{0,2},{1,3},{2,0},{3,1},{4,6},{5,7},{6,4},{7,5},{8,10},{9,11},{10,... | collective-permute-start | bytes 147464 | tf_op jit(solution)/shard_map/ppermute | solution.py:265
  35.4 6.1 %collective-permute-start.10 = (bf16[4,6144]{1,0:T(4,128)(2,1)S(1)}, bf16[4,6144]{1,0:T(4,128)(2,1)S(1)}, u32[]{:S(2)}, u32[]{:S(2)}) collective-permute-start(bf16[4,6144]{1,0:T(4,128)(2,1)S(1)} %get-tuple-element.34), channel_id=1, source_target_pairs={{0,6},{1,7},{2,4},{3,5},{4,2},{5,3},{6,0},{7,1},{8,14},{9,15},{10,... | collective-permute-start | bytes 147464 | tf_op jit(solution)/shard_map/ppermute | solution.py:265
  36.5 5.0 %collective-permute-start.11 = (bf16[4,6144]{1,0:T(4,128)(2,1)S(1)}, bf16[4,6144]{1,0:T(4,128)(2,1)S(1)}, u32[]{:S(2)}, u32[]{:S(2)}) collective-permute-start(bf16[4,6144]{1,0:T(4,128)(2,1)S(1)} %get-tuple-element.35), channel_id=1, source_target_pairs={{0,4},{1,5},{2,6},{3,7},{4,0},{5,1},{6,2},{7,3},{8,12},{9,13},{10,... | collective-permute-start | bytes 147464 | tf_op jit(solution)/shard_map/ppermute | solution.py:265
  37.3 4.2 %collective-permute-start.12 = (bf16[4,6144]{1,0:T(4,128)(2,1)S(1)}, bf16[4,6144]{1,0:T(4,128)(2,1)S(1)}, u32[]{:S(2)}, u32[]{:S(2)}) collective-permute-start(bf16[4,6144]{1,0:T(4,128)(2,1)S(1)} %get-tuple-element.36), channel_id=1, source_target_pairs={{0,2},{1,3},{2,0},{3,1},{4,6},{5,7},{6,4},{7,5},{8,10},{9,11},{10,... | collective-permute-start | bytes 147464 | tf_op jit(solution)/shard_map/ppermute | solution.py:265
  38.9 5.1 %collective-permute-start.16 = (bf16[4,6144]{1,0:T(4,128)(2,1)S(1)}, bf16[4,6144]{1,0:T(4,128)(2,1)S(1)}, u32[]{:S(2)}, u32[]{:S(2)}) collective-permute-start(bf16[4,6144]{1,0:T(4,128)(2,1)S(1)} %shard_map.115), channel_id=1, source_target_pairs={{0,8},{1,9},{2,10},{3,11},{4,12},{5,13},{6,14},{7,15},{8,0},{9,1},... | collective-permute-start | bytes 147464 | tf_op jit(solution)/shard_map/ppermute | solution.py:265

commit v5 on v4

--- a/solution.py
+++ b/solution.py
@@ -164,7 +164,7 @@
         send_ref[:, at] = out[half:2 * half].astype(BF16)
 
 
-def expert_kernel(chips, chunk, *refs):
+def expert_kernel(chips, chunk, depth, *refs):
     pieces = refs[:2 * chips]
     gate_ref, up_ref, down_ref, inner_ref, keep_ref, send_ref, rows_ref = refs[2 * chips:]
     hidden, width = gate_ref.shape
@@ -173,11 +173,13 @@
         rows_ref[i * count:(i + 1) * count, :] = piece[...]
     for i in range(hidden // chunk):
         at = slice(i * chunk, (i + 1) * chunk)
-        rows = rows_ref[...]
-        gate_part = lax.dot_general(gate_ref[at], rows, NT, preferred_element_type=F32)
-        up_part = lax.dot_general(up_ref[at], rows, NT, preferred_element_type=F32)
-        inner = gate_part / (1.0 + jnp.exp(-gate_part)) * up_part
-        inner_ref[:, at] = inner.T.astype(BF16)
+        gate_part = jnp.zeros((rows_ref.shape[0], chunk), F32)
+        up_part = jnp.zeros((chunk, rows_ref.shape[0]), F32)
+        for k in range(0, width, depth):
+            rows = rows_ref[:, k:k + depth]
+            gate_part += lax.dot_general(rows, gate_ref[at, k:k + depth], NT, preferred_element_type=F32)
+            up_part += lax.dot_general(up_ref[at, k:k + depth], rows, NT, preferred_element_type=F32)
+        inner_ref[:, at] = (gate_part / (1.0 + jnp.exp(-gate_part)) * up_part.T).astype(BF16)
     project(inner_ref, down_ref, keep_ref, send_ref, 0)
 
 
@@ -302,12 +304,12 @@
     )(near, arrived)
     mine = [own] + [exchange(own, CORES * j) for j in range(1, chips)]
     beside = [exchange(piece, 1) for piece in mine]
-    chunk = hidden // 6 if hidden % 96 == 0 else hidden
-    steps = hidden // chunk
+    chunk = 336 if hidden % 336 == 0 else hidden
+    depth = 256 if width % 256 == 0 else width
     rows = chips * count
     start = 2 * width // 3 // 1024 * 1024
     inner, keep, send = pl.pallas_call(
-        functools.partial(expert_kernel, chips, chunk),
+        functools.partial(expert_kernel, chips, chunk, depth),
         out_shape=(like(2 * rows, hidden), like(rows, start, dtype=F32), like(rows, start)),
         in_specs=[whole()] * (2 * chips + 3),
         out_specs=(whole(),) * 3,

time: 44.9 us -> 45.3 us (level)
  no operation moved by 1% of the time
where the time goes in v5:
time: 45.3 us; the launch traced here: 45.2 us
  starting transfers between devices  17.9 us (40%)
  Pallas kernels  16 us (35%)
  waiting for transfers between devices  11.2 us (25%)
    ppermute x17, starting transfers between devices, exchange(): return lax.ppermute(value, 'pool', [(i, i ^ bit) for i in range(devices)])  17.9 us
    ppermute x17, waiting for transfers between devices, exchange(): return lax.ppermute(value, 'pool', [(i, i ^ bit) for i in range(devices)])  11.2 us
    pallas_call x1, Pallas kernels, body(): pl.pallas_call(functools.partial(expert_kernel, chips, chunk, depth), out...  10.8 us
    pallas_call x1, Pallas kernels, body(): pl.pallas_call(functools.partial(front_kernel, half), out_shape=(like(req...  2.66 us
    pallas_call x1, Pallas kernels, body(): pl.pallas_call(functools.partial(rest_kernel, start), out_shape=(like(row...  0.98 us
  transfers between devices with their start and end apart: 17, of which 8 were waited for; matrix products, arithmetic and copies ran while one was open for 0% of the time, Pallas kernels for 3%

profile of v5, /device:TPU:0, one launch (start us, length us, event | category | flops | bytes accessed | tf_op | source)
XLA Modules:
  0.0 45.2 jit_solution(12597400583469131702)
XLA Ops:
  0.0 2.7 %shard_map.109 = (f32[8,6144]{1,0:T(8,128)S(1)}, bf16[8,6144]{1,0:T(8,128)(2,1)S(1)}, bf16[4,6144]{1,0:T(4,128)(2,1)S(1)}, bf16[4,6144]{1,0:T(4,128)(2,1)S(1)}) custom-call(bf16[8,6144]{1,0:T(8,128)(2,1)} %hidden_hbm.1, bf16[8,6144]{1,0:T(8,128)(2,1)} %queries_hbm.1, bf16[128,2,1024]{2,1,0:T(2,128)(2,1)} %cached_hbm.1, bf16[8,2,1024]{2,1,0:T(2,128)(2,1)} %own_hbm.1, ...), custom_call_target="tpu_custom_call" | custom-call | flops 199999995904 | bytes 50000000 | tf_op jit(solution)/shard_map/pallas_call | solution.py:277
  2.7 4.1 %collective-permute-start = (bf16[4,6144]{1,0:T(4,128)(2,1)S(1)}, bf16[4,6144]{1,0:T(4,128)(2,1)S(1)}, u32[]{:S(2)}, u32[]{:S(2)}) collective-permute-start(bf16[4,6144]{1,0:T(4,128)(2,1)S(1)} %get-tuple-element.27), channel_id=1, source_target_pairs={{0,8},{1,9},{2,10},{3,11},{4,12},{5,13},{6,14},{7,15},{8,0},{9,1},... | collective-permute-start | bytes 147464 | tf_op jit(solution)/shard_map/ppermute | solution.py:267
  6.8 2.6 %collective-permute-done.arrived_ref = bf16[4,6144]{1,0:T(4,128)(2,1)S(1)} collective-permute-done((bf16[4,6144]{1,0:T(4,128)(2,1)S(1)}, bf16[4,6144]{1,0:T(4,128)(2,1)S(1)}, u32[]{:S(2)}, u32[]{:S(2)}) %collective-permute-start) | collective-permute-done | bytes 49184 | tf_op jit(solution)/shard_map/ppermute | solution.py:267
  9.4 2.4 %collective-permute-start.3 = (bf16[8,6144]{1,0:T(8,128)(2,1)S(1)}, bf16[8,6144]{1,0:T(8,128)(2,1)S(1)}, u32[]{:S(2)}, u32[]{:S(2)}) collective-permute-start(bf16[8,6144]{1,0:T(8,128)(2,1)S(1)} %shard_map.110.refs_0_), channel_id=1, source_target_pairs={{0,6},{1,7},{2,4},{3,5},{4,2},{5,3},{6,0},{7,1},{8,14},{9,15},{10,... | collective-permute-start | bytes 294920 | tf_op jit(solution)/shard_map/ppermute | solution.py:267
  11.8 0.9 %collective-permute-start.2 = (bf16[8,6144]{1,0:T(8,128)(2,1)S(1)}, bf16[8,6144]{1,0:T(8,128)(2,1)S(1)}, u32[]{:S(2)}, u32[]{:S(2)}) collective-permute-start(bf16[8,6144]{1,0:T(8,128)(2,1)S(1)} %shard_map.110.refs_0_), channel_id=1, source_target_pairs={{0,4},{1,5},{2,6},{3,7},{4,0},{5,1},{6,2},{7,3},{8,12},{9,13},{10,... | collective-permute-start | bytes 294920 | tf_op jit(solution)/shard_map/ppermute | solution.py:267
  13.0 2.1 %collective-permute-done.3.refs_3_ = bf16[8,6144]{1,0:T(8,128)(2,1)S(1)} collective-permute-done((bf16[8,6144]{1,0:T(8,128)(2,1)S(1)}, bf16[8,6144]{1,0:T(8,128)(2,1)S(1)}, u32[]{:S(2)}, u32[]{:S(2)}) %collective-permute-start.3) | collective-permute-done | bytes 98336 | tf_op jit(solution)/shard_map/ppermute | solution.py:267
  15.1 1.3 %collective-permute-done.2.refs_2_ = bf16[8,6144]{1,0:T(8,128)(2,1)S(1)} collective-permute-done((bf16[8,6144]{1,0:T(8,128)(2,1)S(1)}, bf16[8,6144]{1,0:T(8,128)(2,1)S(1)}, u32[]{:S(2)}, u32[]{:S(2)}) %collective-permute-start.2) | collective-permute-done | bytes 98336 | tf_op jit(solution)/shard_map/ppermute | solution.py:267
  16.4 0.9 %collective-permute-done.1.refs_1_ = bf16[8,6144]{1,0:T(8,128)(2,1)S(1)} collective-permute-done((bf16[8,6144]{1,0:T(8,128)(2,1)S(1)}, bf16[8,6144]{1,0:T(8,128)(2,1)S(1)}, u32[]{:S(2)}, u32[]{:S(2)}) %collective-permute-start.1) | collective-permute-done | bytes 98336 | tf_op jit(solution)/shard_map/ppermute | solution.py:267
  17.3 0.4 collective-permute-done.6.refs_6_
  17.7 0.9 %collective-permute-done.5.refs_5_ = bf16[8,6144]{1,0:T(8,128)(2,1)S(1)} collective-permute-done((bf16[8,6144]{1,0:T(8,128)(2,1)S(1)}, bf16[8,6144]{1,0:T(8,128)(2,1)S(1)}, u32[]{:S(2)}, u32[]{:S(2)}) %collective-permute-start.5) | collective-permute-done | bytes 98336 | tf_op jit(solution)/shard_map/ppermute | solution.py:267
  18.6 10.8 %shard_map.111 = (bf16[64,1344]{1,0:T(8,128)(2,1)S(1)}, f32[32,4096]{1,0:T(8,128)S(1)}, bf16[32,4096]{1,0:T(8,128)(2,1)S(1)}) custom-call(bf16[8,6144]{1,0:T(8,128)(2,1)S(1)} %shard_map.110.refs_0_, bf16[8,6144]{1,0:T(8,128)(2,1)S(1)} %collective-permute-done.1.refs_1_, bf16[8,6144]{1,0:T(8,128)(2,1)S(1)} %collective-permute-done.2.refs_2_, ...), custom_call_target="tpu_custom_call" | custom-call | tf_op jit(solution)/shard_map/pallas_call | solution.py:311
  29.7 1.0 %shard_map.112 = (f32[32,2048]{1,0:T(8,128)S(1)}, bf16[32,2048]{1,0:T(8,128)(2,1)S(1)}) custom-call(bf16[64,1344]{1,0:T(8,128)(2,1)S(1)} %get-tuple-element.30.inner_ref, bf16[1344,6144]{1,0:T(8,128)(2,1)S(1)} %bitcast.11), custom_call_target="tpu_custom_call" | custom-call | tf_op jit(solution)/shard_map/pallas_call | solution.py:320
  30.7 0.4 collective-permute-start.9
  31.1 1.0 %collective-permute-done.9.recv_rest_ref = bf16[32,2048]{1,0:T(8,128)(2,1)S(1)} collective-permute-done((bf16[32,2048]{1,0:T(8,128)(2,1)S(1)}, bf16[32,2048]{1,0:T(8,128)(2,1)S(1)}, u32[]{:S(2)}, u32[]{:S(2)}) %collective-permute-start.9) | collective-permute-done | bytes 131104 | tf_op jit(solution)/shard_map/ppermute | solution.py:267
  32.2 1.2 %collective-permute-start.13 = (bf16[4,6144]{1,0:T(4,128)(2,1)S(1)}, bf16[4,6144]{1,0:T(4,128)(2,1)S(1)}, u32[]{:S(2)}, u32[]{:S(2)}) collective-permute-start(bf16[4,6144]{1,0:T(4,128)(2,1)S(1)} %get-tuple-element.40), channel_id=1, source_target_pairs={{0,6},{1,7},{2,4},{3,5},{4,2},{5,3},{6,0},{7,1},{8,14},{9,15},{10,... | collective-permute-start | bytes 147464 | tf_op jit(solution)/shard_map/ppermute | solution.py:267
  33.4 0.8 %collective-permute-start.14 = (bf16[4,6144]{1,0:T(4,128)(2,1)S(1)}, bf16[4,6144]{1,0:T(4,128)(2,1)S(1)}, u32[]{:S(2)}, u32[]{:S(2)}) collective-permute-start(bf16[4,6144]{1,0:T(4,128)(2,1)S(1)} %get-tuple-element.41), channel_id=1, source_target_pairs={{0,4},{1,5},{2,6},{3,7},{4,0},{5,1},{6,2},{7,3},{8,12},{9,13},{10,... | collective-permute-start | bytes 147464 | tf_op jit(solution)/shard_map/ppermute | solution.py:267
  34.2 1.5 %collective-permute-start.15 = (bf16[4,6144]{1,0:T(4,128)(2,1)S(1)}, bf16[4,6144]{1,0:T(4,128)(2,1)S(1)}, u32[]{:S(2)}, u32[]{:S(2)}) collective-permute-start(bf16[4,6144]{1,0:T(4,128)(2,1)S(1)} %get-tuple-element.42), channel_id=1, source_target_pairs={{0,2},{1,3},{2,0},{3,1},{4,6},{5,7},{6,4},{7,5},{8,10},{9,11},{10,... | collective-permute-start | bytes 147464 | tf_op jit(solution)/shard_map/ppermute | solution.py:267
  35.8 1.1 %collective-permute-start.10 = (bf16[4,6144]{1,0:T(4,128)(2,1)S(1)}, bf16[4,6144]{1,0:T(4,128)(2,1)S(1)}, u32[]{:S(2)}, u32[]{:S(2)}) collective-permute-start(bf16[4,6144]{1,0:T(4,128)(2,1)S(1)} %get-tuple-element.34), channel_id=1, source_target_pairs={{0,6},{1,7},{2,4},{3,5},{4,2},{5,3},{6,0},{7,1},{8,14},{9,15},{10,... | collective-permute-start | bytes 147464 | tf_op jit(solution)/shard_map/ppermute | solution.py:267
  36.9 0.8 %collective-permute-start.11 = (bf16[4,6144]{1,0:T(4,128)(2,1)S(1)}, bf16[4,6144]{1,0:T(4,128)(2,1)S(1)}, u32[]{:S(2)}, u32[]{:S(2)}) collective-permute-start(bf16[4,6144]{1,0:T(4,128)(2,1)S(1)} %get-tuple-element.35), channel_id=1, source_target_pairs={{0,4},{1,5},{2,6},{3,7},{4,0},{5,1},{6,2},{7,3},{8,12},{9,13},{10,... | collective-permute-start | bytes 147464 | tf_op jit(solution)/shard_map/ppermute | solution.py:267
  37.7 1.5 %collective-permute-start.12 = (bf16[4,6144]{1,0:T(4,128)(2,1)S(1)}, bf16[4,6144]{1,0:T(4,128)(2,1)S(1)}, u32[]{:S(2)}, u32[]{:S(2)}) collective-permute-start(bf16[4,6144]{1,0:T(4,128)(2,1)S(1)} %get-tuple-element.36), channel_id=1, source_target_pairs={{0,2},{1,3},{2,0},{3,1},{4,6},{5,7},{6,4},{7,5},{8,10},{9,11},{10,... | collective-permute-start | bytes 147464 | tf_op jit(solution)/shard_map/ppermute | solution.py:267
  39.3 2.6 %collective-permute-start.16 = (bf16[4,6144]{1,0:T(4,128)(2,1)S(1)}, bf16[4,6144]{1,0:T(4,128)(2,1)S(1)}, u32[]{:S(2)}, u32[]{:S(2)}) collective-permute-start(bf16[4,6144]{1,0:T(4,128)(2,1)S(1)} %shard_map.115), channel_id=1, source_target_pairs={{0,8},{1,9},{2,10},{3,11},{4,12},{5,13},{6,14},{7,15},{8,0},{9,1},... | collective-permute-start | bytes 147464 | tf_op jit(solution)/shard_map/ppermute | solution.py:267
  41.9 0.5 %shard_map.114 = (f32[8,6144]{1,0:T(8,128)S(1)}, f32[8,8]{1,0:T(8,128)S(1)}) custom-call(f32[8,6144]{1,0:T(8,128)S(1)} %get-tuple-element.24.residual_ref, bf16[8,6144]{1,0:T(8,128)(2,1)S(1)} %get-tuple-element.25.normed_ref, bf16[16,6144]{1,0:T(8,128)(2,1)S(1)} %bitcast.14, s32[4,8]{1,0:T(4,128)S(1)} %bitcast.16, f32[4,6144]{1,0:T(4,128)S(1)} %get-tuple-element.33.near_ref, ...), custom_call_target="tpu_custom_call" | custom-call | tf_op jit(solution)/shard_map/pallas_call | solution.py:347
  42.4 2.0 %collective-permute-done.16.far_ref = bf16[4,6144]{1,0:T(4,128)(2,1)S(1)} collective-permute-done((bf16[4,6144]{1,0:T(4,128)(2,1)S(1)}, bf16[4,6144]{1,0:T(4,128)(2,1)S(1)}, u32[]{:S(2)}, u32[]{:S(2)}) %collective-permute-start.16) | collective-permute-done | bytes 49184 | tf_op jit(solution)/shard_map/ppermute | solution.py:267
  44.4 0.8 %shard_map.116 = bf16[8,6144]{1,0:T(8,128)(2,1)} custom-call(f32[8,6144]{1,0:T(8,128)S(1)} %get-tuple-element.37.base_ref, f32[8,8]{1,0:T(8,128)S(1)} %get-tuple-element.38.mix_ref, bf16[4,6144]{1,0:T(4,128)(2,1)S(1)} %collective-permute-done.16.far_ref), custom_call_target="tpu_custom_call" | custom-call | tf_op jit(solution)/shard_map/pallas_call | solution.py:354
  (28 shorter events, 0.7 us)
Async XLA Ops:
  0.0 18.6 %copy-start = (bf16[1,1344,6144]{2,1,0:T(8,128)(2,1)S(1)}, bf16[1,1344,6144]{2,1,0:T(8,128)(2,1)}, u32[]{:S(2)}) copy-start(bf16[1,1344,6144]{2,1,0:T(8,128)(2,1)} %param.21) | copy-start | bytes 49545220
  0.0 18.6 %copy-start.1 = (bf16[1,6144,1344]{1,2,0:T(8,128)(2,1)S(1)}, bf16[1,6144,1344]{1,2,0:T(8,128)(2,1)}, u32[]{:S(2)}) copy-start(bf16[1,6144,1344]{1,2,0:T(8,128)(2,1)} %param.19) | copy-start | bytes 49545220
  0.0 18.6 %copy-start.2 = (bf16[1,6144,1344]{1,2,0:T(8,128)(2,1)S(1)}, bf16[1,6144,1344]{1,2,0:T(8,128)(2,1)}, u32[]{:S(2)}) copy-start(bf16[1,6144,1344]{1,2,0:T(8,128)(2,1)} %param.20) | copy-start | bytes 49545220
  2.7 6.7 %collective-permute-start = (bf16[4,6144]{1,0:T(4,128)(2,1)S(1)}, bf16[4,6144]{1,0:T(4,128)(2,1)S(1)}, u32[]{:S(2)}, u32[]{:S(2)}) collective-permute-start(bf16[4,6144]{1,0:T(4,128)(2,1)S(1)} %get-tuple-element.27), channel_id=1, source_target_pairs={{0,8},{1,9},{2,10},{3,11},{4,12},{5,13},{6,14},{7,15},{8,0},{9,1},... | collective-permute-start | bytes 147464 | tf_op jit(solution)/shard_map/ppermute | solution.py:267
  9.4 5.7 %collective-permute-start.3 = (bf16[8,6144]{1,0:T(8,128)(2,1)S(1)}, bf16[8,6144]{1,0:T(8,128)(2,1)S(1)}, u32[]{:S(2)}, u32[]{:S(2)}) collective-permute-start(bf16[8,6144]{1,0:T(8,128)(2,1)S(1)} %shard_map.110.refs_0_), channel_id=1, source_target_pairs={{0,6},{1,7},{2,4},{3,5},{4,2},{5,3},{6,0},{7,1},{8,14},{9,15},{10,... | collective-permute-start | bytes 294920 | tf_op jit(solution)/shard_map/ppermute | solution.py:267
  11.8 4.6 %collective-permute-start.2 = (bf16[8,6144]{1,0:T(8,128)(2,1)S(1)}, bf16[8,6144]{1,0:T(8,128)(2,1)S(1)}, u32[]{:S(2)}, u32[]{:S(2)}) collective-permute-start(bf16[8,6144]{1,0:T(8,128)(2,1)S(1)} %shard_map.110.refs_0_), channel_id=1, source_target_pairs={{0,4},{1,5},{2,6},{3,7},{4,0},{5,1},{6,2},{7,3},{8,12},{9,13},{10,... | collective-permute-start | bytes 294920 | tf_op jit(solution)/shard_map/ppermute | solution.py:267
  12.7 4.6 %collective-permute-start.1 = (bf16[8,6144]{1,0:T(8,128)(2,1)S(1)}, bf16[8,6144]{1,0:T(8,128)(2,1)S(1)}, u32[]{:S(2)}, u32[]{:S(2)}) collective-permute-start(bf16[8,6144]{1,0:T(8,128)(2,1)S(1)} %shard_map.110.refs_0_), channel_id=1, source_target_pairs={{0,2},{1,3},{2,0},{3,1},{4,6},{5,7},{6,4},{7,5},{8,10},{9,11},{10,... | collective-permute-start | bytes 294920 | tf_op jit(solution)/shard_map/ppermute | solution.py:267
  13.0 4.3 %collective-permute-start.4 = (bf16[8,6144]{1,0:T(8,128)(2,1)S(1)}, bf16[8,6144]{1,0:T(8,128)(2,1)S(1)}, u32[]{:S(2)}, u32[]{:S(2)}) collective-permute-start(bf16[8,6144]{1,0:T(8,128)(2,1)S(1)} %shard_map.110.refs_0_), channel_id=1, source_target_pairs={{0,1},{1,0},{2,3},{3,2},{4,5},{5,4},{6,7},{7,6},{8,9},{9,8},{10,11... | collective-permute-start | bytes 294920 | tf_op jit(solution)/shard_map/ppermute | solution.py:267
  15.1 2.2 %collective-permute-start.7 = (bf16[8,6144]{1,0:T(8,128)(2,1)S(1)}, bf16[8,6144]{1,0:T(8,128)(2,1)S(1)}, u32[]{:S(2)}, u32[]{:S(2)}) collective-permute-start(bf16[8,6144]{1,0:T(8,128)(2,1)S(1)} %collective-permute-done.3.refs_3_), channel_id=1, source_target_pairs={{0,1},{1,0},{2,3},{3,2},{4,5},{5,4},{6,7},{7,6},{8,9},{9,8},{10,11... | collective-permute-start | bytes 294920 | tf_op jit(solution)/shard_map/ppermute | solution.py:267
  16.4 1.3 %collective-permute-start.6 = (bf16[8,6144]{1,0:T(8,128)(2,1)S(1)}, bf16[8,6144]{1,0:T(8,128)(2,1)S(1)}, u32[]{:S(2)}, u32[]{:S(2)}) collective-permute-start(bf16[8,6144]{1,0:T(8,128)(2,1)S(1)} %collective-permute-done.2.refs_2_), channel_id=1, source_target_pairs={{0,1},{1,0},{2,3},{3,2},{4,5},{5,4},{6,7},{7,6},{8,9},{9,8},{10,11... | collective-permute-start | bytes 294920 | tf_op jit(solution)/shard_map/ppermute | solution.py:267
  17.3 1.3 %collective-permute-start.5 = (bf16[8,6144]{1,0:T(8,128)(2,1)S(1)}, bf16[8,6144]{1,0:T(8,128)(2,1)S(1)}, u32[]{:S(2)}, u32[]{:S(2)}) collective-permute-start(bf16[8,6144]{1,0:T(8,128)(2,1)S(1)} %collective-permute-done.1.refs_1_), channel_id=1, source_target_pairs={{0,1},{1,0},{2,3},{3,2},{4,5},{5,4},{6,7},{7,6},{8,9},{9,8},{10,11... | collective-permute-start | bytes 294920 | tf_op jit(solution)/shard_map/ppermute | solution.py:267
  29.5 12.4 %copy-start.3 = (bf16[6144,16]{0,1:T(8,128)(2,1)S(1)}, bf16[6144,16]{0,1:T(8,128)(2,1)}, u32[]{:S(2)}) copy-start(bf16[6144,16]{0,1:T(8,128)(2,1)} %param.18) | copy-start | bytes 589828
  29.5 12.4 %copy-start.4 = (s32[8,4]{0,1:T(4,128)S(1)}, s32[8,4]{0,1:T(4,128)}, u32[]{:S(2)}) copy-start(s32[8,4]{0,1:T(4,128)} %param.16) | copy-start | bytes 388
  29.5 2.6 %collective-permute-start.8 = (bf16[32,4096]{1,0:T(8,128)(2,1)S(1)}, bf16[32,4096]{1,0:T(8,128)(2,1)S(1)}, u32[]{:S(2)}, u32[]{:S(2)}) collective-permute-start(bf16[32,4096]{1,0:T(8,128)(2,1)S(1)} %get-tuple-element.29), channel_id=1, source_target_pairs={{0,1},{1,0},{2,3},{3,2},{4,5},{5,4},{6,7},{7,6},{8,9},{9,8},{10,11... | collective-permute-start | bytes 786440 | tf_op jit(solution)/shard_map/ppermute | solution.py:267
  30.7 1.4 %collective-permute-start.9 = (bf16[32,2048]{1,0:T(8,128)(2,1)S(1)}, bf16[32,2048]{1,0:T(8,128)(2,1)S(1)}, u32[]{:S(2)}, u32[]{:S(2)}) collective-permute-start(bf16[32,2048]{1,0:T(8,128)(2,1)S(1)} %get-tuple-element.32), channel_id=1, source_target_pairs={{0,1},{1,0},{2,3},{3,2},{4,5},{5,4},{6,7},{7,6},{8,9},{9,8},{10,11... | collective-permute-start | bytes 393224 | tf_op jit(solution)/shard_map/ppermute | solution.py:267
  32.2 5.5 %collective-permute-start.13 = (bf16[4,6144]{1,0:T(4,128)(2,1)S(1)}, bf16[4,6144]{1,0:T(4,128)(2,1)S(1)}, u32[]{:S(2)}, u32[]{:S(2)}) collective-permute-start(bf16[4,6144]{1,0:T(4,128)(2,1)S(1)} %get-tuple-element.40), channel_id=1, source_target_pairs={{0,6},{1,7},{2,4},{3,5},{4,2},{5,3},{6,0},{7,1},{8,14},{9,15},{10,... | collective-permute-start | bytes 147464 | tf_op jit(solution)/shard_map/ppermute | solution.py:267
  33.4 5.9 %collective-permute-start.14 = (bf16[4,6144]{1,0:T(4,128)(2,1)S(1)}, bf16[4,6144]{1,0:T(4,128)(2,1)S(1)}, u32[]{:S(2)}, u32[]{:S(2)}) collective-permute-start(bf16[4,6144]{1,0:T(4,128)(2,1)S(1)} %get-tuple-element.41), channel_id=1, source_target_pairs={{0,4},{1,5},{2,6},{3,7},{4,0},{5,1},{6,2},{7,3},{8,12},{9,13},{10,... | collective-permute-start | bytes 147464 | tf_op jit(solution)/shard_map/ppermute | solution.py:267
  34.2 5.0 %collective-permute-start.15 = (bf16[4,6144]{1,0:T(4,128)(2,1)S(1)}, bf16[4,6144]{1,0:T(4,128)(2,1)S(1)}, u32[]{:S(2)}, u32[]{:S(2)}) collective-permute-start(bf16[4,6144]{1,0:T(4,128)(2,1)S(1)} %get-tuple-element.42), channel_id=1, source_target_pairs={{0,2},{1,3},{2,0},{3,1},{4,6},{5,7},{6,4},{7,5},{8,10},{9,11},{10,... | collective-permute-start | bytes 147464 | tf_op jit(solution)/shard_map/ppermute | solution.py:267
  35.8 6.1 %collective-permute-start.10 = (bf16[4,6144]{1,0:T(4,128)(2,1)S(1)}, bf16[4,6144]{1,0:T(4,128)(2,1)S(1)}, u32[]{:S(2)}, u32[]{:S(2)}) collective-permute-start(bf16[4,6144]{1,0:T(4,128)(2,1)S(1)} %get-tuple-element.34), channel_id=1, source_target_pairs={{0,6},{1,7},{2,4},{3,5},{4,2},{5,3},{6,0},{7,1},{8,14},{9,15},{10,... | collective-permute-start | bytes 147464 | tf_op jit(solution)/shard_map/ppermute | solution.py:267
  36.9 5.0 %collective-permute-start.11 = (bf16[4,6144]{1,0:T(4,128)(2,1)S(1)}, bf16[4,6144]{1,0:T(4,128)(2,1)S(1)}, u32[]{:S(2)}, u32[]{:S(2)}) collective-permute-start(bf16[4,6144]{1,0:T(4,128)(2,1)S(1)} %get-tuple-element.35), channel_id=1, source_target_pairs={{0,4},{1,5},{2,6},{3,7},{4,0},{5,1},{6,2},{7,3},{8,12},{9,13},{10,... | collective-permute-start | bytes 147464 | tf_op jit(solution)/shard_map/ppermute | solution.py:267
  37.7 4.2 %collective-permute-start.12 = (bf16[4,6144]{1,0:T(4,128)(2,1)S(1)}, bf16[4,6144]{1,0:T(4,128)(2,1)S(1)}, u32[]{:S(2)}, u32[]{:S(2)}) collective-permute-start(bf16[4,6144]{1,0:T(4,128)(2,1)S(1)} %get-tuple-element.36), channel_id=1, source_target_pairs={{0,2},{1,3},{2,0},{3,1},{4,6},{5,7},{6,4},{7,5},{8,10},{9,11},{10,... | collective-permute-start | bytes 147464 | tf_op jit(solution)/shard_map/ppermute | solution.py:267
  39.3 5.1 %collective-permute-start.16 = (bf16[4,6144]{1,0:T(4,128)(2,1)S(1)}, bf16[4,6144]{1,0:T(4,128)(2,1)S(1)}, u32[]{:S(2)}, u32[]{:S(2)}) collective-permute-start(bf16[4,6144]{1,0:T(4,128)(2,1)S(1)} %shard_map.115), channel_id=1, source_target_pairs={{0,8},{1,9},{2,10},{3,11},{4,12},{5,13},{6,14},{7,15},{8,0},{9,1},... | collective-permute-start | bytes 147464 | tf_op jit(solution)/shard_map/ppermute | solution.py:267

commit v6 on v5

--- a/solution.py
+++ b/solution.py
@@ -166,7 +166,7 @@
 
 def expert_kernel(chips, chunk, depth, *refs):
     pieces = refs[:2 * chips]
-    gate_ref, up_ref, down_ref, inner_ref, keep_ref, send_ref, rows_ref = refs[2 * chips:]
+    gate_ref, up_ref, inner_ref, rows_ref = refs[2 * chips:]
     hidden, width = gate_ref.shape
     count = pieces[0].shape[0]
     for i, piece in enumerate(pieces):
@@ -180,20 +180,16 @@
             gate_part += lax.dot_general(rows, gate_ref[at, k:k + depth], NT, preferred_element_type=F32)
             up_part += lax.dot_general(up_ref[at, k:k + depth], rows, NT, preferred_element_type=F32)
         inner_ref[:, at] = (gate_part / (1.0 + jnp.exp(-gate_part)) * up_part.T).astype(BF16)
-    project(inner_ref, down_ref, keep_ref, send_ref, 0)
 
 
 def rest_kernel(start, inner_ref, down_ref, keep_ref, send_ref):
     project(inner_ref, down_ref, keep_ref, send_ref, start)
 
 
-def core_sum_kernel(keep_ref, recv_ref, keep_rest_ref, recv_rest_ref, near_ref, far_ref, *rest):
+def core_sum_kernel(keep_ref, recv_ref, near_ref, far_ref, *rest):
     capacity = near_ref.shape[0]
     start = keep_ref.shape[1]
-    for keep, recv, at in (
-        (keep_ref, recv_ref, slice(0, start)),
-        (keep_rest_ref, recv_rest_ref, slice(start, near_ref.shape[1])),
-    ):
+    for keep, recv, at in ((keep_ref, recv_ref, slice(0, start)),):
         total = keep[...] + recv[...].astype(F32)
         for i, out in enumerate((near_ref, far_ref) + rest):
             out[:, at] = total[i * capacity:(i + 1) * capacity].astype(out.dtype)
@@ -308,28 +304,31 @@
     depth = 256 if width % 256 == 0 else width
     rows = chips * count
     start = 2 * width // 3 // 1024 * 1024
-    inner, keep, send = pl.pallas_call(
+    inner = pl.pallas_call(
         functools.partial(expert_kernel, chips, chunk, depth),
-        out_shape=(like(2 * rows, hidden), like(rows, start, dtype=F32), like(rows, start)),
-        in_specs=[whole()] * (2 * chips + 3),
-        out_specs=(whole(),) * 3,
+        out_shape=like(2 * rows, hidden),
+        in_specs=[whole()] * (2 * chips + 2),
+        out_specs=whole(),
         scratch_shapes=[pltpu.VMEM((2 * rows, width), BF16)],
-        compiler_params=params(3 if tight else 24),
-    )(*mine, *beside, *weights)
+        compiler_params=params(2 if tight else 24),
+    )(*mine, *beside, *weights[:2])
+
+    def down(start, columns):
+        return pl.pallas_call(
+            functools.partial(rest_kernel, start),
+            out_shape=(like(rows, columns, dtype=F32), like(rows, columns)),
+            in_specs=[whole()] * 2,
+            out_specs=(whole(),) * 2,
+            compiler_params=params(2 if tight else 24),
+        )(inner, weights[2])
+
+    keep, send = down(0, width)
     recv = exchange(send, 1)
-    keep_rest, send_rest = pl.pallas_call(
-        functools.partial(rest_kernel, start),
-        out_shape=(like(rows, width - start, dtype=F32), like(rows, width - start)),
-        in_specs=[whole()] * 2,
-        out_specs=(whole(),) * 2,
-        compiler_params=params(2 if tight else 24),
-    )(inner, weights[2])
-    recv_rest = exchange(send_rest, 1)
-    in_vmem = [pltpu.with_memory_space_constraint(x, pltpu.VMEM) for x in (keep, recv, keep_rest, recv_rest)]
+    in_vmem = [pltpu.with_memory_space_constraint(x, pltpu.VMEM) for x in (keep, recv)]
     near_sum, far_sum, *rest = pl.pallas_call(
         core_sum_kernel,
         out_shape=(like(capacity, width, dtype=F32),) * 2 + (like(capacity, width),) * (2 * chips - 2),
-        in_specs=[whole()] * 4,
+        in_specs=[whole()] * 2,
         out_specs=(whole(),) * (2 * chips),
         compiler_params=params(2 if tight else 24),
     )(*in_vmem)

time: 45.3 us -> 42.9 us (0.947)
  Pallas kernels: 16 us -> 13.4 us
  waiting for transfers between devices: 11.2 us -> 12 us
  starting transfers between devices: 17.9 us -> 17.3 us
    pallas_call x1, Pallas kernels: 10.8 us -> 6.67 us  [body(): pl.pallas_call(functools.partial(expert_kernel, chips, chunk, depth), out...]
    pallas_call x1, Pallas kernels: 0.98 us -> 2.63 us  [down(): pl.pallas_call(functools.partial(rest_kernel, start), out_shape=(like(row...]
    ppermute x17 -> x16, waiting for transfers between devices: 11.2 us -> 12 us  [exchange(): return lax.ppermute(value, 'pool', [(i, i ^ bit) for i in range(devices)])]
    ppermute x17 -> x16, starting transfers between devices: 17.9 us -> 17.3 us  [exchange(): return lax.ppermute(value, 'pool', [(i, i ^ bit) for i in range(devices)])]
  transfers between devices with their start and end apart: 17 -> 16, of which waited for: 8 -> 9; matrix products, arithmetic and copies ran while one was open for 0% -> 0% of each run, Pallas kernels for 3% -> 1%
where the time goes in v6:
time: 42.9 us; the launch traced here: 42.8 us
  starting transfers between devices  17.3 us (40%)
  Pallas kernels  13.4 us (31%)
  waiting for transfers between devices  12 us (28%)
    ppermute x16, starting transfers between devices, exchange(): return lax.ppermute(value, 'pool', [(i, i ^ bit) for i in range(devices)])  17.3 us
    ppermute x16, waiting for transfers between devices, exchange(): return lax.ppermute(value, 'pool', [(i, i ^ bit) for i in range(devices)])  12 us
    pallas_call x1, Pallas kernels, body(): pl.pallas_call(functools.partial(expert_kernel, chips, chunk, depth), out...  6.67 us
    pallas_call x1, Pallas kernels, body(): pl.pallas_call(functools.partial(front_kernel, half), out_shape=(like(req...  2.66 us
    pallas_call x1, Pallas kernels, down(): pl.pallas_call(functools.partial(rest_kernel, start), out_shape=(like(row...  2.63 us
  transfers between devices with their start and end apart: 16, of which 9 were waited for; matrix products, arithmetic and copies ran while one was open for 0% of the time, Pallas kernels for 1%

profile of v6, /device:TPU:0, one launch (start us, length us, event | category | flops | bytes accessed | tf_op | source)
XLA Modules:
  0.0 42.8 jit_solution(1014252638130179570)
XLA Ops:
  0.0 2.7 %shard_map.109 = (f32[8,6144]{1,0:T(8,128)S(1)}, bf16[8,6144]{1,0:T(8,128)(2,1)S(1)}, bf16[4,6144]{1,0:T(4,128)(2,1)S(1)}, bf16[4,6144]{1,0:T(4,128)(2,1)S(1)}) custom-call(bf16[8,6144]{1,0:T(8,128)(2,1)} %hidden_hbm.1, bf16[8,6144]{1,0:T(8,128)(2,1)} %queries_hbm.1, bf16[128,2,1024]{2,1,0:T(2,128)(2,1)} %cached_hbm.1, bf16[8,2,1024]{2,1,0:T(2,128)(2,1)} %own_hbm.1, ...), custom_call_target="tpu_custom_call" | custom-call | flops 199999995904 | bytes 50000000 | tf_op jit(solution)/shard_map/pallas_call | solution.py:273
  2.7 4.1 %collective-permute-start = (bf16[4,6144]{1,0:T(4,128)(2,1)S(1)}, bf16[4,6144]{1,0:T(4,128)(2,1)S(1)}, u32[]{:S(2)}, u32[]{:S(2)}) collective-permute-start(bf16[4,6144]{1,0:T(4,128)(2,1)S(1)} %get-tuple-element.24), channel_id=1, source_target_pairs={{0,8},{1,9},{2,10},{3,11},{4,12},{5,13},{6,14},{7,15},{8,0},{9,1},... | collective-permute-start | bytes 147464 | tf_op jit(solution)/shard_map/ppermute | solution.py:263
  6.8 2.6 %collective-permute-done.arrived_ref = bf16[4,6144]{1,0:T(4,128)(2,1)S(1)} collective-permute-done((bf16[4,6144]{1,0:T(4,128)(2,1)S(1)}, bf16[4,6144]{1,0:T(4,128)(2,1)S(1)}, u32[]{:S(2)}, u32[]{:S(2)}) %collective-permute-start) | collective-permute-done | bytes 49184 | tf_op jit(solution)/shard_map/ppermute | solution.py:263
  9.4 2.4 %collective-permute-start.3 = (bf16[8,6144]{1,0:T(8,128)(2,1)S(1)}, bf16[8,6144]{1,0:T(8,128)(2,1)S(1)}, u32[]{:S(2)}, u32[]{:S(2)}) collective-permute-start(bf16[8,6144]{1,0:T(8,128)(2,1)S(1)} %shard_map.110.refs_0_), channel_id=1, source_target_pairs={{0,6},{1,7},{2,4},{3,5},{4,2},{5,3},{6,0},{7,1},{8,14},{9,15},{10,... | collective-permute-start | bytes 294920 | tf_op jit(solution)/shard_map/ppermute | solution.py:263
  11.8 0.9 %collective-permute-start.2 = (bf16[8,6144]{1,0:T(8,128)(2,1)S(1)}, bf16[8,6144]{1,0:T(8,128)(2,1)S(1)}, u32[]{:S(2)}, u32[]{:S(2)}) collective-permute-start(bf16[8,6144]{1,0:T(8,128)(2,1)S(1)} %shard_map.110.refs_0_), channel_id=1, source_target_pairs={{0,4},{1,5},{2,6},{3,7},{4,0},{5,1},{6,2},{7,3},{8,12},{9,13},{10,... | collective-permute-start | bytes 294920 | tf_op jit(solution)/shard_map/ppermute | solution.py:263
  12.7 0.3 collective-permute-start.1
  13.0 2.1 %collective-permute-done.3.refs_3_ = bf16[8,6144]{1,0:T(8,128)(2,1)S(1)} collective-permute-done((bf16[8,6144]{1,0:T(8,128)(2,1)S(1)}, bf16[8,6144]{1,0:T(8,128)(2,1)S(1)}, u32[]{:S(2)}, u32[]{:S(2)}) %collective-permute-start.3) | collective-permute-done | bytes 98336 | tf_op jit(solution)/shard_map/ppermute | solution.py:263
  15.1 1.3 %collective-permute-done.2.refs_2_ = bf16[8,6144]{1,0:T(8,128)(2,1)S(1)} collective-permute-done((bf16[8,6144]{1,0:T(8,128)(2,1)S(1)}, bf16[8,6144]{1,0:T(8,128)(2,1)S(1)}, u32[]{:S(2)}, u32[]{:S(2)}) %collective-permute-start.2) | collective-permute-done | bytes 98336 | tf_op jit(solution)/shard_map/ppermute | solution.py:263
  16.4 0.9 %collective-permute-done.1.refs_1_ = bf16[8,6144]{1,0:T(8,128)(2,1)S(1)} collective-permute-done((bf16[8,6144]{1,0:T(8,128)(2,1)S(1)}, bf16[8,6144]{1,0:T(8,128)(2,1)S(1)}, u32[]{:S(2)}, u32[]{:S(2)}) %collective-permute-start.1) | collective-permute-done | bytes 98336 | tf_op jit(solution)/shard_map/ppermute | solution.py:263
  17.3 0.4 %collective-permute-done.6.refs_6_ = bf16[8,6144]{1,0:T(8,128)(2,1)S(1)} collective-permute-done((bf16[8,6144]{1,0:T(8,128)(2,1)S(1)}, bf16[8,6144]{1,0:T(8,128)(2,1)S(1)}, u32[]{:S(2)}, u32[]{:S(2)}) %collective-permute-start.6) | collective-permute-done | bytes 98336 | tf_op jit(solution)/shard_map/ppermute | solution.py:263
  17.7 0.9 %collective-permute-done.5.refs_5_ = bf16[8,6144]{1,0:T(8,128)(2,1)S(1)} collective-permute-done((bf16[8,6144]{1,0:T(8,128)(2,1)S(1)}, bf16[8,6144]{1,0:T(8,128)(2,1)S(1)}, u32[]{:S(2)}, u32[]{:S(2)}) %collective-permute-start.5) | collective-permute-done | bytes 98336 | tf_op jit(solution)/shard_map/ppermute | solution.py:263
  18.6 6.7 %shard_map.111.inner_ref = bf16[64,1344]{1,0:T(8,128)(2,1)S(1)} custom-call(bf16[8,6144]{1,0:T(8,128)(2,1)S(1)} %shard_map.110.refs_0_, bf16[8,6144]{1,0:T(8,128)(2,1)S(1)} %collective-permute-done.1.refs_1_, bf16[8,6144]{1,0:T(8,128)(2,1)S(1)} %collective-permute-done.2.refs_2_, bf16[8,6144]{1,0:T(8,128)(2,1)S(1)} %collective-permute-done.3.refs_3_, ...), custom_call_target="tpu_custom_call" | custom-call | tf_op jit(solution)/shard_map/pallas_call | solution.py:307
  25.3 2.6 %shard_map.112 = (f32[32,6144]{1,0:T(8,128)S(1)}, bf16[32,6144]{1,0:T(8,128)(2,1)S(1)}) custom-call(bf16[64,1344]{1,0:T(8,128)(2,1)S(1)} %shard_map.111.inner_ref, bf16[1344,6144]{1,0:T(8,128)(2,1)S(1)} %bitcast.10), custom_call_target="tpu_custom_call" | custom-call | tf_op jit(solution)/shard_map/pallas_call | solution.py:317
  28.2 1.6 %collective-permute-done.8.recv_ref = bf16[32,6144]{1,0:T(8,128)(2,1)S(1)} collective-permute-done((bf16[32,6144]{1,0:T(8,128)(2,1)S(1)}, bf16[32,6144]{1,0:T(8,128)(2,1)S(1)}, u32[]{:S(2)}, u32[]{:S(2)}) %collective-permute-start.8) | collective-permute-done | bytes 393248 | tf_op jit(solution)/shard_map/ppermute | solution.py:263
  29.8 1.2 %collective-permute-start.12 = (bf16[4,6144]{1,0:T(4,128)(2,1)S(1)}, bf16[4,6144]{1,0:T(4,128)(2,1)S(1)}, u32[]{:S(2)}, u32[]{:S(2)}) collective-permute-start(bf16[4,6144]{1,0:T(4,128)(2,1)S(1)} %get-tuple-element.34), channel_id=1, source_target_pairs={{0,6},{1,7},{2,4},{3,5},{4,2},{5,3},{6,0},{7,1},{8,14},{9,15},{10,... | collective-permute-start | bytes 147464 | tf_op jit(solution)/shard_map/ppermute | solution.py:263
  31.0 0.8 %collective-permute-start.13 = (bf16[4,6144]{1,0:T(4,128)(2,1)S(1)}, bf16[4,6144]{1,0:T(4,128)(2,1)S(1)}, u32[]{:S(2)}, u32[]{:S(2)}) collective-permute-start(bf16[4,6144]{1,0:T(4,128)(2,1)S(1)} %get-tuple-element.35), channel_id=1, source_target_pairs={{0,4},{1,5},{2,6},{3,7},{4,0},{5,1},{6,2},{7,3},{8,12},{9,13},{10,... | collective-permute-start | bytes 147464 | tf_op jit(solution)/shard_map/ppermute | solution.py:263
  31.8 1.5 %collective-permute-start.14 = (bf16[4,6144]{1,0:T(4,128)(2,1)S(1)}, bf16[4,6144]{1,0:T(4,128)(2,1)S(1)}, u32[]{:S(2)}, u32[]{:S(2)}) collective-permute-start(bf16[4,6144]{1,0:T(4,128)(2,1)S(1)} %get-tuple-element.36), channel_id=1, source_target_pairs={{0,2},{1,3},{2,0},{3,1},{4,6},{5,7},{6,4},{7,5},{8,10},{9,11},{10,... | collective-permute-start | bytes 147464 | tf_op jit(solution)/shard_map/ppermute | solution.py:263
  33.4 1.1 %collective-permute-start.9 = (bf16[4,6144]{1,0:T(4,128)(2,1)S(1)}, bf16[4,6144]{1,0:T(4,128)(2,1)S(1)}, u32[]{:S(2)}, u32[]{:S(2)}) collective-permute-start(bf16[4,6144]{1,0:T(4,128)(2,1)S(1)} %get-tuple-element.28), channel_id=1, source_target_pairs={{0,6},{1,7},{2,4},{3,5},{4,2},{5,3},{6,0},{7,1},{8,14},{9,15},{10,... | collective-permute-start | bytes 147464 | tf_op jit(solution)/shard_map/ppermute | solution.py:263
  34.5 0.8 %collective-permute-start.10 = (bf16[4,6144]{1,0:T(4,128)(2,1)S(1)}, bf16[4,6144]{1,0:T(4,128)(2,1)S(1)}, u32[]{:S(2)}, u32[]{:S(2)}) collective-permute-start(bf16[4,6144]{1,0:T(4,128)(2,1)S(1)} %get-tuple-element.29), channel_id=1, source_target_pairs={{0,4},{1,5},{2,6},{3,7},{4,0},{5,1},{6,2},{7,3},{8,12},{9,13},{10,... | collective-permute-start | bytes 147464 | tf_op jit(solution)/shard_map/ppermute | solution.py:263
  35.3 1.5 %collective-permute-start.11 = (bf16[4,6144]{1,0:T(4,128)(2,1)S(1)}, bf16[4,6144]{1,0:T(4,128)(2,1)S(1)}, u32[]{:S(2)}, u32[]{:S(2)}) collective-permute-start(bf16[4,6144]{1,0:T(4,128)(2,1)S(1)} %get-tuple-element.30), channel_id=1, source_target_pairs={{0,2},{1,3},{2,0},{3,1},{4,6},{5,7},{6,4},{7,5},{8,10},{9,11},{10,... | collective-permute-start | bytes 147464 | tf_op jit(solution)/shard_map/ppermute | solution.py:263
  36.9 2.4 %collective-permute-start.15 = (bf16[4,6144]{1,0:T(4,128)(2,1)S(1)}, bf16[4,6144]{1,0:T(4,128)(2,1)S(1)}, u32[]{:S(2)}, u32[]{:S(2)}) collective-permute-start(bf16[4,6144]{1,0:T(4,128)(2,1)S(1)} %shard_map.115), channel_id=1, source_target_pairs={{0,8},{1,9},{2,10},{3,11},{4,12},{5,13},{6,14},{7,15},{8,0},{9,1},... | collective-permute-start | bytes 147464 | tf_op jit(solution)/shard_map/ppermute | solution.py:263
  39.4 0.5 %shard_map.114 = (f32[8,6144]{1,0:T(8,128)S(1)}, f32[8,8]{1,0:T(8,128)S(1)}) custom-call(f32[8,6144]{1,0:T(8,128)S(1)} %get-tuple-element.21.residual_ref, bf16[8,6144]{1,0:T(8,128)(2,1)S(1)} %get-tuple-element.22.normed_ref, bf16[16,6144]{1,0:T(8,128)(2,1)S(1)} %bitcast.13, s32[4,8]{1,0:T(4,128)S(1)} %bitcast.15, f32[4,6144]{1,0:T(4,128)S(1)} %get-tuple-element.27.near_ref, ...), custom_call_target="tpu_custom_call" | custom-call | tf_op jit(solution)/shard_map/pallas_call | solution.py:346
  39.9 2.0 %collective-permute-done.15.far_ref = bf16[4,6144]{1,0:T(4,128)(2,1)S(1)} collective-permute-done((bf16[4,6144]{1,0:T(4,128)(2,1)S(1)}, bf16[4,6144]{1,0:T(4,128)(2,1)S(1)}, u32[]{:S(2)}, u32[]{:S(2)}) %collective-permute-start.15) | collective-permute-done | bytes 49184 | tf_op jit(solution)/shard_map/ppermute | solution.py:263
  42.0 0.8 %shard_map.116 = bf16[8,6144]{1,0:T(8,128)(2,1)} custom-call(f32[8,6144]{1,0:T(8,128)S(1)} %get-tuple-element.31.base_ref, f32[8,8]{1,0:T(8,128)S(1)} %get-tuple-element.32.mix_ref, bf16[4,6144]{1,0:T(4,128)(2,1)S(1)} %collective-permute-done.15.far_ref), custom_call_target="tpu_custom_call" | custom-call | tf_op jit(solution)/shard_map/pallas_call | solution.py:353
  (26 shorter events, 0.5 us)
Async XLA Ops:
  0.0 18.6 %copy-start.1 = (bf16[1,6144,1344]{1,2,0:T(8,128)(2,1)S(1)}, bf16[1,6144,1344]{1,2,0:T(8,128)(2,1)}, u32[]{:S(2)}) copy-start(bf16[1,6144,1344]{1,2,0:T(8,128)(2,1)} %param.19) | copy-start | bytes 49545220
  0.0 18.6 %copy-start.2 = (bf16[1,6144,1344]{1,2,0:T(8,128)(2,1)S(1)}, bf16[1,6144,1344]{1,2,0:T(8,128)(2,1)}, u32[]{:S(2)}) copy-start(bf16[1,6144,1344]{1,2,0:T(8,128)(2,1)} %param.20) | copy-start | bytes 49545220
  2.7 6.7 %collective-permute-start = (bf16[4,6144]{1,0:T(4,128)(2,1)S(1)}, bf16[4,6144]{1,0:T(4,128)(2,1)S(1)}, u32[]{:S(2)}, u32[]{:S(2)}) collective-permute-start(bf16[4,6144]{1,0:T(4,128)(2,1)S(1)} %get-tuple-element.24), channel_id=1, source_target_pairs={{0,8},{1,9},{2,10},{3,11},{4,12},{5,13},{6,14},{7,15},{8,0},{9,1},... | collective-permute-start | bytes 147464 | tf_op jit(solution)/shard_map/ppermute | solution.py:263
  9.4 5.7 %collective-permute-start.3 = (bf16[8,6144]{1,0:T(8,128)(2,1)S(1)}, bf16[8,6144]{1,0:T(8,128)(2,1)S(1)}, u32[]{:S(2)}, u32[]{:S(2)}) collective-permute-start(bf16[8,6144]{1,0:T(8,128)(2,1)S(1)} %shard_map.110.refs_0_), channel_id=1, source_target_pairs={{0,6},{1,7},{2,4},{3,5},{4,2},{5,3},{6,0},{7,1},{8,14},{9,15},{10,... | collective-permute-start | bytes 294920 | tf_op jit(solution)/shard_map/ppermute | solution.py:263
  11.8 4.6 %collective-permute-start.2 = (bf16[8,6144]{1,0:T(8,128)(2,1)S(1)}, bf16[8,6144]{1,0:T(8,128)(2,1)S(1)}, u32[]{:S(2)}, u32[]{:S(2)}) collective-permute-start(bf16[8,6144]{1,0:T(8,128)(2,1)S(1)} %shard_map.110.refs_0_), channel_id=1, source_target_pairs={{0,4},{1,5},{2,6},{3,7},{4,0},{5,1},{6,2},{7,3},{8,12},{9,13},{10,... | collective-permute-start | bytes 294920 | tf_op jit(solution)/shard_map/ppermute | solution.py:263
  12.7 4.6 %collective-permute-start.1 = (bf16[8,6144]{1,0:T(8,128)(2,1)S(1)}, bf16[8,6144]{1,0:T(8,128)(2,1)S(1)}, u32[]{:S(2)}, u32[]{:S(2)}) collective-permute-start(bf16[8,6144]{1,0:T(8,128)(2,1)S(1)} %shard_map.110.refs_0_), channel_id=1, source_target_pairs={{0,2},{1,3},{2,0},{3,1},{4,6},{5,7},{6,4},{7,5},{8,10},{9,11},{10,... | collective-permute-start | bytes 294920 | tf_op jit(solution)/shard_map/ppermute | solution.py:263
  13.0 4.3 %collective-permute-start.4 = (bf16[8,6144]{1,0:T(8,128)(2,1)S(1)}, bf16[8,6144]{1,0:T(8,128)(2,1)S(1)}, u32[]{:S(2)}, u32[]{:S(2)}) collective-permute-start(bf16[8,6144]{1,0:T(8,128)(2,1)S(1)} %shard_map.110.refs_0_), channel_id=1, source_target_pairs={{0,1},{1,0},{2,3},{3,2},{4,5},{5,4},{6,7},{7,6},{8,9},{9,8},{10,11... | collective-permute-start | bytes 294920 | tf_op jit(solution)/shard_map/ppermute | solution.py:263
  15.1 2.2 %collective-permute-start.7 = (bf16[8,6144]{1,0:T(8,128)(2,1)S(1)}, bf16[8,6144]{1,0:T(8,128)(2,1)S(1)}, u32[]{:S(2)}, u32[]{:S(2)}) collective-permute-start(bf16[8,6144]{1,0:T(8,128)(2,1)S(1)} %collective-permute-done.3.refs_3_), channel_id=1, source_target_pairs={{0,1},{1,0},{2,3},{3,2},{4,5},{5,4},{6,7},{7,6},{8,9},{9,8},{10,11... | collective-permute-start | bytes 294920 | tf_op jit(solution)/shard_map/ppermute | solution.py:263
  16.4 1.3 %collective-permute-start.6 = (bf16[8,6144]{1,0:T(8,128)(2,1)S(1)}, bf16[8,6144]{1,0:T(8,128)(2,1)S(1)}, u32[]{:S(2)}, u32[]{:S(2)}) collective-permute-start(bf16[8,6144]{1,0:T(8,128)(2,1)S(1)} %collective-permute-done.2.refs_2_), channel_id=1, source_target_pairs={{0,1},{1,0},{2,3},{3,2},{4,5},{5,4},{6,7},{7,6},{8,9},{9,8},{10,11... | collective-permute-start | bytes 294920 | tf_op jit(solution)/shard_map/ppermute | solution.py:263
  17.3 1.3 %collective-permute-start.5 = (bf16[8,6144]{1,0:T(8,128)(2,1)S(1)}, bf16[8,6144]{1,0:T(8,128)(2,1)S(1)}, u32[]{:S(2)}, u32[]{:S(2)}) collective-permute-start(bf16[8,6144]{1,0:T(8,128)(2,1)S(1)} %collective-permute-done.1.refs_1_), channel_id=1, source_target_pairs={{0,1},{1,0},{2,3},{3,2},{4,5},{5,4},{6,7},{7,6},{8,9},{9,8},{10,11... | collective-permute-start | bytes 294920 | tf_op jit(solution)/shard_map/ppermute | solution.py:263
  18.6 6.7 %copy-start = (bf16[1,1344,6144]{2,1,0:T(8,128)(2,1)S(1)}, bf16[1,1344,6144]{2,1,0:T(8,128)(2,1)}, u32[]{:S(2)}) copy-start(bf16[1,1344,6144]{2,1,0:T(8,128)(2,1)} %param.21) | copy-start | bytes 49545220
  25.3 14.2 %copy-start.3 = (bf16[6144,16]{0,1:T(8,128)(2,1)S(1)}, bf16[6144,16]{0,1:T(8,128)(2,1)}, u32[]{:S(2)}) copy-start(bf16[6144,16]{0,1:T(8,128)(2,1)} %param.18) | copy-start | bytes 589828
  25.3 14.1 %copy-start.4 = (s32[8,4]{0,1:T(4,128)S(1)}, s32[8,4]{0,1:T(4,128)}, u32[]{:S(2)}) copy-start(s32[8,4]{0,1:T(4,128)} %param.16) | copy-start | bytes 388
  27.9 1.8 %collective-permute-start.8 = (bf16[32,6144]{1,0:T(8,128)(2,1)S(1)}, bf16[32,6144]{1,0:T(8,128)(2,1)S(1)}, u32[]{:S(2)}, u32[]{:S(2)}) collective-permute-start(bf16[32,6144]{1,0:T(8,128)(2,1)S(1)} %get-tuple-element.26), channel_id=1, source_target_pairs={{0,1},{1,0},{2,3},{3,2},{4,5},{5,4},{6,7},{7,6},{8,9},{9,8},{10,11... | collective-permute-start | bytes 1179656 | tf_op jit(solution)/shard_map/ppermute | solution.py:263
  29.8 5.5 %collective-permute-start.12 = (bf16[4,6144]{1,0:T(4,128)(2,1)S(1)}, bf16[4,6144]{1,0:T(4,128)(2,1)S(1)}, u32[]{:S(2)}, u32[]{:S(2)}) collective-permute-start(bf16[4,6144]{1,0:T(4,128)(2,1)S(1)} %get-tuple-element.34), channel_id=1, source_target_pairs={{0,6},{1,7},{2,4},{3,5},{4,2},{5,3},{6,0},{7,1},{8,14},{9,15},{10,... | collective-permute-start | bytes 147464 | tf_op jit(solution)/shard_map/ppermute | solution.py:263
  31.0 5.9 %collective-permute-start.13 = (bf16[4,6144]{1,0:T(4,128)(2,1)S(1)}, bf16[4,6144]{1,0:T(4,128)(2,1)S(1)}, u32[]{:S(2)}, u32[]{:S(2)}) collective-permute-start(bf16[4,6144]{1,0:T(4,128)(2,1)S(1)} %get-tuple-element.35), channel_id=1, source_target_pairs={{0,4},{1,5},{2,6},{3,7},{4,0},{5,1},{6,2},{7,3},{8,12},{9,13},{10,... | collective-permute-start | bytes 147464 | tf_op jit(solution)/shard_map/ppermute | solution.py:263
  31.8 5.0 %collective-permute-start.14 = (bf16[4,6144]{1,0:T(4,128)(2,1)S(1)}, bf16[4,6144]{1,0:T(4,128)(2,1)S(1)}, u32[]{:S(2)}, u32[]{:S(2)}) collective-permute-start(bf16[4,6144]{1,0:T(4,128)(2,1)S(1)} %get-tuple-element.36), channel_id=1, source_target_pairs={{0,2},{1,3},{2,0},{3,1},{4,6},{5,7},{6,4},{7,5},{8,10},{9,11},{10,... | collective-permute-start | bytes 147464 | tf_op jit(solution)/shard_map/ppermute | solution.py:263
  33.4 5.9 %collective-permute-start.9 = (bf16[4,6144]{1,0:T(4,128)(2,1)S(1)}, bf16[4,6144]{1,0:T(4,128)(2,1)S(1)}, u32[]{:S(2)}, u32[]{:S(2)}) collective-permute-start(bf16[4,6144]{1,0:T(4,128)(2,1)S(1)} %get-tuple-element.28), channel_id=1, source_target_pairs={{0,6},{1,7},{2,4},{3,5},{4,2},{5,3},{6,0},{7,1},{8,14},{9,15},{10,... | collective-permute-start | bytes 147464 | tf_op jit(solution)/shard_map/ppermute | solution.py:263
  34.5 4.8 %collective-permute-start.10 = (bf16[4,6144]{1,0:T(4,128)(2,1)S(1)}, bf16[4,6144]{1,0:T(4,128)(2,1)S(1)}, u32[]{:S(2)}, u32[]{:S(2)}) collective-permute-start(bf16[4,6144]{1,0:T(4,128)(2,1)S(1)} %get-tuple-element.29), channel_id=1, source_target_pairs={{0,4},{1,5},{2,6},{3,7},{4,0},{5,1},{6,2},{7,3},{8,12},{9,13},{10,... | collective-permute-start | bytes 147464 | tf_op jit(solution)/shard_map/ppermute | solution.py:263
  35.3 4.1 %collective-permute-start.11 = (bf16[4,6144]{1,0:T(4,128)(2,1)S(1)}, bf16[4,6144]{1,0:T(4,128)(2,1)S(1)}, u32[]{:S(2)}, u32[]{:S(2)}) collective-permute-start(bf16[4,6144]{1,0:T(4,128)(2,1)S(1)} %get-tuple-element.30), channel_id=1, source_target_pairs={{0,2},{1,3},{2,0},{3,1},{4,6},{5,7},{6,4},{7,5},{8,10},{9,11},{10,... | collective-permute-start | bytes 147464 | tf_op jit(solution)/shard_map/ppermute | solution.py:263
  36.9 5.1 %collective-permute-start.15 = (bf16[4,6144]{1,0:T(4,128)(2,1)S(1)}, bf16[4,6144]{1,0:T(4,128)(2,1)S(1)}, u32[]{:S(2)}, u32[]{:S(2)}) collective-permute-start(bf16[4,6144]{1,0:T(4,128)(2,1)S(1)} %shard_map.115), channel_id=1, source_target_pairs={{0,8},{1,9},{2,10},{3,11},{4,12},{5,13},{6,14},{7,15},{8,0},{9,1},... | collective-permute-start | bytes 147464 | tf_op jit(solution)/shard_map/ppermute | solution.py:263

commit v7 on v6

--- a/solution.py
+++ b/solution.py
@@ -76,6 +76,14 @@
     inside = (column >= 2 * starts) & (column < 2 * ends) & (column % 2 == 0)
     bias = jnp.where(inside, 0.0, -jnp.inf).astype(F32)
     bias = jnp.concatenate([bias] * groups, axis=0)
+    copies[6].wait()
+    mine = half()
+    slot = iota((near_ref.shape[0], requests), 0).astype(F32)
+    placing = []
+    for expert in (mine, 1 - mine):
+        named, before = slot_rows(routes_ref[...], expert)
+        placing.append(jnp.where(before == slot, named, 0.0))
+    placing = jnp.concatenate(placing, axis=0).astype(BF16)
     copies[1].wait()
     queries = queries_ref[...].astype(F32)
     copies[3].wait()
@@ -114,14 +122,10 @@
     copies[5].wait()
     normed = (centered * lax.rsqrt(spread_of + EPSILON) * gain_ref[...]).astype(BF16)
     normed_ref[...] = normed
-    copies[6].wait()
-    mine = half()
     capacity = near_ref.shape[0]
-    slot = iota((capacity, requests), 0).astype(F32)
-    for expert, out in ((mine, near_ref), (1 - mine, far_ref)):
-        named, before = slot_rows(routes_ref[...], expert)
-        placing = jnp.where(before == slot, named, 0.0).astype(BF16)
-        out[...] = jnp.dot(placing, normed, preferred_element_type=F32).astype(BF16)
+    packed = jnp.dot(placing, normed, preferred_element_type=F32).astype(BF16)
+    near_ref[...] = packed[:capacity]
+    far_ref[...] = packed[capacity:]
 
 
 def gate_mix(half, normed_ref, router_ref, routes_ref, capacity):
@@ -218,9 +222,19 @@
     base_ref[...] = residual_ref[...] + weighted(mix, total.astype(BF16).astype(F32), 0)
 
 
-def mix_kernel(base_ref, mix_ref, far_ref, out_ref):
-    rows = far_ref[...].astype(F32)
-    out_ref[...] = (base_ref[...] + weighted(mix_ref[...], rows, rows.shape[0])).astype(BF16)
+def mix_kernel(base_ref, mix_ref, far_ref, out_hbm, out_ref, sems):
+    mix = mix_ref[...]
+    width = base_ref.shape[1]
+    part = width // 3 // 128 * 128
+    copies = []
+    for i, start in enumerate(range(0, width, part)):
+        at = pl.ds(start, part)
+        rows = far_ref[:, at].astype(F32)
+        out_ref[:, at] = (base_ref[:, at] + weighted(mix, rows, rows.shape[0])).astype(BF16)
+        copies.append(pltpu.make_async_copy(out_ref.at[:, at], out_hbm.at[:, at], sems.at[i]))
+        copies[-1].start()
+    for copy in copies:
+        copy.wait()
 
 
 def like(*shape, dtype=BF16):
@@ -354,7 +368,8 @@
         mix_kernel,
         out_shape=like(requests, width),
         in_specs=[whole()] * 3,
-        out_specs=whole(),
+        out_specs=whole(pltpu.HBM),
+        scratch_shapes=[pltpu.VMEM((requests, width), BF16), pltpu.SemaphoreType.DMA((3,))],
         compiler_params=params(2 if tight else 24),
     )(base, mix, back)
 

time: 42.9 us -> 42.8 us (level)
  no operation moved by 1% of the time
where the time goes in v7:
time: 42.8 us; the launch traced here: 42.6 us
  starting transfers between devices  17.3 us (40%)
  Pallas kernels  13.2 us (31%)
  waiting for transfers between devices  11.9 us (28%)
    ppermute x16, starting transfers between devices, exchange(): return lax.ppermute(value, 'pool', [(i, i ^ bit) for i in range(devices)])  17.3 us
    ppermute x16, waiting for transfers between devices, exchange(): return lax.ppermute(value, 'pool', [(i, i ^ bit) for i in range(devices)])  11.9 us
    pallas_call x1, Pallas kernels, body(): pl.pallas_call(functools.partial(expert_kernel, chips, chunk, depth), out...  6.66 us
    pallas_call x1, Pallas kernels, down(): pl.pallas_call(functools.partial(rest_kernel, start), out_shape=(like(row...  2.63 us
    pallas_call x1, Pallas kernels, body(): pl.pallas_call(functools.partial(front_kernel, half), out_shape=(like(req...  2.49 us
  transfers between devices with their start and end apart: 16, of which 9 were waited for; matrix products, arithmetic and copies ran while one was open for 0% of the time, Pallas kernels for 1%

profile of v7, /device:TPU:0, one launch (start us, length us, event | category | flops | bytes accessed | tf_op | source)
XLA Modules:
  0.0 42.6 jit_solution(14388693918372650160)
XLA Ops:
  0.0 2.5 %shard_map.109 = (f32[8,6144]{1,0:T(8,128)S(1)}, bf16[8,6144]{1,0:T(8,128)(2,1)S(1)}, bf16[4,6144]{1,0:T(4,128)(2,1)S(1)}, bf16[4,6144]{1,0:T(4,128)(2,1)S(1)}) custom-call(bf16[8,6144]{1,0:T(8,128)(2,1)} %hidden_hbm.1, bf16[8,6144]{1,0:T(8,128)(2,1)} %queries_hbm.1, bf16[128,2,1024]{2,1,0:T(2,128)(2,1)} %cached_hbm.1, bf16[8,2,1024]{2,1,0:T(2,128)(2,1)} %own_hbm.1, ...), custom_call_target="tpu_custom_call" | custom-call | flops 199999995904 | bytes 50000000 | tf_op jit(solution)/shard_map/pallas_call | solution.py:287
  2.5 4.1 %collective-permute-start = (bf16[4,6144]{1,0:T(4,128)(2,1)S(1)}, bf16[4,6144]{1,0:T(4,128)(2,1)S(1)}, u32[]{:S(2)}, u32[]{:S(2)}) collective-permute-start(bf16[4,6144]{1,0:T(4,128)(2,1)S(1)} %get-tuple-element.24), channel_id=1, source_target_pairs={{0,8},{1,9},{2,10},{3,11},{4,12},{5,13},{6,14},{7,15},{8,0},{9,1},... | collective-permute-start | bytes 147464 | tf_op jit(solution)/shard_map/ppermute | solution.py:277
  6.6 2.6 %collective-permute-done.arrived_ref = bf16[4,6144]{1,0:T(4,128)(2,1)S(1)} collective-permute-done((bf16[4,6144]{1,0:T(4,128)(2,1)S(1)}, bf16[4,6144]{1,0:T(4,128)(2,1)S(1)}, u32[]{:S(2)}, u32[]{:S(2)}) %collective-permute-start) | collective-permute-done | bytes 49184 | tf_op jit(solution)/shard_map/ppermute | solution.py:277
  9.2 2.4 %collective-permute-start.3 = (bf16[8,6144]{1,0:T(8,128)(2,1)S(1)}, bf16[8,6144]{1,0:T(8,128)(2,1)S(1)}, u32[]{:S(2)}, u32[]{:S(2)}) collective-permute-start(bf16[8,6144]{1,0:T(8,128)(2,1)S(1)} %shard_map.110.refs_0_), channel_id=1, source_target_pairs={{0,6},{1,7},{2,4},{3,5},{4,2},{5,3},{6,0},{7,1},{8,14},{9,15},{10,... | collective-permute-start | bytes 294920 | tf_op jit(solution)/shard_map/ppermute | solution.py:277
  11.6 0.9 %collective-permute-start.2 = (bf16[8,6144]{1,0:T(8,128)(2,1)S(1)}, bf16[8,6144]{1,0:T(8,128)(2,1)S(1)}, u32[]{:S(2)}, u32[]{:S(2)}) collective-permute-start(bf16[8,6144]{1,0:T(8,128)(2,1)S(1)} %shard_map.110.refs_0_), channel_id=1, source_target_pairs={{0,4},{1,5},{2,6},{3,7},{4,0},{5,1},{6,2},{7,3},{8,12},{9,13},{10,... | collective-permute-start | bytes 294920 | tf_op jit(solution)/shard_map/ppermute | solution.py:277
  12.5 0.3 collective-permute-start.1
  12.8 2.1 %collective-permute-done.3.refs_3_ = bf16[8,6144]{1,0:T(8,128)(2,1)S(1)} collective-permute-done((bf16[8,6144]{1,0:T(8,128)(2,1)S(1)}, bf16[8,6144]{1,0:T(8,128)(2,1)S(1)}, u32[]{:S(2)}, u32[]{:S(2)}) %collective-permute-start.3) | collective-permute-done | bytes 98336 | tf_op jit(solution)/shard_map/ppermute | solution.py:277
  14.9 1.3 %collective-permute-done.2.refs_2_ = bf16[8,6144]{1,0:T(8,128)(2,1)S(1)} collective-permute-done((bf16[8,6144]{1,0:T(8,128)(2,1)S(1)}, bf16[8,6144]{1,0:T(8,128)(2,1)S(1)}, u32[]{:S(2)}, u32[]{:S(2)}) %collective-permute-start.2) | collective-permute-done | bytes 98336 | tf_op jit(solution)/shard_map/ppermute | solution.py:277
  16.3 0.9 %collective-permute-done.1.refs_1_ = bf16[8,6144]{1,0:T(8,128)(2,1)S(1)} collective-permute-done((bf16[8,6144]{1,0:T(8,128)(2,1)S(1)}, bf16[8,6144]{1,0:T(8,128)(2,1)S(1)}, u32[]{:S(2)}, u32[]{:S(2)}) %collective-permute-start.1) | collective-permute-done | bytes 98336 | tf_op jit(solution)/shard_map/ppermute | solution.py:277
  17.1 0.4 %collective-permute-done.6.refs_6_ = bf16[8,6144]{1,0:T(8,128)(2,1)S(1)} collective-permute-done((bf16[8,6144]{1,0:T(8,128)(2,1)S(1)}, bf16[8,6144]{1,0:T(8,128)(2,1)S(1)}, u32[]{:S(2)}, u32[]{:S(2)}) %collective-permute-start.6) | collective-permute-done | bytes 98336 | tf_op jit(solution)/shard_map/ppermute | solution.py:277
  17.6 0.9 %collective-permute-done.5.refs_5_ = bf16[8,6144]{1,0:T(8,128)(2,1)S(1)} collective-permute-done((bf16[8,6144]{1,0:T(8,128)(2,1)S(1)}, bf16[8,6144]{1,0:T(8,128)(2,1)S(1)}, u32[]{:S(2)}, u32[]{:S(2)}) %collective-permute-start.5) | collective-permute-done | bytes 98336 | tf_op jit(solution)/shard_map/ppermute | solution.py:277
  18.4 6.7 %shard_map.111.inner_ref = bf16[64,1344]{1,0:T(8,128)(2,1)S(1)} custom-call(bf16[8,6144]{1,0:T(8,128)(2,1)S(1)} %shard_map.110.refs_0_, bf16[8,6144]{1,0:T(8,128)(2,1)S(1)} %collective-permute-done.1.refs_1_, bf16[8,6144]{1,0:T(8,128)(2,1)S(1)} %collective-permute-done.2.refs_2_, bf16[8,6144]{1,0:T(8,128)(2,1)S(1)} %collective-permute-done.3.refs_3_, ...), custom_call_target="tpu_custom_call" | custom-call | tf_op jit(solution)/shard_map/pallas_call | solution.py:321
  25.1 2.6 %shard_map.112 = (f32[32,6144]{1,0:T(8,128)S(1)}, bf16[32,6144]{1,0:T(8,128)(2,1)S(1)}) custom-call(bf16[64,1344]{1,0:T(8,128)(2,1)S(1)} %shard_map.111.inner_ref, bf16[1344,6144]{1,0:T(8,128)(2,1)S(1)} %bitcast.10), custom_call_target="tpu_custom_call" | custom-call | tf_op jit(solution)/shard_map/pallas_call | solution.py:331
  28.0 1.6 %collective-permute-done.8.recv_ref = bf16[32,6144]{1,0:T(8,128)(2,1)S(1)} collective-permute-done((bf16[32,6144]{1,0:T(8,128)(2,1)S(1)}, bf16[32,6144]{1,0:T(8,128)(2,1)S(1)}, u32[]{:S(2)}, u32[]{:S(2)}) %collective-permute-start.8) | collective-permute-done | bytes 393248 | tf_op jit(solution)/shard_map/ppermute | solution.py:277
  29.6 1.2 %collective-permute-start.12 = (bf16[4,6144]{1,0:T(4,128)(2,1)S(1)}, bf16[4,6144]{1,0:T(4,128)(2,1)S(1)}, u32[]{:S(2)}, u32[]{:S(2)}) collective-permute-start(bf16[4,6144]{1,0:T(4,128)(2,1)S(1)} %get-tuple-element.34), channel_id=1, source_target_pairs={{0,6},{1,7},{2,4},{3,5},{4,2},{5,3},{6,0},{7,1},{8,14},{9,15},{10,... | collective-permute-start | bytes 147464 | tf_op jit(solution)/shard_map/ppermute | solution.py:277
  30.8 0.8 %collective-permute-start.13 = (bf16[4,6144]{1,0:T(4,128)(2,1)S(1)}, bf16[4,6144]{1,0:T(4,128)(2,1)S(1)}, u32[]{:S(2)}, u32[]{:S(2)}) collective-permute-start(bf16[4,6144]{1,0:T(4,128)(2,1)S(1)} %get-tuple-element.35), channel_id=1, source_target_pairs={{0,4},{1,5},{2,6},{3,7},{4,0},{5,1},{6,2},{7,3},{8,12},{9,13},{10,... | collective-permute-start | bytes 147464 | tf_op jit(solution)/shard_map/ppermute | solution.py:277
  31.7 1.5 %collective-permute-start.14 = (bf16[4,6144]{1,0:T(4,128)(2,1)S(1)}, bf16[4,6144]{1,0:T(4,128)(2,1)S(1)}, u32[]{:S(2)}, u32[]{:S(2)}) collective-permute-start(bf16[4,6144]{1,0:T(4,128)(2,1)S(1)} %get-tuple-element.36), channel_id=1, source_target_pairs={{0,2},{1,3},{2,0},{3,1},{4,6},{5,7},{6,4},{7,5},{8,10},{9,11},{10,... | collective-permute-start | bytes 147464 | tf_op jit(solution)/shard_map/ppermute | solution.py:277
  33.2 1.1 %collective-permute-start.9 = (bf16[4,6144]{1,0:T(4,128)(2,1)S(1)}, bf16[4,6144]{1,0:T(4,128)(2,1)S(1)}, u32[]{:S(2)}, u32[]{:S(2)}) collective-permute-start(bf16[4,6144]{1,0:T(4,128)(2,1)S(1)} %get-tuple-element.28), channel_id=1, source_target_pairs={{0,6},{1,7},{2,4},{3,5},{4,2},{5,3},{6,0},{7,1},{8,14},{9,15},{10,... | collective-permute-start | bytes 147464 | tf_op jit(solution)/shard_map/ppermute | solution.py:277
  34.3 0.8 %collective-permute-start.10 = (bf16[4,6144]{1,0:T(4,128)(2,1)S(1)}, bf16[4,6144]{1,0:T(4,128)(2,1)S(1)}, u32[]{:S(2)}, u32[]{:S(2)}) collective-permute-start(bf16[4,6144]{1,0:T(4,128)(2,1)S(1)} %get-tuple-element.29), channel_id=1, source_target_pairs={{0,4},{1,5},{2,6},{3,7},{4,0},{5,1},{6,2},{7,3},{8,12},{9,13},{10,... | collective-permute-start | bytes 147464 | tf_op jit(solution)/shard_map/ppermute | solution.py:277
  35.2 1.5 %collective-permute-start.11 = (bf16[4,6144]{1,0:T(4,128)(2,1)S(1)}, bf16[4,6144]{1,0:T(4,128)(2,1)S(1)}, u32[]{:S(2)}, u32[]{:S(2)}) collective-permute-start(bf16[4,6144]{1,0:T(4,128)(2,1)S(1)} %get-tuple-element.30), channel_id=1, source_target_pairs={{0,2},{1,3},{2,0},{3,1},{4,6},{5,7},{6,4},{7,5},{8,10},{9,11},{10,... | collective-permute-start | bytes 147464 | tf_op jit(solution)/shard_map/ppermute | solution.py:277
  36.7 2.4 %collective-permute-start.15 = (bf16[4,6144]{1,0:T(4,128)(2,1)S(1)}, bf16[4,6144]{1,0:T(4,128)(2,1)S(1)}, u32[]{:S(2)}, u32[]{:S(2)}) collective-permute-start(bf16[4,6144]{1,0:T(4,128)(2,1)S(1)} %shard_map.115), channel_id=1, source_target_pairs={{0,8},{1,9},{2,10},{3,11},{4,12},{5,13},{6,14},{7,15},{8,0},{9,1},... | collective-permute-start | bytes 147464 | tf_op jit(solution)/shard_map/ppermute | solution.py:277
  39.3 0.5 %shard_map.114 = (f32[8,6144]{1,0:T(8,128)S(1)}, f32[8,8]{1,0:T(8,128)S(1)}) custom-call(f32[8,6144]{1,0:T(8,128)S(1)} %get-tuple-element.21.residual_ref, bf16[8,6144]{1,0:T(8,128)(2,1)S(1)} %get-tuple-element.22.normed_ref, bf16[16,6144]{1,0:T(8,128)(2,1)S(1)} %bitcast.13, s32[4,8]{1,0:T(4,128)S(1)} %bitcast.15, f32[4,6144]{1,0:T(4,128)S(1)} %get-tuple-element.27.near_ref, ...), custom_call_target="tpu_custom_call" | custom-call | tf_op jit(solution)/shard_map/pallas_call | solution.py:360
  39.8 2.0 %collective-permute-done.15.far_ref = bf16[4,6144]{1,0:T(4,128)(2,1)S(1)} collective-permute-done((bf16[4,6144]{1,0:T(4,128)(2,1)S(1)}, bf16[4,6144]{1,0:T(4,128)(2,1)S(1)}, u32[]{:S(2)}, u32[]{:S(2)}) %collective-permute-start.15) | collective-permute-done | bytes 49184 | tf_op jit(solution)/shard_map/ppermute | solution.py:277
  41.8 0.8 %shard_map.116 = bf16[8,6144]{1,0:T(8,128)(2,1)} custom-call(f32[8,6144]{1,0:T(8,128)S(1)} %get-tuple-element.31.base_ref, f32[8,8]{1,0:T(8,128)S(1)} %get-tuple-element.32.mix_ref, bf16[4,6144]{1,0:T(4,128)(2,1)S(1)} %collective-permute-done.15.far_ref), custom_call_target="tpu_custom_call" | custom-call | tf_op jit(solution)/shard_map/pallas_call | solution.py:367
  (26 shorter events, 0.6 us)
Async XLA Ops:
  0.0 18.4 %copy-start.1 = (bf16[1,6144,1344]{1,2,0:T(8,128)(2,1)S(1)}, bf16[1,6144,1344]{1,2,0:T(8,128)(2,1)}, u32[]{:S(2)}) copy-start(bf16[1,6144,1344]{1,2,0:T(8,128)(2,1)} %param.19) | copy-start | bytes 49545220
  0.0 18.4 %copy-start.2 = (bf16[1,6144,1344]{1,2,0:T(8,128)(2,1)S(1)}, bf16[1,6144,1344]{1,2,0:T(8,128)(2,1)}, u32[]{:S(2)}) copy-start(bf16[1,6144,1344]{1,2,0:T(8,128)(2,1)} %param.20) | copy-start | bytes 49545220
  2.5 6.7 %collective-permute-start = (bf16[4,6144]{1,0:T(4,128)(2,1)S(1)}, bf16[4,6144]{1,0:T(4,128)(2,1)S(1)}, u32[]{:S(2)}, u32[]{:S(2)}) collective-permute-start(bf16[4,6144]{1,0:T(4,128)(2,1)S(1)} %get-tuple-element.24), channel_id=1, source_target_pairs={{0,8},{1,9},{2,10},{3,11},{4,12},{5,13},{6,14},{7,15},{8,0},{9,1},... | collective-permute-start | bytes 147464 | tf_op jit(solution)/shard_map/ppermute | solution.py:277
  9.2 5.7 %collective-permute-start.3 = (bf16[8,6144]{1,0:T(8,128)(2,1)S(1)}, bf16[8,6144]{1,0:T(8,128)(2,1)S(1)}, u32[]{:S(2)}, u32[]{:S(2)}) collective-permute-start(bf16[8,6144]{1,0:T(8,128)(2,1)S(1)} %shard_map.110.refs_0_), channel_id=1, source_target_pairs={{0,6},{1,7},{2,4},{3,5},{4,2},{5,3},{6,0},{7,1},{8,14},{9,15},{10,... | collective-permute-start | bytes 294920 | tf_op jit(solution)/shard_map/ppermute | solution.py:277
  11.6 4.6 %collective-permute-start.2 = (bf16[8,6144]{1,0:T(8,128)(2,1)S(1)}, bf16[8,6144]{1,0:T(8,128)(2,1)S(1)}, u32[]{:S(2)}, u32[]{:S(2)}) collective-permute-start(bf16[8,6144]{1,0:T(8,128)(2,1)S(1)} %shard_map.110.refs_0_), channel_id=1, source_target_pairs={{0,4},{1,5},{2,6},{3,7},{4,0},{5,1},{6,2},{7,3},{8,12},{9,13},{10,... | collective-permute-start | bytes 294920 | tf_op jit(solution)/shard_map/ppermute | solution.py:277
  12.5 4.6 %collective-permute-start.1 = (bf16[8,6144]{1,0:T(8,128)(2,1)S(1)}, bf16[8,6144]{1,0:T(8,128)(2,1)S(1)}, u32[]{:S(2)}, u32[]{:S(2)}) collective-permute-start(bf16[8,6144]{1,0:T(8,128)(2,1)S(1)} %shard_map.110.refs_0_), channel_id=1, source_target_pairs={{0,2},{1,3},{2,0},{3,1},{4,6},{5,7},{6,4},{7,5},{8,10},{9,11},{10,... | collective-permute-start | bytes 294920 | tf_op jit(solution)/shard_map/ppermute | solution.py:277
  12.8 4.3 %collective-permute-start.4 = (bf16[8,6144]{1,0:T(8,128)(2,1)S(1)}, bf16[8,6144]{1,0:T(8,128)(2,1)S(1)}, u32[]{:S(2)}, u32[]{:S(2)}) collective-permute-start(bf16[8,6144]{1,0:T(8,128)(2,1)S(1)} %shard_map.110.refs_0_), channel_id=1, source_target_pairs={{0,1},{1,0},{2,3},{3,2},{4,5},{5,4},{6,7},{7,6},{8,9},{9,8},{10,11... | collective-permute-start | bytes 294920 | tf_op jit(solution)/shard_map/ppermute | solution.py:277
  14.9 2.2 %collective-permute-start.7 = (bf16[8,6144]{1,0:T(8,128)(2,1)S(1)}, bf16[8,6144]{1,0:T(8,128)(2,1)S(1)}, u32[]{:S(2)}, u32[]{:S(2)}) collective-permute-start(bf16[8,6144]{1,0:T(8,128)(2,1)S(1)} %collective-permute-done.3.refs_3_), channel_id=1, source_target_pairs={{0,1},{1,0},{2,3},{3,2},{4,5},{5,4},{6,7},{7,6},{8,9},{9,8},{10,11... | collective-permute-start | bytes 294920 | tf_op jit(solution)/shard_map/ppermute | solution.py:277
  16.3 1.3 %collective-permute-start.6 = (bf16[8,6144]{1,0:T(8,128)(2,1)S(1)}, bf16[8,6144]{1,0:T(8,128)(2,1)S(1)}, u32[]{:S(2)}, u32[]{:S(2)}) collective-permute-start(bf16[8,6144]{1,0:T(8,128)(2,1)S(1)} %collective-permute-done.2.refs_2_), channel_id=1, source_target_pairs={{0,1},{1,0},{2,3},{3,2},{4,5},{5,4},{6,7},{7,6},{8,9},{9,8},{10,11... | collective-permute-start | bytes 294920 | tf_op jit(solution)/shard_map/ppermute | solution.py:277
  17.1 1.3 %collective-permute-start.5 = (bf16[8,6144]{1,0:T(8,128)(2,1)S(1)}, bf16[8,6144]{1,0:T(8,128)(2,1)S(1)}, u32[]{:S(2)}, u32[]{:S(2)}) collective-permute-start(bf16[8,6144]{1,0:T(8,128)(2,1)S(1)} %collective-permute-done.1.refs_1_), channel_id=1, source_target_pairs={{0,1},{1,0},{2,3},{3,2},{4,5},{5,4},{6,7},{7,6},{8,9},{9,8},{10,11... | collective-permute-start | bytes 294920 | tf_op jit(solution)/shard_map/ppermute | solution.py:277
  18.4 6.7 %copy-start = (bf16[1,1344,6144]{2,1,0:T(8,128)(2,1)S(1)}, bf16[1,1344,6144]{2,1,0:T(8,128)(2,1)}, u32[]{:S(2)}) copy-start(bf16[1,1344,6144]{2,1,0:T(8,128)(2,1)} %param.21) | copy-start | bytes 49545220
  25.1 14.2 %copy-start.3 = (bf16[6144,16]{0,1:T(8,128)(2,1)S(1)}, bf16[6144,16]{0,1:T(8,128)(2,1)}, u32[]{:S(2)}) copy-start(bf16[6144,16]{0,1:T(8,128)(2,1)} %param.18) | copy-start | bytes 589828
  25.1 14.1 %copy-start.4 = (s32[8,4]{0,1:T(4,128)S(1)}, s32[8,4]{0,1:T(4,128)}, u32[]{:S(2)}) copy-start(s32[8,4]{0,1:T(4,128)} %param.16) | copy-start | bytes 388
  27.8 1.8 %collective-permute-start.8 = (bf16[32,6144]{1,0:T(8,128)(2,1)S(1)}, bf16[32,6144]{1,0:T(8,128)(2,1)S(1)}, u32[]{:S(2)}, u32[]{:S(2)}) collective-permute-start(bf16[32,6144]{1,0:T(8,128)(2,1)S(1)} %get-tuple-element.26), channel_id=1, source_target_pairs={{0,1},{1,0},{2,3},{3,2},{4,5},{5,4},{6,7},{7,6},{8,9},{9,8},{10,11... | collective-permute-start | bytes 1179656 | tf_op jit(solution)/shard_map/ppermute | solution.py:277
  29.6 5.5 %collective-permute-start.12 = (bf16[4,6144]{1,0:T(4,128)(2,1)S(1)}, bf16[4,6144]{1,0:T(4,128)(2,1)S(1)}, u32[]{:S(2)}, u32[]{:S(2)}) collective-permute-start(bf16[4,6144]{1,0:T(4,128)(2,1)S(1)} %get-tuple-element.34), channel_id=1, source_target_pairs={{0,6},{1,7},{2,4},{3,5},{4,2},{5,3},{6,0},{7,1},{8,14},{9,15},{10,... | collective-permute-start | bytes 147464 | tf_op jit(solution)/shard_map/ppermute | solution.py:277
  30.8 5.9 %collective-permute-start.13 = (bf16[4,6144]{1,0:T(4,128)(2,1)S(1)}, bf16[4,6144]{1,0:T(4,128)(2,1)S(1)}, u32[]{:S(2)}, u32[]{:S(2)}) collective-permute-start(bf16[4,6144]{1,0:T(4,128)(2,1)S(1)} %get-tuple-element.35), channel_id=1, source_target_pairs={{0,4},{1,5},{2,6},{3,7},{4,0},{5,1},{6,2},{7,3},{8,12},{9,13},{10,... | collective-permute-start | bytes 147464 | tf_op jit(solution)/shard_map/ppermute | solution.py:277
  31.7 5.0 %collective-permute-start.14 = (bf16[4,6144]{1,0:T(4,128)(2,1)S(1)}, bf16[4,6144]{1,0:T(4,128)(2,1)S(1)}, u32[]{:S(2)}, u32[]{:S(2)}) collective-permute-start(bf16[4,6144]{1,0:T(4,128)(2,1)S(1)} %get-tuple-element.36), channel_id=1, source_target_pairs={{0,2},{1,3},{2,0},{3,1},{4,6},{5,7},{6,4},{7,5},{8,10},{9,11},{10,... | collective-permute-start | bytes 147464 | tf_op jit(solution)/shard_map/ppermute | solution.py:277
  33.2 5.9 %collective-permute-start.9 = (bf16[4,6144]{1,0:T(4,128)(2,1)S(1)}, bf16[4,6144]{1,0:T(4,128)(2,1)S(1)}, u32[]{:S(2)}, u32[]{:S(2)}) collective-permute-start(bf16[4,6144]{1,0:T(4,128)(2,1)S(1)} %get-tuple-element.28), channel_id=1, source_target_pairs={{0,6},{1,7},{2,4},{3,5},{4,2},{5,3},{6,0},{7,1},{8,14},{9,15},{10,... | collective-permute-start | bytes 147464 | tf_op jit(solution)/shard_map/ppermute | solution.py:277
  34.3 4.8 %collective-permute-start.10 = (bf16[4,6144]{1,0:T(4,128)(2,1)S(1)}, bf16[4,6144]{1,0:T(4,128)(2,1)S(1)}, u32[]{:S(2)}, u32[]{:S(2)}) collective-permute-start(bf16[4,6144]{1,0:T(4,128)(2,1)S(1)} %get-tuple-element.29), channel_id=1, source_target_pairs={{0,4},{1,5},{2,6},{3,7},{4,0},{5,1},{6,2},{7,3},{8,12},{9,13},{10,... | collective-permute-start | bytes 147464 | tf_op jit(solution)/shard_map/ppermute | solution.py:277
  35.2 4.1 %collective-permute-start.11 = (bf16[4,6144]{1,0:T(4,128)(2,1)S(1)}, bf16[4,6144]{1,0:T(4,128)(2,1)S(1)}, u32[]{:S(2)}, u32[]{:S(2)}) collective-permute-start(bf16[4,6144]{1,0:T(4,128)(2,1)S(1)} %get-tuple-element.30), channel_id=1, source_target_pairs={{0,2},{1,3},{2,0},{3,1},{4,6},{5,7},{6,4},{7,5},{8,10},{9,11},{10,... | collective-permute-start | bytes 147464 | tf_op jit(solution)/shard_map/ppermute | solution.py:277
  36.7 5.1 %collective-permute-start.15 = (bf16[4,6144]{1,0:T(4,128)(2,1)S(1)}, bf16[4,6144]{1,0:T(4,128)(2,1)S(1)}, u32[]{:S(2)}, u32[]{:S(2)}) collective-permute-start(bf16[4,6144]{1,0:T(4,128)(2,1)S(1)} %shard_map.115), channel_id=1, source_target_pairs={{0,8},{1,9},{2,10},{3,11},{4,12},{5,13},{6,14},{7,15},{8,0},{9,1},... | collective-permute-start | bytes 147464 | tf_op jit(solution)/shard_map/ppermute | solution.py:277

commit v8 on v7

--- a/solution.py
+++ b/solution.py
@@ -155,17 +155,19 @@
     out_ref[...] = jnp.concatenate([near_ref[...], arrived_ref[...]], axis=0)
 
 
-def project(inner_ref, down_ref, keep_ref, send_ref, start):
+def project(inner_ref, down_ref, keep_ref, *sends):
     rows = inner_ref[...]
     half = rows.shape[0] // 2
+    each = half // len(sends)
     doubled = jnp.concatenate([rows, rows], axis=0)
     width = keep_ref.shape[1]
     part = 1024 if width % 1024 == 0 else width
     for i in range(width // part):
         at = slice(i * part, (i + 1) * part)
-        out = jnp.dot(doubled, down_ref[:, start + i * part:start + (i + 1) * part], preferred_element_type=F32)
+        out = jnp.dot(doubled, down_ref[:, at], preferred_element_type=F32)
         keep_ref[:, at] = out[:half]
-        send_ref[:, at] = out[half:2 * half].astype(BF16)
+        for j, send in enumerate(sends):
+            send[:, at] = out[half + j * each:half + (j + 1) * each].astype(BF16)
 
 
 def expert_kernel(chips, chunk, depth, *refs):
@@ -186,17 +188,15 @@
         inner_ref[:, at] = (gate_part / (1.0 + jnp.exp(-gate_part)) * up_part.T).astype(BF16)
 
 
-def rest_kernel(start, inner_ref, down_ref, keep_ref, send_ref):
-    project(inner_ref, down_ref, keep_ref, send_ref, start)
-
-
-def core_sum_kernel(keep_ref, recv_ref, near_ref, far_ref, *rest):
-    capacity = near_ref.shape[0]
-    start = keep_ref.shape[1]
-    for keep, recv, at in ((keep_ref, recv_ref, slice(0, start)),):
-        total = keep[...] + recv[...].astype(F32)
-        for i, out in enumerate((near_ref, far_ref) + rest):
-            out[:, at] = total[i * capacity:(i + 1) * capacity].astype(out.dtype)
+def core_sum_kernel(split, keep_ref, *refs):
+    received, outs = refs[:split], refs[split:]
+    capacity = outs[0].shape[0]
+    each = received[0].shape[0]
+    for j, recv in enumerate(received):
+        total = keep_ref[j * each:(j + 1) * each] + recv[...].astype(F32)
+        for i in range(each // capacity):
+            out = outs[j * (each // capacity) + i]
+            out[...] = total[i * capacity:(i + 1) * capacity].astype(out.dtype)
 
 
 def far_sum_kernel(far_ref, *refs):
@@ -317,7 +317,6 @@
     chunk = 336 if hidden % 336 == 0 else hidden
     depth = 256 if width % 256 == 0 else width
     rows = chips * count
-    start = 2 * width // 3 // 1024 * 1024
     inner = pl.pallas_call(
         functools.partial(expert_kernel, chips, chunk, depth),
         out_shape=like(2 * rows, hidden),
@@ -327,22 +326,20 @@
         compiler_params=params(2 if tight else 24),
     )(*mine, *beside, *weights[:2])
 
-    def down(start, columns):
-        return pl.pallas_call(
-            functools.partial(rest_kernel, start),
-            out_shape=(like(rows, columns, dtype=F32), like(rows, columns)),
-            in_specs=[whole()] * 2,
-            out_specs=(whole(),) * 2,
-            compiler_params=params(2 if tight else 24),
-        )(inner, weights[2])
-
-    keep, send = down(0, width)
-    recv = exchange(send, 1)
-    in_vmem = [pltpu.with_memory_space_constraint(x, pltpu.VMEM) for x in (keep, recv)]
+    split = 2
+    keep, *sends = pl.pallas_call(
+        project,
+        out_shape=(like(rows, width, dtype=F32),) + (like(rows // split, width),) * split,
+        in_specs=[whole()] * 2,
+        out_specs=(whole(),) * (1 + split),
+        compiler_params=params(2 if tight else 24),
+    )(inner, weights[2])
+    received = [exchange(send, 1) for send in sends]
+    in_vmem = [pltpu.with_memory_space_constraint(x, pltpu.VMEM) for x in (keep, *received)]
     near_sum, far_sum, *rest = pl.pallas_call(
-        core_sum_kernel,
+        functools.partial(core_sum_kernel, split),
         out_shape=(like(capacity, width, dtype=F32),) * 2 + (like(capacity, width),) * (2 * chips - 2),
-        in_specs=[whole()] * 2,
+        in_specs=[whole()] * (1 + split),
         out_specs=(whole(),) * (2 * chips),
         compiler_params=params(2 if tight else 24),
     )(*in_vmem)

time: 42.8 us -> 42.8 us (level)
    ppermute x16 -> x17, waiting for transfers between devices: 11.9 us -> 11.5 us  [exchange(): return lax.ppermute(value, 'pool', [(i, i ^ bit) for i in range(devices)])]
    ppermute x16 -> x17, starting transfers between devices: 17.3 us -> 17.7 us  [exchange(): return lax.ppermute(value, 'pool', [(i, i ^ bit) for i in range(devices)])]
  transfers between devices with their start and end apart: 16 -> 17, of which waited for: 9 -> 10; matrix products, arithmetic and copies ran while one was open for 0% -> 0% of each run, Pallas kernels for 1% -> 1%
where the time goes in v8:
time: 42.8 us; the launch traced here: 42.6 us
  starting transfers between devices  17.7 us (41%)
  Pallas kernels  13.2 us (31%)
  waiting for transfers between devices  11.5 us (27%)
    ppermute x17, starting transfers between devices, exchange(): return lax.ppermute(value, 'pool', [(i, i ^ bit) for i in range(devices)])  17.7 us
    ppermute x17, waiting for transfers between devices, exchange(): return lax.ppermute(value, 'pool', [(i, i ^ bit) for i in range(devices)])  11.5 us
    pallas_call x1, Pallas kernels, body(): pl.pallas_call(functools.partial(expert_kernel, chips, chunk, depth), out...  6.66 us
    pallas_call x1, Pallas kernels, body(): pl.pallas_call(project, out_shape=(like(rows, width, dtype=F32),) + (like...  2.63 us
    pallas_call x1, Pallas kernels, body(): pl.pallas_call(functools.partial(front_kernel, half), out_shape=(like(req...  2.49 us
  transfers between devices with their start and end apart: 17, of which 10 were waited for; matrix products, arithmetic and copies ran while one was open for 0% of the time, Pallas kernels for 1%

profile of v8, /device:TPU:0, one launch (start us, length us, event | category | flops | bytes accessed | tf_op | source)
XLA Modules:
  0.0 42.6 jit_solution(1948923258905679458)
XLA Ops:
  0.0 2.5 %shard_map.109 = (f32[8,6144]{1,0:T(8,128)S(1)}, bf16[8,6144]{1,0:T(8,128)(2,1)S(1)}, bf16[4,6144]{1,0:T(4,128)(2,1)S(1)}, bf16[4,6144]{1,0:T(4,128)(2,1)S(1)}) custom-call(bf16[8,6144]{1,0:T(8,128)(2,1)} %hidden_hbm.1, bf16[8,6144]{1,0:T(8,128)(2,1)} %queries_hbm.1, bf16[128,2,1024]{2,1,0:T(2,128)(2,1)} %cached_hbm.1, bf16[8,2,1024]{2,1,0:T(2,128)(2,1)} %own_hbm.1, ...), custom_call_target="tpu_custom_call" | custom-call | flops 199999995904 | bytes 50000000 | tf_op jit(solution)/shard_map/pallas_call | solution.py:287
  2.5 4.1 %collective-permute-start = (bf16[4,6144]{1,0:T(4,128)(2,1)S(1)}, bf16[4,6144]{1,0:T(4,128)(2,1)S(1)}, u32[]{:S(2)}, u32[]{:S(2)}) collective-permute-start(bf16[4,6144]{1,0:T(4,128)(2,1)S(1)} %get-tuple-element.25), channel_id=1, source_target_pairs={{0,8},{1,9},{2,10},{3,11},{4,12},{5,13},{6,14},{7,15},{8,0},{9,1},... | collective-permute-start | bytes 147464 | tf_op jit(solution)/shard_map/ppermute | solution.py:277
  6.6 2.6 %collective-permute-done.arrived_ref = bf16[4,6144]{1,0:T(4,128)(2,1)S(1)} collective-permute-done((bf16[4,6144]{1,0:T(4,128)(2,1)S(1)}, bf16[4,6144]{1,0:T(4,128)(2,1)S(1)}, u32[]{:S(2)}, u32[]{:S(2)}) %collective-permute-start) | collective-permute-done | bytes 49184 | tf_op jit(solution)/shard_map/ppermute | solution.py:277
  9.2 2.4 %collective-permute-start.3 = (bf16[8,6144]{1,0:T(8,128)(2,1)S(1)}, bf16[8,6144]{1,0:T(8,128)(2,1)S(1)}, u32[]{:S(2)}, u32[]{:S(2)}) collective-permute-start(bf16[8,6144]{1,0:T(8,128)(2,1)S(1)} %shard_map.110.refs_0_), channel_id=1, source_target_pairs={{0,6},{1,7},{2,4},{3,5},{4,2},{5,3},{6,0},{7,1},{8,14},{9,15},{10,... | collective-permute-start | bytes 294920 | tf_op jit(solution)/shard_map/ppermute | solution.py:277
  11.6 0.9 %collective-permute-start.2 = (bf16[8,6144]{1,0:T(8,128)(2,1)S(1)}, bf16[8,6144]{1,0:T(8,128)(2,1)S(1)}, u32[]{:S(2)}, u32[]{:S(2)}) collective-permute-start(bf16[8,6144]{1,0:T(8,128)(2,1)S(1)} %shard_map.110.refs_0_), channel_id=1, source_target_pairs={{0,4},{1,5},{2,6},{3,7},{4,0},{5,1},{6,2},{7,3},{8,12},{9,13},{10,... | collective-permute-start | bytes 294920 | tf_op jit(solution)/shard_map/ppermute | solution.py:277
  12.8 2.1 %collective-permute-done.3.refs_3_ = bf16[8,6144]{1,0:T(8,128)(2,1)S(1)} collective-permute-done((bf16[8,6144]{1,0:T(8,128)(2,1)S(1)}, bf16[8,6144]{1,0:T(8,128)(2,1)S(1)}, u32[]{:S(2)}, u32[]{:S(2)}) %collective-permute-start.3) | collective-permute-done | bytes 98336 | tf_op jit(solution)/shard_map/ppermute | solution.py:277
  14.9 1.3 %collective-permute-done.2.refs_2_ = bf16[8,6144]{1,0:T(8,128)(2,1)S(1)} collective-permute-done((bf16[8,6144]{1,0:T(8,128)(2,1)S(1)}, bf16[8,6144]{1,0:T(8,128)(2,1)S(1)}, u32[]{:S(2)}, u32[]{:S(2)}) %collective-permute-start.2) | collective-permute-done | bytes 98336 | tf_op jit(solution)/shard_map/ppermute | solution.py:277
  16.3 0.9 %collective-permute-done.1.refs_1_ = bf16[8,6144]{1,0:T(8,128)(2,1)S(1)} collective-permute-done((bf16[8,6144]{1,0:T(8,128)(2,1)S(1)}, bf16[8,6144]{1,0:T(8,128)(2,1)S(1)}, u32[]{:S(2)}, u32[]{:S(2)}) %collective-permute-start.1) | collective-permute-done | bytes 98336 | tf_op jit(solution)/shard_map/ppermute | solution.py:277
  17.1 0.4 %collective-permute-done.6.refs_6_ = bf16[8,6144]{1,0:T(8,128)(2,1)S(1)} collective-permute-done((bf16[8,6144]{1,0:T(8,128)(2,1)S(1)}, bf16[8,6144]{1,0:T(8,128)(2,1)S(1)}, u32[]{:S(2)}, u32[]{:S(2)}) %collective-permute-start.6) | collective-permute-done | bytes 98336 | tf_op jit(solution)/shard_map/ppermute | solution.py:277
  17.6 0.9 %collective-permute-done.5.refs_5_ = bf16[8,6144]{1,0:T(8,128)(2,1)S(1)} collective-permute-done((bf16[8,6144]{1,0:T(8,128)(2,1)S(1)}, bf16[8,6144]{1,0:T(8,128)(2,1)S(1)}, u32[]{:S(2)}, u32[]{:S(2)}) %collective-permute-start.5) | collective-permute-done | bytes 98336 | tf_op jit(solution)/shard_map/ppermute | solution.py:277
  18.4 6.7 %shard_map.111.inner_ref = bf16[64,1344]{1,0:T(8,128)(2,1)S(1)} custom-call(bf16[8,6144]{1,0:T(8,128)(2,1)S(1)} %shard_map.110.refs_0_, bf16[8,6144]{1,0:T(8,128)(2,1)S(1)} %collective-permute-done.1.refs_1_, bf16[8,6144]{1,0:T(8,128)(2,1)S(1)} %collective-permute-done.2.refs_2_, bf16[8,6144]{1,0:T(8,128)(2,1)S(1)} %collective-permute-done.3.refs_3_, ...), custom_call_target="tpu_custom_call" | custom-call | tf_op jit(solution)/shard_map/pallas_call | solution.py:320
  25.1 2.6 %shard_map.112 = (f32[32,6144]{1,0:T(8,128)S(1)}, bf16[16,6144]{1,0:T(8,128)(2,1)S(1)}, bf16[16,6144]{1,0:T(8,128)(2,1)S(1)}) custom-call(bf16[64,1344]{1,0:T(8,128)(2,1)S(1)} %shard_map.111.inner_ref, bf16[1344,6144]{1,0:T(8,128)(2,1)S(1)} %bitcast.10), custom_call_target="tpu_custom_call" | custom-call | tf_op jit(solution)/shard_map/pallas_call | solution.py:330
  28.0 0.4 collective-permute-start.9
  28.3 0.9 %collective-permute-done.8.refs_0_ = bf16[16,6144]{1,0:T(8,128)(2,1)S(1)} collective-permute-done((bf16[16,6144]{1,0:T(8,128)(2,1)S(1)}, bf16[16,6144]{1,0:T(8,128)(2,1)S(1)}, u32[]{:S(2)}, u32[]{:S(2)}) %collective-permute-start.8) | collective-permute-done | bytes 196640 | tf_op jit(solution)/shard_map/ppermute | solution.py:277
  29.6 1.2 %collective-permute-start.13 = (bf16[4,6144]{1,0:T(4,128)(2,1)S(1)}, bf16[4,6144]{1,0:T(4,128)(2,1)S(1)}, u32[]{:S(2)}, u32[]{:S(2)}) collective-permute-start(bf16[4,6144]{1,0:T(4,128)(2,1)S(1)} %get-tuple-element.36), channel_id=1, source_target_pairs={{0,6},{1,7},{2,4},{3,5},{4,2},{5,3},{6,0},{7,1},{8,14},{9,15},{10,... | collective-permute-start | bytes 147464 | tf_op jit(solution)/shard_map/ppermute | solution.py:277
  30.8 0.8 %collective-permute-start.14 = (bf16[4,6144]{1,0:T(4,128)(2,1)S(1)}, bf16[4,6144]{1,0:T(4,128)(2,1)S(1)}, u32[]{:S(2)}, u32[]{:S(2)}) collective-permute-start(bf16[4,6144]{1,0:T(4,128)(2,1)S(1)} %get-tuple-element.37), channel_id=1, source_target_pairs={{0,4},{1,5},{2,6},{3,7},{4,0},{5,1},{6,2},{7,3},{8,12},{9,13},{10,... | collective-permute-start | bytes 147464 | tf_op jit(solution)/shard_map/ppermute | solution.py:277
  31.7 1.5 %collective-permute-start.15 = (bf16[4,6144]{1,0:T(4,128)(2,1)S(1)}, bf16[4,6144]{1,0:T(4,128)(2,1)S(1)}, u32[]{:S(2)}, u32[]{:S(2)}) collective-permute-start(bf16[4,6144]{1,0:T(4,128)(2,1)S(1)} %get-tuple-element.38), channel_id=1, source_target_pairs={{0,2},{1,3},{2,0},{3,1},{4,6},{5,7},{6,4},{7,5},{8,10},{9,11},{10,... | collective-permute-start | bytes 147464 | tf_op jit(solution)/shard_map/ppermute | solution.py:277
  33.2 1.1 %collective-permute-start.10 = (bf16[4,6144]{1,0:T(4,128)(2,1)S(1)}, bf16[4,6144]{1,0:T(4,128)(2,1)S(1)}, u32[]{:S(2)}, u32[]{:S(2)}) collective-permute-start(bf16[4,6144]{1,0:T(4,128)(2,1)S(1)} %get-tuple-element.30), channel_id=1, source_target_pairs={{0,6},{1,7},{2,4},{3,5},{4,2},{5,3},{6,0},{7,1},{8,14},{9,15},{10,... | collective-permute-start | bytes 147464 | tf_op jit(solution)/shard_map/ppermute | solution.py:277
  34.3 0.8 %collective-permute-start.11 = (bf16[4,6144]{1,0:T(4,128)(2,1)S(1)}, bf16[4,6144]{1,0:T(4,128)(2,1)S(1)}, u32[]{:S(2)}, u32[]{:S(2)}) collective-permute-start(bf16[4,6144]{1,0:T(4,128)(2,1)S(1)} %get-tuple-element.31), channel_id=1, source_target_pairs={{0,4},{1,5},{2,6},{3,7},{4,0},{5,1},{6,2},{7,3},{8,12},{9,13},{10,... | collective-permute-start | bytes 147464 | tf_op jit(solution)/shard_map/ppermute | solution.py:277
  35.2 1.5 %collective-permute-start.12 = (bf16[4,6144]{1,0:T(4,128)(2,1)S(1)}, bf16[4,6144]{1,0:T(4,128)(2,1)S(1)}, u32[]{:S(2)}, u32[]{:S(2)}) collective-permute-start(bf16[4,6144]{1,0:T(4,128)(2,1)S(1)} %get-tuple-element.32), channel_id=1, source_target_pairs={{0,2},{1,3},{2,0},{3,1},{4,6},{5,7},{6,4},{7,5},{8,10},{9,11},{10,... | collective-permute-start | bytes 147464 | tf_op jit(solution)/shard_map/ppermute | solution.py:277
  36.7 2.4 %collective-permute-start.16 = (bf16[4,6144]{1,0:T(4,128)(2,1)S(1)}, bf16[4,6144]{1,0:T(4,128)(2,1)S(1)}, u32[]{:S(2)}, u32[]{:S(2)}) collective-permute-start(bf16[4,6144]{1,0:T(4,128)(2,1)S(1)} %shard_map.115), channel_id=1, source_target_pairs={{0,8},{1,9},{2,10},{3,11},{4,12},{5,13},{6,14},{7,15},{8,0},{9,1},... | collective-permute-start | bytes 147464 | tf_op jit(solution)/shard_map/ppermute | solution.py:277
  39.3 0.5 %shard_map.114 = (f32[8,6144]{1,0:T(8,128)S(1)}, f32[8,8]{1,0:T(8,128)S(1)}) custom-call(f32[8,6144]{1,0:T(8,128)S(1)} %get-tuple-element.22.residual_ref, bf16[8,6144]{1,0:T(8,128)(2,1)S(1)} %get-tuple-element.23.normed_ref, bf16[16,6144]{1,0:T(8,128)(2,1)S(1)} %bitcast.13, s32[4,8]{1,0:T(4,128)S(1)} %bitcast.15, f32[4,6144]{1,0:T(4,128)S(1)} %get-tuple-element.29.near_ref, ...), custom_call_target="tpu_custom_call" | custom-call | tf_op jit(solution)/shard_map/pallas_call | solution.py:357
  39.8 2.0 %collective-permute-done.16.far_ref = bf16[4,6144]{1,0:T(4,128)(2,1)S(1)} collective-permute-done((bf16[4,6144]{1,0:T(4,128)(2,1)S(1)}, bf16[4,6144]{1,0:T(4,128)(2,1)S(1)}, u32[]{:S(2)}, u32[]{:S(2)}) %collective-permute-start.16) | collective-permute-done | bytes 49184 | tf_op jit(solution)/shard_map/ppermute | solution.py:277
  41.8 0.8 %shard_map.116 = bf16[8,6144]{1,0:T(8,128)(2,1)} custom-call(f32[8,6144]{1,0:T(8,128)S(1)} %get-tuple-element.33.base_ref, f32[8,8]{1,0:T(8,128)S(1)} %get-tuple-element.34.mix_ref, bf16[4,6144]{1,0:T(4,128)(2,1)S(1)} %collective-permute-done.16.far_ref), custom_call_target="tpu_custom_call" | custom-call | tf_op jit(solution)/shard_map/pallas_call | solution.py:364
  (28 shorter events, 1.1 us)
Async XLA Ops:
  0.0 18.4 %copy-start.1 = (bf16[1,6144,1344]{1,2,0:T(8,128)(2,1)S(1)}, bf16[1,6144,1344]{1,2,0:T(8,128)(2,1)}, u32[]{:S(2)}) copy-start(bf16[1,6144,1344]{1,2,0:T(8,128)(2,1)} %param.19) | copy-start | bytes 49545220
  0.0 18.4 %copy-start.2 = (bf16[1,6144,1344]{1,2,0:T(8,128)(2,1)S(1)}, bf16[1,6144,1344]{1,2,0:T(8,128)(2,1)}, u32[]{:S(2)}) copy-start(bf16[1,6144,1344]{1,2,0:T(8,128)(2,1)} %param.20) | copy-start | bytes 49545220
  2.5 6.7 %collective-permute-start = (bf16[4,6144]{1,0:T(4,128)(2,1)S(1)}, bf16[4,6144]{1,0:T(4,128)(2,1)S(1)}, u32[]{:S(2)}, u32[]{:S(2)}) collective-permute-start(bf16[4,6144]{1,0:T(4,128)(2,1)S(1)} %get-tuple-element.25), channel_id=1, source_target_pairs={{0,8},{1,9},{2,10},{3,11},{4,12},{5,13},{6,14},{7,15},{8,0},{9,1},... | collective-permute-start | bytes 147464 | tf_op jit(solution)/shard_map/ppermute | solution.py:277
  9.2 5.7 %collective-permute-start.3 = (bf16[8,6144]{1,0:T(8,128)(2,1)S(1)}, bf16[8,6144]{1,0:T(8,128)(2,1)S(1)}, u32[]{:S(2)}, u32[]{:S(2)}) collective-permute-start(bf16[8,6144]{1,0:T(8,128)(2,1)S(1)} %shard_map.110.refs_0_), channel_id=1, source_target_pairs={{0,6},{1,7},{2,4},{3,5},{4,2},{5,3},{6,0},{7,1},{8,14},{9,15},{10,... | collective-permute-start | bytes 294920 | tf_op jit(solution)/shard_map/ppermute | solution.py:277
  11.6 4.6 %collective-permute-start.2 = (bf16[8,6144]{1,0:T(8,128)(2,1)S(1)}, bf16[8,6144]{1,0:T(8,128)(2,1)S(1)}, u32[]{:S(2)}, u32[]{:S(2)}) collective-permute-start(bf16[8,6144]{1,0:T(8,128)(2,1)S(1)} %shard_map.110.refs_0_), channel_id=1, source_target_pairs={{0,4},{1,5},{2,6},{3,7},{4,0},{5,1},{6,2},{7,3},{8,12},{9,13},{10,... | collective-permute-start | bytes 294920 | tf_op jit(solution)/shard_map/ppermute | solution.py:277
  12.5 4.6 %collective-permute-start.1 = (bf16[8,6144]{1,0:T(8,128)(2,1)S(1)}, bf16[8,6144]{1,0:T(8,128)(2,1)S(1)}, u32[]{:S(2)}, u32[]{:S(2)}) collective-permute-start(bf16[8,6144]{1,0:T(8,128)(2,1)S(1)} %shard_map.110.refs_0_), channel_id=1, source_target_pairs={{0,2},{1,3},{2,0},{3,1},{4,6},{5,7},{6,4},{7,5},{8,10},{9,11},{10,... | collective-permute-start | bytes 294920 | tf_op jit(solution)/shard_map/ppermute | solution.py:277
  12.8 4.3 %collective-permute-start.4 = (bf16[8,6144]{1,0:T(8,128)(2,1)S(1)}, bf16[8,6144]{1,0:T(8,128)(2,1)S(1)}, u32[]{:S(2)}, u32[]{:S(2)}) collective-permute-start(bf16[8,6144]{1,0:T(8,128)(2,1)S(1)} %shard_map.110.refs_0_), channel_id=1, source_target_pairs={{0,1},{1,0},{2,3},{3,2},{4,5},{5,4},{6,7},{7,6},{8,9},{9,8},{10,11... | collective-permute-start | bytes 294920 | tf_op jit(solution)/shard_map/ppermute | solution.py:277
  14.9 2.2 %collective-permute-start.7 = (bf16[8,6144]{1,0:T(8,128)(2,1)S(1)}, bf16[8,6144]{1,0:T(8,128)(2,1)S(1)}, u32[]{:S(2)}, u32[]{:S(2)}) collective-permute-start(bf16[8,6144]{1,0:T(8,128)(2,1)S(1)} %collective-permute-done.3.refs_3_), channel_id=1, source_target_pairs={{0,1},{1,0},{2,3},{3,2},{4,5},{5,4},{6,7},{7,6},{8,9},{9,8},{10,11... | collective-permute-start | bytes 294920 | tf_op jit(solution)/shard_map/ppermute | solution.py:277
  16.3 1.3 %collective-permute-start.6 = (bf16[8,6144]{1,0:T(8,128)(2,1)S(1)}, bf16[8,6144]{1,0:T(8,128)(2,1)S(1)}, u32[]{:S(2)}, u32[]{:S(2)}) collective-permute-start(bf16[8,6144]{1,0:T(8,128)(2,1)S(1)} %collective-permute-done.2.refs_2_), channel_id=1, source_target_pairs={{0,1},{1,0},{2,3},{3,2},{4,5},{5,4},{6,7},{7,6},{8,9},{9,8},{10,11... | collective-permute-start | bytes 294920 | tf_op jit(solution)/shard_map/ppermute | solution.py:277
  17.1 1.3 %collective-permute-start.5 = (bf16[8,6144]{1,0:T(8,128)(2,1)S(1)}, bf16[8,6144]{1,0:T(8,128)(2,1)S(1)}, u32[]{:S(2)}, u32[]{:S(2)}) collective-permute-start(bf16[8,6144]{1,0:T(8,128)(2,1)S(1)} %collective-permute-done.1.refs_1_), channel_id=1, source_target_pairs={{0,1},{1,0},{2,3},{3,2},{4,5},{5,4},{6,7},{7,6},{8,9},{9,8},{10,11... | collective-permute-start | bytes 294920 | tf_op jit(solution)/shard_map/ppermute | solution.py:277
  18.4 6.7 %copy-start = (bf16[1,1344,6144]{2,1,0:T(8,128)(2,1)S(1)}, bf16[1,1344,6144]{2,1,0:T(8,128)(2,1)}, u32[]{:S(2)}) copy-start(bf16[1,1344,6144]{2,1,0:T(8,128)(2,1)} %param.21) | copy-start | bytes 49545220
  25.1 14.2 %copy-start.3 = (bf16[6144,16]{0,1:T(8,128)(2,1)S(1)}, bf16[6144,16]{0,1:T(8,128)(2,1)}, u32[]{:S(2)}) copy-start(bf16[6144,16]{0,1:T(8,128)(2,1)} %param.18) | copy-start | bytes 589828
  25.1 14.1 %copy-start.4 = (s32[8,4]{0,1:T(4,128)S(1)}, s32[8,4]{0,1:T(4,128)}, u32[]{:S(2)}) copy-start(s32[8,4]{0,1:T(4,128)} %param.16) | copy-start | bytes 388
  27.8 1.5 %collective-permute-start.8 = (bf16[16,6144]{1,0:T(8,128)(2,1)S(1)}, bf16[16,6144]{1,0:T(8,128)(2,1)S(1)}, u32[]{:S(2)}, u32[]{:S(2)}) collective-permute-start(bf16[16,6144]{1,0:T(8,128)(2,1)S(1)} %get-tuple-element.27), channel_id=1, source_target_pairs={{0,1},{1,0},{2,3},{3,2},{4,5},{5,4},{6,7},{7,6},{8,9},{9,8},{10,11... | collective-permute-start | bytes 589832 | tf_op jit(solution)/shard_map/ppermute | solution.py:277
  28.0 1.6 %collective-permute-start.9 = (bf16[16,6144]{1,0:T(8,128)(2,1)S(1)}, bf16[16,6144]{1,0:T(8,128)(2,1)S(1)}, u32[]{:S(2)}, u32[]{:S(2)}) collective-permute-start(bf16[16,6144]{1,0:T(8,128)(2,1)S(1)} %get-tuple-element.28), channel_id=1, source_target_pairs={{0,1},{1,0},{2,3},{3,2},{4,5},{5,4},{6,7},{7,6},{8,9},{9,8},{10,11... | collective-permute-start | bytes 589832 | tf_op jit(solution)/shard_map/ppermute | solution.py:277
  29.6 5.5 %collective-permute-start.13 = (bf16[4,6144]{1,0:T(4,128)(2,1)S(1)}, bf16[4,6144]{1,0:T(4,128)(2,1)S(1)}, u32[]{:S(2)}, u32[]{:S(2)}) collective-permute-start(bf16[4,6144]{1,0:T(4,128)(2,1)S(1)} %get-tuple-element.36), channel_id=1, source_target_pairs={{0,6},{1,7},{2,4},{3,5},{4,2},{5,3},{6,0},{7,1},{8,14},{9,15},{10,... | collective-permute-start | bytes 147464 | tf_op jit(solution)/shard_map/ppermute | solution.py:277
  30.8 5.9 %collective-permute-start.14 = (bf16[4,6144]{1,0:T(4,128)(2,1)S(1)}, bf16[4,6144]{1,0:T(4,128)(2,1)S(1)}, u32[]{:S(2)}, u32[]{:S(2)}) collective-permute-start(bf16[4,6144]{1,0:T(4,128)(2,1)S(1)} %get-tuple-element.37), channel_id=1, source_target_pairs={{0,4},{1,5},{2,6},{3,7},{4,0},{5,1},{6,2},{7,3},{8,12},{9,13},{10,... | collective-permute-start | bytes 147464 | tf_op jit(solution)/shard_map/ppermute | solution.py:277
  31.7 5.0 %collective-permute-start.15 = (bf16[4,6144]{1,0:T(4,128)(2,1)S(1)}, bf16[4,6144]{1,0:T(4,128)(2,1)S(1)}, u32[]{:S(2)}, u32[]{:S(2)}) collective-permute-start(bf16[4,6144]{1,0:T(4,128)(2,1)S(1)} %get-tuple-element.38), channel_id=1, source_target_pairs={{0,2},{1,3},{2,0},{3,1},{4,6},{5,7},{6,4},{7,5},{8,10},{9,11},{10,... | collective-permute-start | bytes 147464 | tf_op jit(solution)/shard_map/ppermute | solution.py:277
  33.2 6.0 %collective-permute-start.10 = (bf16[4,6144]{1,0:T(4,128)(2,1)S(1)}, bf16[4,6144]{1,0:T(4,128)(2,1)S(1)}, u32[]{:S(2)}, u32[]{:S(2)}) collective-permute-start(bf16[4,6144]{1,0:T(4,128)(2,1)S(1)} %get-tuple-element.30), channel_id=1, source_target_pairs={{0,6},{1,7},{2,4},{3,5},{4,2},{5,3},{6,0},{7,1},{8,14},{9,15},{10,... | collective-permute-start | bytes 147464 | tf_op jit(solution)/shard_map/ppermute | solution.py:277
  34.3 4.9 %collective-permute-start.11 = (bf16[4,6144]{1,0:T(4,128)(2,1)S(1)}, bf16[4,6144]{1,0:T(4,128)(2,1)S(1)}, u32[]{:S(2)}, u32[]{:S(2)}) collective-permute-start(bf16[4,6144]{1,0:T(4,128)(2,1)S(1)} %get-tuple-element.31), channel_id=1, source_target_pairs={{0,4},{1,5},{2,6},{3,7},{4,0},{5,1},{6,2},{7,3},{8,12},{9,13},{10,... | collective-permute-start | bytes 147464 | tf_op jit(solution)/shard_map/ppermute | solution.py:277
  35.2 4.1 %collective-permute-start.12 = (bf16[4,6144]{1,0:T(4,128)(2,1)S(1)}, bf16[4,6144]{1,0:T(4,128)(2,1)S(1)}, u32[]{:S(2)}, u32[]{:S(2)}) collective-permute-start(bf16[4,6144]{1,0:T(4,128)(2,1)S(1)} %get-tuple-element.32), channel_id=1, source_target_pairs={{0,2},{1,3},{2,0},{3,1},{4,6},{5,7},{6,4},{7,5},{8,10},{9,11},{10,... | collective-permute-start | bytes 147464 | tf_op jit(solution)/shard_map/ppermute | solution.py:277
  36.7 5.1 %collective-permute-start.16 = (bf16[4,6144]{1,0:T(4,128)(2,1)S(1)}, bf16[4,6144]{1,0:T(4,128)(2,1)S(1)}, u32[]{:S(2)}, u32[]{:S(2)}) collective-permute-start(bf16[4,6144]{1,0:T(4,128)(2,1)S(1)} %shard_map.115), channel_id=1, source_target_pairs={{0,8},{1,9},{2,10},{3,11},{4,12},{5,13},{6,14},{7,15},{8,0},{9,1},... | collective-permute-start | bytes 147464 | tf_op jit(solution)/shard_map/ppermute | solution.py:277
